TPU v7x, 32 devices: a whole 2x2x4 slice. The times are simulated.
32 devices in a mesh: dp: 4 (over x, core), ctx: 8 (over z, y).
Axes of the slice: x: 2, y: 2, z: 4, core: 2. Of those that a mesh axis runs over, the one named last changes fastest.
Arguments:
- inputs: bfloat16 [8, 2048, 896], P('dp', 'ctx'), may hold values from -6 to 6
- cotangent: bfloat16 [8, 2048, 896], P('dp', 'ctx'), may hold values from -6 to 6
- lengths: int32 [8], P('dp'), may hold values from 256 to 2048, as said below
- qkv_weight: float32 [896, 1152], P(('dp', 'ctx')), may hold values from -0.1875 to 0.1875
- out_weight: float32 [896, 896], P(('dp', 'ctx')), may hold values from -2 to 2
- gate_up_weight: float32 [896, 9728], P(('dp', 'ctx')), may hold values from -0.1875 to 0.1875
- down_weight: float32 [4864, 896], P(('dp', 'ctx')), may hold values from -0.078125 to 0.078125
- gains_biases: float32 [2944], P(('dp', 'ctx')), may hold values from -2 to 2.5
- qkv_moment: float32 [896, 1152], P(('dp', 'ctx')), may hold values from -0.0004272461 to 0.0004272461
- qkv_square: float32 [896, 1152], P(('dp', 'ctx')), may hold values from 3.5272696e-09 to 1.4082255e-08
- out_moment: float32 [896, 896], P(('dp', 'ctx')), may hold values from -0.0004272461 to 0.0004272461
- out_square: float32 [896, 896], P(('dp', 'ctx')), may hold values from 3.5272696e-09 to 1.4082255e-08
- gate_up_moment: float32 [896, 9728], P(('dp', 'ctx')), may hold values from -0.0004272461 to 0.0004272461
- gate_up_square: float32 [896, 9728], P(('dp', 'ctx')), may hold values from 3.5272696e-09 to 1.4082255e-08
- down_moment: float32 [4864, 896], P(('dp', 'ctx')), may hold values from -0.0004272461 to 0.0004272461
- down_square: float32 [4864, 896], P(('dp', 'ctx')), may hold values from 3.5272696e-09 to 1.4082255e-08
- small_moment: float32 [2944], P(('dp', 'ctx')), may hold values from -0.0004272461 to 0.0004272461
- small_square: float32 [2944], P(('dp', 'ctx')), may hold values from 4.5130275e-07 to 1.8038698e-06
Outputs:
- output: bfloat16 [8, 2048, 896], P('dp', 'ctx')
- input_grad: bfloat16 [8, 2048, 896], P('dp', 'ctx')
- grad_norm: float32 [], replicated
- qkv_grad: float32 [896, 1152], P(('dp', 'ctx'))
- qkv_moment_new: float32 [896, 1152], P(('dp', 'ctx'))
- qkv_square_new: float32 [896, 1152], P(('dp', 'ctx'))
- qkv_weight_new: float32 [896, 1152], P(('dp', 'ctx'))
- out_grad: float32 [896, 896], P(('dp', 'ctx'))
- out_moment_new: float32 [896, 896], P(('dp', 'ctx'))
- out_square_new: float32 [896, 896], P(('dp', 'ctx'))
- out_weight_new: float32 [896, 896], P(('dp', 'ctx'))
- gate_up_grad: float32 [896, 9728], P(('dp', 'ctx'))
- gate_up_moment_new: float32 [896, 9728], P(('dp', 'ctx'))
- gate_up_square_new: float32 [896, 9728], P(('dp', 'ctx'))
- gate_up_weight_new: float32 [896, 9728], P(('dp', 'ctx'))
- down_grad: float32 [4864, 896], P(('dp', 'ctx'))
- down_moment_new: float32 [4864, 896], P(('dp', 'ctx'))
- down_square_new: float32 [4864, 896], P(('dp', 'ctx'))
- down_weight_new: float32 [4864, 896], P(('dp', 'ctx'))
- small_grad: float32 [2944], P(('dp', 'ctx'))
- small_moment_new: float32 [2944], P(('dp', 'ctx'))
- small_square_new: float32 [2944], P(('dp', 'ctx'))
- small_weight_new: float32 [2944], P(('dp', 'ctx'))
Inputs may be any that keep to these rules, and one draw needn't show every extreme that they name: `lengths`: in each group of 2 sequences of one index of dp, one sequence has length exactly 2048.
All inputs are finite; a program needn't handle non-finite values.
Results may differ from a plain program's by a relative error of at most 0.018.
The roundings to bfloat16 on the way count: a program that leaves them out, or rounds other values in their place, can miss the bound.
Values may be sent and summed in bfloat16 or wider, within the bound.
No kernel may reach another device: no remote copies, remote signals or barrier semaphores. Data moves between devices by JAX's collectives and lax.ppermute only.
A program may use at most 256 MiB of HBM per device.

v0:
```python
import math

import jax
import jax.numpy as jnp
from jax import lax
from jax.sharding import PartitionSpec as P

D = 896
HEADS = 14
KVH = 2
HD = 64
FF = 4864
STEP = 5
QD = 896


EPS = 1e-06
NEG = -1e30
BASE = 1000000.0
CLIP = 1.0
BETA_ONE = 0.9
BETA_TWO = 0.95
ADAM_EPS = 1e-08
RATES = (0.06, 1.0, 0.06, 0.03, 3.0)
DECAYS = (0.1, 0.1, 0.1, 0.1, 0.0)


def rotate(tensor, positions, sign):
    half = tensor.shape[-1] // 2
    freq = jnp.exp(jnp.arange(half, dtype=jnp.float32) * (-2.0 * math.log(BASE) / tensor.shape[-1]))
    angle = positions.astype(jnp.float32)[:, None] * freq[None, :]
    cosine = jnp.cos(angle)[:, None, :]
    sine = sign * jnp.sin(angle)[:, None, :]
    first = tensor[..., :half]
    second = tensor[..., half:]
    return jnp.concatenate([first * cosine - second * sine, second * cosine + first * sine], -1)


def across_tokens(left, right):
    flat_left = left.reshape(-1, left.shape[-1])
    flat_right = right.reshape(-1, right.shape[-1])
    return lax.dot_general(
        flat_left, flat_right, (((0,), (0,)), ((), ())), preferred_element_type=jnp.float32
    )


def against_weight(values, weight):
    return lax.dot_general(
        values, weight, (((values.ndim - 1,), (1,)), ((), ())), preferred_element_type=jnp.float32
    )


def norm_back(state, inverse, gain, upstream):
    scaled = gain * upstream
    change = inverse * scaled - state * inverse**3 * jnp.mean(scaled * state, -1, keepdims=True)
    gain_grad = jnp.sum((upstream * state * inverse).reshape(-1, state.shape[-1]), 0)
    return (change, gain_grad)


def adam_step(gradient, moment, square, weight, factor, rate, decay):
    gradient = gradient * factor
    moment = BETA_ONE * moment + (1.0 - BETA_ONE) * gradient
    square = BETA_TWO * square + (1.0 - BETA_TWO) * gradient * gradient
    corr_one = 1.0 - BETA_ONE**STEP
    corr_two = 1.0 - BETA_TWO**STEP
    update = moment / corr_one / (jnp.sqrt(square / corr_two) + ADAM_EPS)
    weight = weight * (1.0 - rate * decay) - rate * update
    return (gradient, moment, square, weight)


def softmax_fold(grouped, lengths, query_pos, scale):
    last_query = jnp.max(query_pos)

    def fold(carry, piece, start):
        keys, values = piece
        count = keys.shape[1]
        block = math.gcd(count, 512)

        def step(index, state):
            first = index * block

            def step_compute(state):
                top, total, accum = state
                key_part = lax.dynamic_slice_in_dim(keys, first, block, 1)
                value_part = lax.dynamic_slice_in_dim(values, first, block, 1)
                key_pos = first + jnp.arange(block, dtype=jnp.int32)
                scores = (
                    jnp.einsum(
                        "rhqd,rkhd->rhqk", grouped, key_part, preferred_element_type=jnp.float32
                    )
                    * scale
                )
                allowed = (key_pos[None, None, None, :] <= query_pos[None, None, :, None]) & (
                    key_pos[None, None, None, :] < lengths[:, None, None, None]
                )
                scores = jnp.where(allowed, scores, NEG)
                new_top = jnp.maximum(top, jnp.max(scores, -1))
                factor = jnp.exp(top - new_top)
                probs = jnp.where(allowed, jnp.exp(scores - new_top[..., None]), 0.0)
                total = total * factor + jnp.sum(probs, -1)
                accum = accum * factor[..., None] + jnp.einsum(
                    "rhqk,rkhd->rhqd",
                    probs.astype(jnp.bfloat16),
                    value_part,
                    preferred_element_type=jnp.float32,
                )
                return (new_top, total, accum)

            def unchanged(state):
                return state

            return lax.cond(first <= last_query, step_compute, unchanged, state)

        return lax.fori_loop(0, count // block, step, carry)

    return fold


def on_device(
    inputs,
    cotangent,
    lengths,
    qkv_weight,
    out_weight,
    gate_up_weight,
    down_weight,
    gains_biases,
    qkv_moment,
    qkv_square,
    out_moment,
    out_square,
    gate_up_moment,
    gate_up_square,
    down_moment,
    down_square,
    small_moment,
    small_square,
):
    rows, block_len, width = inputs.shape
    ctx_index = lax.axis_index("ctx")
    positions = ctx_index * block_len + jnp.arange(block_len, dtype=jnp.int32)
    group = HEADS // KVH
    kv_width = KVH * HD
    scale = HD ** (-0.5)
    full_qkv, full_out, full_gu, full_down, full_small = (
        lax.all_gather(qkv_weight.astype(jnp.bfloat16), ("dp", "ctx"), axis=0, tiled=True),
        lax.all_gather(out_weight.astype(jnp.bfloat16), ("dp", "ctx"), axis=0, tiled=True),
        lax.all_gather(gate_up_weight.astype(jnp.bfloat16), ("dp", "ctx"), axis=0, tiled=True),
        lax.all_gather(down_weight.astype(jnp.bfloat16), ("dp", "ctx"), axis=0, tiled=True),
        lax.all_gather(gains_biases.astype(jnp.bfloat16), ("dp", "ctx"), axis=0, tiled=True),
    )
    small_used = full_small.astype(jnp.float32)
    gain_attn = small_used[:D]
    gain_mlp = small_used[D : 2 * D]
    bias = small_used[2 * D :]
    state = inputs.astype(jnp.float32)
    inverse_attn = lax.rsqrt(jnp.mean(state * state, -1, keepdims=True) + EPS)
    normed = (state * inverse_attn * gain_attn).astype(jnp.bfloat16)
    qkv = jnp.dot(normed, full_qkv, preferred_element_type=jnp.float32) + bias
    query = rotate(qkv[..., :QD].reshape(rows, block_len, HEADS, HD), positions, 1.0).astype(
        jnp.bfloat16
    )
    keys = rotate(
        qkv[..., QD : QD + kv_width].reshape(rows, block_len, KVH, HD), positions, 1.0
    ).astype(jnp.bfloat16)
    values = qkv[..., QD + kv_width :].reshape(rows, block_len, KVH, HD).astype(jnp.bfloat16)
    grouped = (
        query.reshape(rows, block_len, KVH, group, HD)
        .transpose(0, 2, 3, 1, 4)
        .reshape(rows, KVH, group * block_len, HD)
    )
    query_pos = jnp.tile(positions, group)
    start_top = jnp.full((rows, KVH, group * block_len), NEG, jnp.float32)
    initial = (
        start_top,
        jnp.zeros_like(start_top),
        jnp.zeros((rows, KVH, group * block_len, HD), jnp.float32),
    )
    fold = softmax_fold(grouped, lengths, query_pos, scale)
    top, total, accum = fold(
        initial,
        (
            lax.all_gather(keys, "ctx", axis=1, tiled=True),
            lax.all_gather(values, "ctx", axis=1, tiled=True),
        ),
        jnp.int32(0),
    )
    attended = accum / total[..., None]
    log_total = top + jnp.log(total)
    mixed = (
        attended.reshape(rows, KVH, group, block_len, HD)
        .transpose(0, 3, 1, 2, 4)
        .reshape(rows, block_len, QD)
    )
    mixed_low = mixed.astype(jnp.bfloat16)
    hidden_state = state + jnp.dot(mixed_low, full_out, preferred_element_type=jnp.float32)
    inverse_mlp = lax.rsqrt(jnp.mean(hidden_state * hidden_state, -1, keepdims=True) + EPS)
    normed2 = (hidden_state * inverse_mlp * gain_mlp).astype(jnp.bfloat16)
    both = jnp.dot(normed2, full_gu, preferred_element_type=jnp.float32)
    gate = both[..., :FF]
    up_part = both[..., FF:]
    sigma = jax.nn.sigmoid(gate)
    activated = gate * sigma
    inner = (activated * up_part).astype(jnp.bfloat16)
    output = hidden_state + jnp.dot(inner, full_down, preferred_element_type=jnp.float32)
    back_qkv, back_out, back_gu, back_down = (
        lax.all_gather(qkv_weight.astype(jnp.bfloat16), ("dp", "ctx"), axis=0, tiled=True),
        lax.all_gather(out_weight.astype(jnp.bfloat16), ("dp", "ctx"), axis=0, tiled=True),
        lax.all_gather(gate_up_weight.astype(jnp.bfloat16), ("dp", "ctx"), axis=0, tiled=True),
        lax.all_gather(down_weight.astype(jnp.bfloat16), ("dp", "ctx"), axis=0, tiled=True),
    )
    valid = (positions[None, :] < lengths[:, None]).astype(jnp.float32)[..., None]
    upstream = cotangent.astype(jnp.float32) * valid
    upstream_low = upstream.astype(jnp.bfloat16)
    grad_down = across_tokens(inner, upstream_low)
    d_inner = against_weight(upstream_low, back_down)
    d_gate = d_inner * up_part * sigma * (1.0 + gate * (1.0 - sigma))
    d_up = d_inner * activated
    d_both = jnp.concatenate([d_gate, d_up], -1).astype(jnp.bfloat16)
    grad_gu = across_tokens(normed2, d_both)
    d_normed2 = against_weight(d_both, back_gu)
    change_mlp, grad_gain_mlp = norm_back(hidden_state, inverse_mlp, gain_mlp, d_normed2)
    d_hidden = upstream + change_mlp
    d_hidden_low = d_hidden.astype(jnp.bfloat16)
    grad_out = across_tokens(mixed_low, d_hidden_low)
    d_mixed = against_weight(d_hidden_low, back_out).astype(jnp.bfloat16)
    d_grouped = (
        d_mixed.reshape(rows, block_len, KVH, group, HD)
        .transpose(0, 2, 3, 1, 4)
        .reshape(rows, KVH, group * block_len, HD)
    )
    delta = jnp.sum(d_grouped.astype(jnp.float32) * attended, -1)
    back_keys, back_values = (
        lax.all_gather(keys, "ctx", axis=1, tiled=True),
        lax.all_gather(values, "ctx", axis=1, tiled=True),
    )
    seq_len = back_keys.shape[1]
    key_block = math.gcd(seq_len, 512)
    last_query = ctx_index * block_len + block_len - 1

    def back_step(d_query, index):
        first = index * key_block

        def back_compute(d_query):
            key_part = lax.dynamic_slice_in_dim(back_keys, first, key_block, 1)
            value_part = lax.dynamic_slice_in_dim(back_values, first, key_block, 1)
            key_pos = first + jnp.arange(key_block, dtype=jnp.int32)
            scores = (
                jnp.einsum("rhqd,rkhd->rhqk", grouped, key_part, preferred_element_type=jnp.float32)
                * scale
            )
            allowed = (key_pos[None, None, None, :] <= query_pos[None, None, :, None]) & (
                key_pos[None, None, None, :] < lengths[:, None, None, None]
            )
            probs = jnp.where(allowed, jnp.exp(scores - log_total[..., None]), 0.0)
            d_probs = jnp.einsum(
                "rhqd,rkhd->rhqk", d_grouped, value_part, preferred_element_type=jnp.float32
            )
            d_scores = (probs * (d_probs - delta[..., None])).astype(jnp.bfloat16)
            d_query = d_query + jnp.einsum(
                "rhqk,rkhd->rhqd", d_scores, key_part, preferred_element_type=jnp.float32
            )
            d_key = (
                jnp.einsum("rhqk,rhqd->krhd", d_scores, grouped, preferred_element_type=jnp.float32)
                * scale
            )
            d_value = jnp.einsum(
                "rhqk,rhqd->krhd",
                probs.astype(jnp.bfloat16),
                d_grouped,
                preferred_element_type=jnp.float32,
            )
            return (d_query, (d_key, d_value))

        def skipped(d_query):
            empty = jnp.zeros((key_block, rows, KVH, HD), jnp.float32)
            return (d_query, (empty, empty))

        return lax.cond(first <= last_query, back_compute, skipped, d_query)

    d_query, (key_terms, value_terms) = lax.scan(
        back_step,
        jnp.zeros((rows, KVH, group * block_len, HD), jnp.float32),
        jnp.arange(seq_len // key_block, dtype=jnp.int32),
    )
    key_grads, value_grads = (
        lax.psum_scatter(
            key_terms.reshape(seq_len, rows, kv_width).astype(jnp.bfloat16),
            "ctx",
            scatter_dimension=0,
            tiled=True,
        ).astype(jnp.float32),
        lax.psum_scatter(
            value_terms.reshape(seq_len, rows, kv_width).astype(jnp.bfloat16),
            "ctx",
            scatter_dimension=0,
            tiled=True,
        ).astype(jnp.float32),
    )
    d_query = (
        (d_query * scale)
        .reshape(rows, KVH, group, block_len, HD)
        .transpose(0, 3, 1, 2, 4)
        .reshape(rows, block_len, HEADS, HD)
    )
    d_query_pre = rotate(d_query, positions, -1.0).reshape(rows, block_len, QD)
    d_key_pre = rotate(
        key_grads.transpose(1, 0, 2).reshape(rows, block_len, KVH, HD), positions, -1.0
    ).reshape(rows, block_len, kv_width)
    d_qkv = jnp.concatenate([d_query_pre, d_key_pre, value_grads.transpose(1, 0, 2)], -1).astype(
        jnp.bfloat16
    )
    grad_bias = jnp.sum(d_qkv.astype(jnp.float32).reshape(-1, QD + 2 * kv_width), 0)
    grad_qkv = across_tokens(normed, d_qkv)
    d_normed = against_weight(d_qkv, back_qkv)
    change_attn, grad_gain_attn = norm_back(state, inverse_attn, gain_attn, d_normed)
    input_grad = (d_hidden + change_attn).astype(jnp.bfloat16)
    grad_small = jnp.concatenate([grad_gain_attn, grad_gain_mlp, grad_bias])
    red_qkv, red_out, red_gu, red_down, red_small = (
        lax.psum_scatter(grad_qkv, ("dp", "ctx"), scatter_dimension=0, tiled=True),
        lax.psum_scatter(grad_out, ("dp", "ctx"), scatter_dimension=0, tiled=True),
        lax.psum_scatter(grad_gu, ("dp", "ctx"), scatter_dimension=0, tiled=True),
        lax.psum_scatter(grad_down, ("dp", "ctx"), scatter_dimension=0, tiled=True),
        lax.psum_scatter(grad_small, ("dp", "ctx"), scatter_dimension=0, tiled=True),
    )
    local_square = (
        jnp.sum(red_qkv * red_qkv)
        + jnp.sum(red_out * red_out)
        + jnp.sum(red_gu * red_gu)
        + jnp.sum(red_down * red_down)
        + jnp.sum(red_small * red_small)
    )
    square_sum = lax.psum(local_square, ("dp", "ctx"))
    grad_norm = jnp.sqrt(square_sum)
    factor = CLIP / jnp.maximum(grad_norm, CLIP)
    qkv_new = adam_step(red_qkv, qkv_moment, qkv_square, qkv_weight, factor, RATES[0], DECAYS[0])
    out_new = adam_step(red_out, out_moment, out_square, out_weight, factor, RATES[1], DECAYS[1])
    gu_new = adam_step(
        red_gu, gate_up_moment, gate_up_square, gate_up_weight, factor, RATES[2], DECAYS[2]
    )
    down_new = adam_step(
        red_down, down_moment, down_square, down_weight, factor, RATES[3], DECAYS[3]
    )
    small_new = adam_step(
        red_small, small_moment, small_square, gains_biases, factor, RATES[4], DECAYS[4]
    )
    return (
        output.astype(jnp.bfloat16),
        input_grad,
        grad_norm,
        qkv_new[0],
        qkv_new[1],
        qkv_new[2],
        qkv_new[3],
        out_new[0],
        out_new[1],
        out_new[2],
        out_new[3],
        gu_new[0],
        gu_new[1],
        gu_new[2],
        gu_new[3],
        down_new[0],
        down_new[1],
        down_new[2],
        down_new[3],
        small_new[0],
        small_new[1],
        small_new[2],
        small_new[3],
    )


def solution(mesh):
    placed = (
        P("dp", "ctx", None),
        P("dp", "ctx", None),
        P("dp"),
        P(("dp", "ctx"), None),
        P(("dp", "ctx"), None),
        P(("dp", "ctx"), None),
        P(("dp", "ctx"), None),
        P(("dp", "ctx")),
        P(("dp", "ctx"), None),
        P(("dp", "ctx"), None),
        P(("dp", "ctx"), None),
        P(("dp", "ctx"), None),
        P(("dp", "ctx"), None),
        P(("dp", "ctx"), None),
        P(("dp", "ctx"), None),
        P(("dp", "ctx"), None),
        P(("dp", "ctx")),
        P(("dp", "ctx")),
    )
    return jax.shard_map(
        on_device,
        mesh=mesh,
        in_specs=placed,
        out_specs=(
            P("dp", "ctx", None),
            P("dp", "ctx", None),
            P(),
            P(("dp", "ctx"), None),
            P(("dp", "ctx"), None),
            P(("dp", "ctx"), None),
            P(("dp", "ctx"), None),
            P(("dp", "ctx"), None),
            P(("dp", "ctx"), None),
            P(("dp", "ctx"), None),
            P(("dp", "ctx"), None),
            P(("dp", "ctx"), None),
            P(("dp", "ctx"), None),
            P(("dp", "ctx"), None),
            P(("dp", "ctx"), None),
            P(("dp", "ctx"), None),
            P(("dp", "ctx"), None),
            P(("dp", "ctx"), None),
            P(("dp", "ctx"), None),
            P(("dp", "ctx")),
            P(("dp", "ctx")),
            P(("dp", "ctx")),
            P(("dp", "ctx")),
        ),
        check_vma=False,
    )
```

profile of v0, /device:TPU:0, one launch (start us, length us, event | category | flops | bytes accessed | tf_op | source)
XLA Modules:
  0.0 2491.6 jit_solution(16586442119494460934)
XLA Ops:
  11.3 42.1 %all-reduce = bf16[2944]{0:T(1024)(128)(2,1)S(1)} all-reduce(bf16[2944]{0:T(1024)(128)(2,1)S(1)} %dynamic-update-slice), channel_id=1, replica_groups=mesh['dp'=4,'ctx'=8] {'dp','ctx'}, use_global_device_ids=true, to_apply=%add | all-reduce | flops 2944 | bytes 11776
  84.0 45.9 %all-gather.18.cloned.1.call-done = bf16[32,28,896]{2,1,0:T(8,128)(2,1)} async-done(((bf16[1,28,896]{2,1,0:T(8,128)(2,1)}), bf16[32,28,896]{2,1,0:T(8,128)(2,1)}) %all-gather.18.cloned.1.call-update) | async-done | bytes 1605648 | tf_op jit(solution)/shard_map/all_gather | solution.py:147
  138.7 32.3 %all-gather.10.cloned.1.call-done = bf16[2,2048,2,64]{1,3,2,0:T(8,128)(2,1)} async-done(((bf16[2,256,2,64]{1,3,2,0:T(8,128)(2,1)}), bf16[2,2048,2,64]{1,3,2,0:T(8,128)(2,1)}) %all-gather.10.cloned.1.call-update) | async-done | bytes 1048592 | tf_op jit(solution)/shard_map/all_gather | solution.py:183
  171.0 40.9 %all-gather.12.cloned.1.call-done = bf16[2,2048,2,64]{1,3,2,0:T(8,128)(2,1)} async-done(((bf16[2,256,2,64]{1,3,2,0:T(8,128)(2,1)}), bf16[2,2048,2,64]{1,3,2,0:T(8,128)(2,1)}) %all-gather.12.cloned.1.call-update) | async-done | bytes 1048592 | tf_op jit(solution)/shard_map/all_gather | solution.py:184
  213.3 19.7 while.36
  214.0 17.0 conditional.6
  241.8 101.9 %all-gather.20.cloned.1.call-done = bf16[32,28,9728]{2,1,0:T(8,128)(2,1)} async-done(((bf16[1,28,9728]{2,1,0:T(8,128)(2,1)}), bf16[32,28,9728]{2,1,0:T(8,128)(2,1)}) %all-gather.20.cloned.1.call-update) | async-done | bytes 17432592 | tf_op jit(solution)/shard_map/all_gather | solution.py:148
  343.7 19.6 reshape.455
  363.4 18.2 fusion.71
  381.5 42.5 %all-gather.14.cloned.1.call-done = bf16[4864,896]{1,0:T(8,128)(2,1)} async-done(((bf16[152,896]{1,0:T(8,128)(2,1)}), bf16[4864,896]{1,0:T(8,128)(2,1)}) %all-gather.14.cloned.1.call-update) | async-done | bytes 8716304 | tf_op jit(solution)/shard_map/all_gather | solution.py:149
  424.1 17.6 multiply_convert_fusion.1
  441.6 16.2 multiply_reduce_fusion
  463.9 43.2 %while.37 = (s32[]{:T(128)}, f32[2,2,1792,64]{2,3,1,0:T(8,128)S(1)}, bf16[4,512,2,2,64]{1,4,3,2,0:T(8,128)(2,1)}, bf16[4,512,2,2,64]{1,4,3,2,0:T(8,128)(2,1)}, s...) while((s32[]{:T(128)}, ...), condition=%wide.region_14.15_spmd.clone, body=%wide.region_11.14_spmd.clone.sunk | while | flops 2388985344 | bytes 94234504 | solution.py:281
  465.6 34.0 %conditional.7 = (f32[2,2,1792,64]{2,3,1,0:T(8,128)S(1)}, bf16[1,512,2,2,64]{1,4,3,2,0:T(8,128)(2,1)S(1)}, bf16[1,512,2,2,64]{1,4,3,2,0:T(8,128)(2,1)S(1)}) conditional(s32[]{:T(128)} %convert_element_type.238, f32[2,2,1792,64]{2,3,1,0:T(8,128)S(1)} %get-tuple-element.749, (s32[]{:T(128)}, s32[256]{0:T(256)S(1)}, s32[2]{0:T(128)S(1)}, ...), branch_computations={%region_12.12_spmd, %region_13.13_spmd} | conditional | flops 2388985344 | bytes 93185152 | solution.py:279
  545.5 19.1 convolution_bitcast_fusion
  564.6 112.3 %reduce-scatter.13.cloned.1.call-done = bf16[256,2,128]{0,2,1:T(8,128)(2,1)} async-done(((bf16[2048,2,128]{0,2,1:T(8,128)(2,1)}), bf16[256,2,128]{0,2,1:T(8,128)(2,1)}) %reduce-scatter.13.cloned.1.call-update) | async-done | bytes 131088 | tf_op jit(solution)/shard_map/reduce_scatter | solution.py:287
  678.1 65.6 %reduce-scatter.15.cloned.1.call-done = bf16[256,2,128]{2,0,1:T(8,128)(2,1)} async-done(((bf16[2048,2,128]{2,0,1:T(8,128)(2,1)}), bf16[256,2,128]{2,0,1:T(8,128)(2,1)}) %reduce-scatter.15.cloned.1.call-update) | async-done | bytes 131088 | tf_op jit(solution)/shard_map/reduce_scatter | solution.py:293
  748.7 1374.1 %fusion.80 = (f32[32,1152]{1,0:T(8,128)S(1)}, f32[32,896]{1,0:T(8,128)S(1)}, f32[32,9728]{1,0:T(8,128)S(1)}) fusion(f32[896,1152]{1,0:T(8,128)} %convolution_bitcast_fusion.2, f32[896,896]{1,0:T(8,128)} %convolution_bitcast_fusion.3, f32[896,9728]{1,0:T(8,128)} %convolution_bitcast_fusion), kind=kCustom, calls=%all-reduce-scatter.3 | all-reduce-scatter fusion | flops 12058625 | bytes 43712512
  2149.3 31.7 %collective-permute-start.9 = (f32[32,9728]{1,0:T(8,128)S(1)}, f32[32,9728]{1,0:T(8,128)}, u32[]{:S(2)}, u32[]{:S(2)}) collective-permute-start(f32[32,9728]{1,0:T(8,128)S(1)} %get-tuple-element.471), channel_id=1, source_target_pairs={{0,2},{1,3},{2,4},{3,5},{4,6},{5,7},{6,8},{7,9},{8,10},{9,11},{10,... | collective-permute-start | bytes 3735560
  2200.5 35.3 %collective-permute-done.3 = f32[28,1152]{1,0:T(8,128)S(1)} collective-permute-done((f32[28,1152]{1,0:T(8,128)S(1)}, f32[28,1152]{1,0:T(8,128)S(1)}, u32[]{:S(2)}, u32[]{:S(2)}) %collective-permute-start.3) | collective-permute-done | bytes 129056
  2255.1 69.2 %collective-permute-start.1 = (f32[32,1152]{1,0:T(8,128)S(1)}, f32[32,1152]{1,0:T(8,128)}, u32[]{:S(2)}, u32[]{:S(2)}) collective-permute-start(f32[32,1152]{1,0:T(8,128)S(1)} %get-tuple-element.469), channel_id=1, source_target_pairs={{0,2},{1,3},{2,4},{3,5},{4,6},{5,7},{6,8},{7,9},{8,10},{9,11},{10,... | collective-permute-start | bytes 442376
  2325.8 39.8 %all-reduce.5 = f32[2944]{0:T(1024)S(1)} all-reduce(f32[2944]{0:T(1024)S(1)} %pad_maximum_fusion.7), channel_id=8, replica_groups=mesh['dp'=4,'ctx'=8] {'dp','ctx'}, use_global_device_ids=true, to_apply=%region_29.30.clone | all-reduce | flops 2944 | bytes 23552
  2392.0 31.5 %concatenate.55 = f32[156,9728]{1,0:T(8,128)} concatenate(f32[28,9728]{1,0:T(8,128)} %collective-permute-done.11, f32[32,9728]{1,0:T(8,128)} %collective-permute-done.10, f32[32,9728]{1,0:T(8,128)} %collective-permute-done.9, f32[32,9728]{1,0:T(8,128)} %collective-permute-done.8, f32[32,9728]{1,0:T(8,128)S(1)} %get-tuple-element.471), dimensions={0} | concatenate | bytes 12140544
  2433.0 39.3 %psum.7 = f32[]{:T(128)} all-reduce(f32[]{:T(128)S(6)} %add.245), channel_id=1, replica_groups=mesh['dp'=4,'ctx'=8] {'dp','ctx'}, use_global_device_ids=true, to_apply=%region_31.32 | all-reduce | flops 1 | bytes 8 | tf_op jit(solution)/shard_map/psum | solution.py:333
  (285 shorter events, 270.3 us)
Async XLA Ops:
  7.2 64.4 %all-gather.16.cloned.1.call-start = ((), (), s32[]{:S(2)}) async-start(), calls=%async_computation.8 | async-start | bytes 2433024 | tf_op jit(solution)/shard_map/all_gather | solution.py:146
  8.8 121.1 %all-gather.18.cloned.1.call-start = ((), (), s32[]{:S(2)}) async-start(), calls=%async_computation.9 | async-start | bytes 1892352 | tf_op jit(solution)/shard_map/all_gather | solution.py:147
  10.4 160.6 %all-gather.10.cloned.1.call-start = ((), (), s32[]{:S(2)}) async-start(), calls=%async_computation.3 | async-start | bytes 1179648 | tf_op jit(solution)/shard_map/all_gather | solution.py:183
  55.5 402.3 %copy-start.31 = (f32[896]{0:T(1024)}, f32[896]{0:T(1024)S(1)}, u32[]{:S(2)}) copy-start(f32[896]{0:T(1024)S(1)} %get-tuple-element.509) | copy-start | bytes 10756
  79.4 132.5 %all-gather.12.cloned.1.call-start = ((), (), s32[]{:S(2)}) async-start(), calls=%async_computation.4 | async-start | bytes 1179648 | tf_op jit(solution)/shard_map/all_gather | solution.py:184
  81.2 262.5 %all-gather.20.cloned.1.call-start = ((), (), s32[]{:S(2)}) async-start(), calls=%async_computation.10 | async-start | bytes 20545536 | tf_op jit(solution)/shard_map/all_gather | solution.py:148
  82.2 341.9 %all-gather.14.cloned.1.call-start = ((), (), s32[]{:S(2)}) async-start(), calls=%async_computation.5 | async-start | bytes 8988672 | tf_op jit(solution)/shard_map/all_gather | solution.py:149
  83.0 593.9 %reduce-scatter.13.cloned.1.call-start = ((), (), s32[]{:S(2)}) async-start(), calls=%async_computation.6 | async-start | bytes 1179648 | tf_op jit(solution)/shard_map/reduce_scatter | solution.py:287
  241.8 216.0 %copy-start.5 = (f32[2,256,896]{2,1,0:T(8,128)}, f32[2,256,896]{2,1,0:T(8,128)S(1)}, u32[]{:S(2)}) copy-start(f32[2,256,896]{2,1,0:T(8,128)S(1)} %get-tuple-element.519) | copy-start | bytes 5505028
  241.8 216.0 %copy-start.34 = (f32[2,256]{1,0:T(2,128)}, f32[2,256]{1,0:T(2,128)S(1)}, u32[]{:S(2)}) copy-start(f32[2,256]{1,0:T(2,128)S(1)} %get-tuple-element.514) | copy-start | bytes 6148
  512.7 231.0 %reduce-scatter.15.cloned.1.call-start = ((), (), s32[]{:S(2)}) async-start(), calls=%async_computation.7 | async-start | bytes 1179648 | tf_op jit(solution)/shard_map/reduce_scatter | solution.py:293
  523.6 1902.9 %reduce-scatter.17.cloned.1.call-start = ((), (), s32[]{:S(2)}) async-start(), calls=%async_computation.11 | async-start | bytes 17977344
  2122.8 26.5 %collective-permute-start.4 = (f32[32,896]{1,0:T(8,128)S(1)}, f32[32,896]{1,0:T(8,128)}, u32[]{:S(2)}, u32[]{:S(2)}) collective-permute-start(f32[32,896]{1,0:T(8,128)S(1)} %get-tuple-element.470), channel_id=1, source_target_pairs={{0,1},{1,2},{2,3},{3,4},{4,5},{5,6},{6,7},{7,8},{8,9},{9,10},{10,1... | collective-permute-start | bytes 344072
  2124.8 56.3 %collective-permute-start.5 = (f32[32,896]{1,0:T(8,128)S(1)}, f32[32,896]{1,0:T(8,128)}, u32[]{:S(2)}, u32[]{:S(2)}) collective-permute-start(f32[32,896]{1,0:T(8,128)S(1)} %get-tuple-element.470), channel_id=1, source_target_pairs={{0,2},{1,3},{2,4},{3,5},{4,6},{5,7},{6,8},{7,9},{8,10},{9,11},{10,... | collective-permute-start | bytes 344072
  2127.1 59.2 %collective-permute-start.6 = (f32[32,896]{1,0:T(8,128)S(1)}, f32[32,896]{1,0:T(8,128)}, u32[]{:S(2)}, u32[]{:S(2)}) collective-permute-start(f32[32,896]{1,0:T(8,128)S(1)} %get-tuple-element.470), channel_id=1, source_target_pairs={{0,3},{1,4},{2,5},{3,6},{4,7},{5,8},{6,9},{7,10},{8,11},{9,12},{10... | collective-permute-start | bytes 344072
  2138.1 7.3 collective-permute-start.7
  2142.1 249.9 %collective-permute-start.10 = (f32[32,9728]{1,0:T(8,128)S(1)}, f32[32,9728]{1,0:T(8,128)}, u32[]{:S(2)}, u32[]{:S(2)}) collective-permute-start(f32[32,9728]{1,0:T(8,128)S(1)} %get-tuple-element.471), channel_id=1, source_target_pairs={{0,3},{1,4},{2,5},{3,6},{4,7},{5,8},{6,9},{7,10},{8,11},{9,12},{10... | collective-permute-start | bytes 3735560
  2145.4 246.6 %collective-permute-start.8 = (f32[32,9728]{1,0:T(8,128)S(1)}, f32[32,9728]{1,0:T(8,128)}, u32[]{:S(2)}, u32[]{:S(2)}) collective-permute-start(f32[32,9728]{1,0:T(8,128)S(1)} %get-tuple-element.471), channel_id=1, source_target_pairs={{0,1},{1,2},{2,3},{3,4},{4,5},{5,6},{6,7},{7,8},{8,9},{9,10},{10,1... | collective-permute-start | bytes 3735560
  2149.3 242.7 %collective-permute-start.9 = (f32[32,9728]{1,0:T(8,128)S(1)}, f32[32,9728]{1,0:T(8,128)}, u32[]{:S(2)}, u32[]{:S(2)}) collective-permute-start(f32[32,9728]{1,0:T(8,128)S(1)} %get-tuple-element.471), channel_id=1, source_target_pairs={{0,2},{1,3},{2,4},{3,5},{4,6},{5,7},{6,8},{7,9},{8,10},{9,11},{10,... | collective-permute-start | bytes 3735560
  2181.1 210.9 %collective-permute-start.11 = (f32[28,9728]{1,0:T(8,128)}, f32[28,9728]{1,0:T(8,128)}, u32[]{:S(2)}, u32[]{:S(2)}) collective-permute-start(f32[28,9728]{1,0:T(8,128)} %slice.83), channel_id=1, source_target_pairs={{0,4},{1,5},{2,6},{3,7},{4,8},{5,9},{6,10},{7,11},{8,12},{9,13},{1... | collective-permute-start | bytes 3268616
  2186.4 49.4 %collective-permute-start.3 = (f32[28,1152]{1,0:T(8,128)S(1)}, f32[28,1152]{1,0:T(8,128)S(1)}, u32[]{:S(2)}, u32[]{:S(2)}) collective-permute-start(f32[28,1152]{1,0:T(8,128)S(1)} %slice.81), channel_id=1, source_target_pairs={{0,4},{1,5},{2,6},{3,7},{4,8},{5,9},{6,10},{7,11},{8,12},{9,13},{1... | collective-permute-start | bytes 387080
  2235.8 19.3 collective-permute-start
  2255.1 111.2 %collective-permute-start.1 = (f32[32,1152]{1,0:T(8,128)S(1)}, f32[32,1152]{1,0:T(8,128)}, u32[]{:S(2)}, u32[]{:S(2)}) collective-permute-start(f32[32,1152]{1,0:T(8,128)S(1)} %get-tuple-element.469), channel_id=1, source_target_pairs={{0,2},{1,3},{2,4},{3,5},{4,6},{5,7},{6,8},{7,9},{8,10},{9,11},{10,... | collective-permute-start | bytes 442376
  2366.3 14.8 collective-permute-start.2
  (51 other events, 1397.0 us)
Sparse Core Ops, SparseCore 0:
  11.5 60.0 all-gather.15
  75.1 54.7 all-gather.17
  132.5 38.4 all-gather.9
  173.5 38.4 all-gather.11
  215.3 128.4 all-gather.19
  347.0 77.0 all-gather.13
  512.8 164.0 reduce-scatter.12
  681.3 62.3 reduce-scatter.14
  746.0 760.0 reduce-scatter.16
where the time goes:
time: 2500 us; the launch traced here: 2490 us
  blocking collectives  1500 us (60%)
  waiting for transfers between devices  492 us (20%)
  matrix products  154 us (6%)
  starting transfers between devices  153 us (6%)
  local copies, waits for them, and re-layouts  121 us (5%)
  other arithmetic  50.2 us (2%)
    unnamed x3, blocking collectives  1460 us
    unnamed x13, starting transfers between devices  152 us
    reduce_scatter x1, waiting for transfers between devices, on_device(): lax.psum_scatter(key_terms.reshape(seq_len, rows, kv_width).astype(jnp.bf...  112 us
    all_gather x1, waiting for transfers between devices, on_device(): lax.all_gather(gate_up_weight.astype(jnp.bfloat16), ('dp', 'ctx'), axis=0...  102 us
    unnamed x117, local copies, waits for them, and re-layouts  82.3 us
    reduce_scatter x1, waiting for transfers between devices, on_device(): lax.psum_scatter(value_terms.reshape(seq_len, rows, kv_width).astype(jnp....  65.6 us
  transfers between devices with their start and end apart: 21, of which 9 were waited for; matrix products, arithmetic and copies ran while one was open for 64% of the time, Pallas kernels for 0%

commit v1 on v0

v1 whole, which is shorter than its diff:
```python
import functools
import math

import jax
import jax.numpy as jnp
from jax import lax
from jax.experimental import pallas as pl
from jax.experimental.pallas import tpu as pltpu
from jax.sharding import Mesh
from jax.sharding import PartitionSpec as P

D = 896
HEADS = 14
KVH = 2
HD = 64
FF = 4864
STEP = 5
QD = 896


EPS = 1e-06
NEG = -1e30
BASE = 1000000.0
CLIP = 1.0
BETA_ONE = 0.9
BETA_TWO = 0.95
ADAM_EPS = 1e-08
RATES = (0.06, 1.0, 0.06, 0.03, 3.0)
DECAYS = (0.1, 0.1, 0.1, 0.1, 0.0)


def across_tokens(left, right):
    flat_left = left.reshape(-1, left.shape[-1])
    flat_right = right.reshape(-1, right.shape[-1])
    return lax.dot_general(
        flat_left, flat_right, (((0,), (0,)), ((), ())), preferred_element_type=jnp.float32
    )


def against_weight(values, weight):
    return lax.dot_general(
        values, weight, (((values.ndim - 1,), (1,)), ((), ())), preferred_element_type=jnp.float32
    )


def norm_back(state, inverse, gain, upstream):
    scaled = gain * upstream
    change = inverse * scaled - state * inverse**3 * jnp.mean(scaled * state, -1, keepdims=True)
    gain_grad = jnp.sum((upstream * state * inverse).reshape(-1, state.shape[-1]), 0)
    return (change, gain_grad)


def adam_step(gradient, moment, square, weight, factor, rate, decay):
    gradient = gradient * factor
    moment = BETA_ONE * moment + (1.0 - BETA_ONE) * gradient
    square = BETA_TWO * square + (1.0 - BETA_TWO) * gradient * gradient
    corr_one = 1.0 - BETA_ONE**STEP
    corr_two = 1.0 - BETA_TWO**STEP
    update = moment / corr_one / (jnp.sqrt(square / corr_two) + ADAM_EPS)
    weight = weight * (1.0 - rate * decay) - rate * update
    return (gradient, moment, square, weight)


def swap(axis, value, count, step):
    return lax.ppermute(value, axis, [(i, i ^ step) for i in range(count)])


def pick(array, index, dim=0):
    return lax.dynamic_index_in_dim(array, index, dim, keepdims=False)


def place(pieces, index):
    out = jnp.zeros((len(pieces),) + pieces[0].shape, pieces[0].dtype)
    for step, piece in enumerate(pieces):
        out = lax.dynamic_update_index_in_dim(out, piece, index ^ step, 0)
    return out


def gather_axis(value, axis, count, up_only=False):
    index = lax.axis_index(axis)
    pieces = [value]
    for step in range(1, count):
        routes = [(i, i ^ step) for i in range(count) if i < i ^ step or not up_only]
        pieces.append(lax.ppermute(value, axis, routes))
    return place(pieces, index)


def add_up(parts):
    total = parts[0].astype(jnp.float32)
    for part in parts[1:]:
        total = total + part.astype(jnp.float32)
    return total.astype(jnp.bfloat16)


def reduce_axis(array, axis, dim, count, down_only=False):
    index = lax.axis_index(axis)
    total = pick(array, index, dim).astype(jnp.float32)
    for step in range(1, count):
        routes = [(i, i ^ step) for i in range(count) if i ^ step < i or not down_only]
        part = lax.ppermute(pick(array, index ^ step, dim), axis, routes)
        total = total + part.astype(jnp.float32)
    return total


def hold(*values):
    return lax.optimization_barrier(values)


def to_owners(grad, sizes):
    xs, zs, ys = sizes
    grad = grad.reshape(xs, 2, zs, *grad.shape[1:])
    grad = reduce_axis(grad, "core", 1, 2).astype(jnp.bfloat16)
    grad = reduce_axis(grad, "x", 0, xs).astype(jnp.bfloat16)
    return reduce_axis(grad, "z", 0, zs).astype(jnp.bfloat16)


def tree_sum(value, axis, count):
    terms = [value] + [swap(axis, value, count, step) for step in range(1, count)]
    while len(terms) > 1:
        terms = [terms[i] + terms[i + 1] for i in range(0, len(terms), 2)]
    return terms[0]


def across(left, right, left_dim, right_dim):
    return lax.dot_general(
        left, right, (((left_dim,), (right_dim,)), ((), ())), preferred_element_type=jnp.float32
    )


def rotation(positions, rows):
    half = HD // 2
    freq = jnp.exp(jnp.arange(half, dtype=jnp.float32) * (-2.0 * math.log(BASE) / HD))
    angle = jnp.tile(freq[:, None] * positions.astype(jnp.float32)[None, :], (1, rows))
    return (jnp.cos(angle), jnp.sin(angle))


def turn(tensor, angles, sign):
    cosine, sine = angles[0], sign * angles[1]
    first, second = jnp.split(tensor.reshape(-1, 2, HD // 2, tensor.shape[-1]), 2, 1)
    return jnp.concatenate(
        [first * cosine - second * sine, second * cosine + first * sine], 1
    ).reshape(tensor.shape)


def attend_kernel(group, block, meta, q_ref, kv_ref, out_ref, log_ref, top, total, accum):
    ctx, length = meta[0], meta[1 + pl.program_id(1)]
    blocks_y = kv_ref.shape[0]
    top[...] = jnp.full(top.shape, NEG, jnp.float32)
    total[...] = jnp.zeros(total.shape, jnp.float32)
    accum[...] = jnp.zeros(accum.shape, jnp.float32)

    def step(index, masked):
        pair = kv_ref[index % blocks_y, index // blocks_y, 0, 0]
        keys = pair[:, :HD]
        values = pair.T[HD:]
        if masked:
            key_pos = index * block + lax.broadcasted_iota(jnp.int32, (block, block), 0)
            query_pos = ctx * block + lax.broadcasted_iota(jnp.int32, (block, block), 1)
            allowed = (key_pos <= query_pos) & (key_pos < length)
        heads = range(group)
        span = [slice(head * HD, (head + 1) * HD) for head in heads]
        scores = [
            jnp.dot(keys, q_ref[span[head]], preferred_element_type=jnp.float32) for head in heads
        ]
        if masked:
            scores = [jnp.where(allowed, part, NEG) for part in scores]
        old = top[...]
        new = jnp.maximum(
            old, jnp.concatenate([jnp.max(part, 0, keepdims=True) for part in scores], 0)
        )
        factor = jnp.exp(old - new)
        top[...] = new
        probs = [jnp.exp(scores[head] - new[head : head + 1]) for head in heads]
        total[...] = total[...] * factor + jnp.concatenate(
            [jnp.sum(part, 0, keepdims=True) for part in probs], 0
        )
        weighted = [
            jnp.dot(values, part.astype(jnp.bfloat16), preferred_element_type=jnp.float32)
            for part in probs
        ]
        for head in heads:
            accum[span[head]] = accum[span[head]] * factor[head : head + 1] + weighted[head]

    clear = jnp.minimum(ctx, length // block)
    last = jnp.minimum(ctx + 1, (length + block - 1) // block)
    pl.loop(0, clear)(lambda index: step(index, False))
    pl.loop(clear, last)(lambda index: step(index, True))
    for head in range(group):
        rows = slice(head * HD, (head + 1) * HD)
        out_ref[rows] = accum[rows] / total[head : head + 1]
    log_ref[0] = top[...] + jnp.log(total[...])


def attend_back_kernel(
    group, block, meta, q_ref, g_ref, out_ref, log_ref, kv_ref, dq_ref, dkv_ref, both, delta
):
    ctx, length = meta[0], meta[1 + pl.program_id(0)]
    blocks_y, blocks_z = kv_ref.shape[0], kv_ref.shape[1]
    dq_ref[...] = jnp.zeros(dq_ref.shape, jnp.float32)
    for head in range(group):
        rows = slice(head * HD, (head + 1) * HD)
        query, upper = q_ref[rows], g_ref[rows]
        both[head] = jnp.concatenate([query, upper], 0).T
        delta[head : head + 1] = jnp.sum(upper.astype(jnp.float32) * out_ref[rows], 0, keepdims=True)
    lane = lax.broadcasted_iota(jnp.int32, (block, 2 * HD), 1)

    def step(index, masked):
        pair = kv_ref[index % blocks_y, index // blocks_y, 0, 0]
        keys, values = pair[:, :HD], pair[:, HD:]
        keys_across = pair.T[:HD]
        if masked:
            key_pos = index * block + lax.broadcasted_iota(jnp.int32, (block, block), 0)
            query_pos = ctx * block + lax.broadcasted_iota(jnp.int32, (block, block), 1)
            allowed = (key_pos <= query_pos) & (key_pos < length)
        d_keys = jnp.zeros((block, 2 * HD), jnp.float32)
        d_values = jnp.zeros((block, 2 * HD), jnp.float32)
        heads = range(group)
        span = [slice(head * HD, (head + 1) * HD) for head in heads]
        scores = [
            jnp.dot(keys, q_ref[span[head]], preferred_element_type=jnp.float32) for head in heads
        ]
        d_probs = [
            jnp.dot(values, g_ref[span[head]], preferred_element_type=jnp.float32) for head in heads
        ]
        probs = [jnp.exp(scores[head] - log_ref[0, head : head + 1]) for head in heads]
        if masked:
            probs = [jnp.where(allowed, part, 0.0) for part in probs]
        d_scores = [
            (probs[head] * (d_probs[head] - delta[head : head + 1])).astype(jnp.bfloat16)
            for head in heads
        ]
        probs = [part.astype(jnp.bfloat16) for part in probs]
        d_query = [
            jnp.dot(keys_across, part, preferred_element_type=jnp.float32) for part in d_scores
        ]
        for head in heads:
            d_keys += jnp.dot(d_scores[head], both[head], preferred_element_type=jnp.float32)
        for head in heads:
            d_values += jnp.dot(probs[head], both[head], preferred_element_type=jnp.float32)
        for head in heads:
            dq_ref[span[head]] += d_query[head]
        merged = jnp.where(lane < HD, d_keys, d_values)
        dkv_ref[index % blocks_y, index // blocks_y, 0] = merged.astype(jnp.bfloat16)

    clear = jnp.minimum(ctx, length // block)
    last = jnp.minimum(ctx + 1, (length + block - 1) // block)
    pl.loop(0, clear)(lambda index: step(index, False))
    pl.loop(clear, last)(lambda index: step(index, True))

    @pl.loop(last, blocks_y * blocks_z)
    def _(index):
        dkv_ref[index % blocks_y, index // blocks_y, 0] = jnp.zeros(
            (block, 2 * HD), jnp.bfloat16
        )


def attention(meta, query, all_kv, block):
    ys, zs, _, rows, _, _ = all_kv.shape
    group = HEADS // KVH
    wide = pl.BlockSpec((group * HD, block), lambda h, r, meta: (h, r))
    pairs = pl.BlockSpec((ys, zs, 1, 1, block, 2 * HD), lambda h, r, meta: (0, 0, h, r, 0, 0))
    logs = pl.BlockSpec((1, group, block), lambda h, r, meta: (h, 0, r))
    work = rows * HEADS * block * ys * zs * block
    return pl.pallas_call(
        functools.partial(attend_kernel, group, block),
        grid_spec=pltpu.PrefetchScalarGridSpec(
            num_scalar_prefetch=1,
            grid=(KVH, rows),
            in_specs=[wide, pairs],
            out_specs=[wide, logs],
            scratch_shapes=[
                pltpu.VMEM((group, block), jnp.float32),
                pltpu.VMEM((group, block), jnp.float32),
                pltpu.VMEM((group * HD, block), jnp.float32),
            ],
        ),
        out_shape=[
            jax.ShapeDtypeStruct((QD, rows * block), jnp.float32),
            jax.ShapeDtypeStruct((KVH, group, rows * block), jnp.float32),
        ],
        compiler_params=pltpu.CompilerParams(vmem_limit_bytes=32 * 2**20),
        cost_estimate=pl.CostEstimate(
            flops=4 * work * HD, bytes_accessed=4 * all_kv.size, transcendentals=work
        ),
        name="attend",
    )(meta, query, all_kv)


def attention_back(h, meta, query, upper, attended, logs, all_kv, block):
    ys, zs, _, rows, _, _ = all_kv.shape
    group = HEADS // KVH
    wide = pl.BlockSpec((group * HD, block), lambda r, meta: (h, r))
    narrow = pl.BlockSpec((group * HD, block), lambda r, meta: (0, r))
    pairs = pl.BlockSpec((ys, zs, 1, 1, block, 2 * HD), lambda r, meta: (0, 0, h, r, 0, 0))
    terms = pl.BlockSpec((ys, zs, 1, block, 2 * HD), lambda r, meta: (0, 0, r, 0, 0))
    log_spec = pl.BlockSpec((1, group, block), lambda r, meta: (h, 0, r))
    work = rows * group * block * ys * zs * block
    return pl.pallas_call(
        functools.partial(attend_back_kernel, group, block),
        grid_spec=pltpu.PrefetchScalarGridSpec(
            num_scalar_prefetch=1,
            grid=(rows,),
            in_specs=[wide, wide, wide, log_spec, pairs],
            out_specs=[narrow, terms],
            scratch_shapes=[
                pltpu.VMEM((group, block, 2 * HD), jnp.bfloat16),
                pltpu.VMEM((group, block), jnp.float32),
            ],
        ),
        out_shape=[
            jax.ShapeDtypeStruct((group * HD, rows * block), jnp.float32),
            jax.ShapeDtypeStruct((ys, zs, rows, block, 2 * HD), jnp.bfloat16),
        ],
        compiler_params=pltpu.CompilerParams(vmem_limit_bytes=32 * 2**20),
        cost_estimate=pl.CostEstimate(
            flops=10 * work * HD, bytes_accessed=4 * all_kv.size, transcendentals=work
        ),
        name="attend_back",
    )(meta, query, upper, attended, logs, all_kv)


def layer(
    sizes,
    inputs,
    cotangent,
    lengths,
    qkv_weight,
    out_weight,
    gate_up_weight,
    down_weight,
    gains_biases,
    qkv_moment,
    qkv_square,
    out_moment,
    out_square,
    gate_up_moment,
    gate_up_square,
    down_moment,
    down_square,
    small_moment,
    small_square,
):
    xs, zs, ys = sizes
    everyone = ("x", "core", "z", "y")
    chips = ("x", "z", "y")
    low = jnp.bfloat16
    rows, block_len, width = inputs.shape
    tokens = rows * block_len
    core, y_index = lax.axis_index("core"), lax.axis_index("y")
    ctx_index = lax.axis_index("z") * ys + y_index
    positions = ctx_index * block_len + jnp.arange(block_len, dtype=jnp.int32)
    kv_width = KVH * HD
    qkv_width = QD + 2 * kv_width
    scale = HD ** (-0.5)
    share = qkv_weight.shape[0]
    small_share = gains_biases.shape[0]
    ff_share = down_weight.shape[0]
    ff_slab = ff_share * zs * ys
    half = FF // 2
    x_index, z_index = lax.axis_index("x"), lax.axis_index("z")

    small_row = jnp.zeros((1, qkv_width), low).at[0, :small_share].set(gains_biases.astype(low))
    own_attn = jnp.concatenate([qkv_weight.astype(low), out_weight.astype(low)], 1)
    own_attn = jnp.concatenate([own_attn, jnp.pad(small_row, ((0, 0), (0, D)))], 0)
    other = swap("y", own_attn, ys, 1)
    lower = jnp.where(y_index == 0, own_attn, other)
    upper = jnp.where(y_index == 0, other, own_attn)
    pair_out = jnp.concatenate([lower[:share, qkv_width:], upper[:share, qkv_width:]], 0)
    lower, upper = lower[:, :qkv_width], upper[:, :qkv_width]
    spare = jnp.zeros((-2 * (share + 1) % 8, qkv_width), low)
    full_qkv = gather_axis(
        jnp.concatenate([lower[:share], upper[:share], lower[share:], upper[share:], spare], 0),
        "z",
        zs,
    )

    own_gu = (
        gate_up_weight.astype(low)
        .reshape(share, 2, xs, 2, ff_slab)
        .transpose(3, 1, 0, 2, 4)
        .reshape(4, share, half)
    )
    quad = core * 2 + y_index
    quads = place(
        [pick(own_gu, quad)]
        + [swap(("core", "y"), pick(own_gu, quad ^ step), 4, step) for step in range(1, 4)],
        quad,
    ).reshape(2, 2 * share, half)
    quads = jnp.concatenate([quads[0], pair_out, quads[1]], 1)
    quads = [quads] + [swap("z", quads, zs, step) for step in range(1, zs)]
    full_qkv = gather_axis(gather_axis(full_qkv, "x", xs), "core", 2).swapaxes(0, 1)
    full_small = full_qkv[..., 2 * share : 2 * share + ys, :small_share].reshape(-1)
    full_qkv = full_qkv[..., : 2 * share, :].reshape(D, qkv_width)
    full_down = lax.all_gather(down_weight.astype(low), chips, axis=0, tiled=True)

    small_used = full_small.astype(jnp.float32)
    gain_attn = small_used[:D]
    gain_mlp = small_used[D : 2 * D]
    bias = small_used[2 * D :]
    state = inputs.reshape(tokens, D).astype(jnp.float32)
    inverse_attn = lax.rsqrt(jnp.mean(state * state, -1, keepdims=True) + EPS)
    normed = (state * inverse_attn * gain_attn).astype(low)
    qkv = across(full_qkv, normed, 0, 1) + bias[:, None]
    angles = rotation(positions, rows)
    query = (turn(qkv[:QD], angles, 1.0) * scale).astype(low)
    keys = turn(qkv[QD : QD + kv_width], angles, 1.0).astype(low)
    values = qkv[QD + kv_width :].astype(low)
    own_kv = jnp.concatenate(
        [keys.reshape(KVH, HD, tokens), values.reshape(KVH, HD, tokens)], 1
    ).transpose(0, 2, 1)
    own_kv = own_kv.reshape(KVH, rows, block_len, 2 * HD)

    own_kv, quads = hold(own_kv, quads)
    all_kv = gather_axis(own_kv, "z", zs, True)
    first = place([part[:, : half + D] for part in quads], z_index)
    second = place([part[:, half + D :] for part in quads], z_index)
    first = [first] + [swap("x", first, xs, step) for step in range(1, xs)]
    second = [second, swap("y", second, ys, 1)]
    all_kv, first, second = hold(all_kv, first, second)
    all_kv = gather_axis(all_kv, "y", ys)
    first = place(first, x_index)
    first, full_out = first[..., :half], first[..., half:]
    full_out = gather_axis(full_out, "core", 2).swapaxes(0, 1).reshape(QD, D)
    second = place(second, y_index)
    second = [second] + [swap("x", second, xs, step) for step in range(1, xs)]
    all_kv, first = hold(all_kv, first)
    first = [first, swap("y", first, ys, 1)]
    meta = jnp.concatenate([ctx_index.astype(jnp.int32).reshape(1), lengths])
    attended, logs = attention(meta, query, all_kv, block_len)
    attended, first, second = hold(attended, first, second)
    second = place(second, x_index)
    is_gate = y_index == 0
    first = [jnp.where(is_gate, first[0], first[1]), jnp.where(is_gate, first[1], first[0])]
    full_gate = jnp.stack([first[0], second[:, 0]], 1).reshape(D, half)
    full_up = jnp.stack([first[1], second[:, 1]], 1).reshape(D, half)
    mixed_low = attended.astype(low)
    hidden_state = state + across(mixed_low, full_out, 0, 0)
    inverse_mlp = lax.rsqrt(jnp.mean(hidden_state * hidden_state, -1, keepdims=True) + EPS)
    normed2 = (hidden_state * inverse_mlp * gain_mlp).astype(low)
    valid = (positions[None, :] < lengths[:, None]).astype(jnp.float32)
    upstream = cotangent.reshape(tokens, D).astype(jnp.float32) * valid.reshape(tokens, 1)

    def pair(value):
        return jnp.concatenate([value, swap("core", value, 2, 1)], 0)

    def pair_sum(value):
        return value[:tokens] + swap("core", value[tokens:], 2, 1)

    pair_up = pair(upstream.astype(low))
    pair_normed = pair(normed2)
    gate = jnp.dot(pair_normed, full_gate, preferred_element_type=jnp.float32)
    up_part = jnp.dot(pair_normed, full_up, preferred_element_type=jnp.float32)
    sigma = jax.nn.sigmoid(gate)
    activated = gate * sigma
    inner = (activated * up_part).astype(low)
    d_inner = against_weight(pair_up, full_down)
    d_gate = (d_inner * up_part * sigma * (1.0 + gate * (1.0 - sigma))).astype(low)
    d_up = (d_inner * activated).astype(low)
    grad_down = across_tokens(inner, pair_up).astype(low)
    grad_down, d_gate, d_up = hold(grad_down, d_gate, d_up)
    red_down = lax.psum_scatter(grad_down, chips, scatter_dimension=0, tiled=True)
    red_down = red_down.astype(jnp.float32)
    grad_gate = across_tokens(pair_normed, d_gate).astype(low)
    grad_up = across_tokens(pair_normed, d_up).astype(low)
    grad_gate, grad_up, d_gate, d_up = hold(grad_gate, grad_up, d_gate, d_up)
    grad_gate = grad_gate.reshape(xs, 2, zs, 2 * share, half)
    grad_up = grad_up.reshape(xs, 2, zs, 2 * share, half)

    first = [grad_gate[:, 0], grad_up[:, 0]]
    first = [jnp.where(is_gate, first[0], first[1]), jnp.where(is_gate, first[1], first[0])]
    first[1] = swap("y", first[1], ys, 1)
    second = jnp.stack([grad_gate[:, 1], grad_up[:, 1]], 1)
    second = [pick(second, x_index)] + [
        swap("x", pick(second, x_index ^ step), xs, step) for step in range(1, xs)
    ]
    d_normed2 = pair_sum(against_weight(d_gate, full_gate) + against_weight(d_up, full_up))
    output = hidden_state + pair_sum(jnp.dot(inner, full_down, preferred_element_type=jnp.float32))

    change_mlp, grad_gain_mlp = norm_back(hidden_state, inverse_mlp, gain_mlp, d_normed2)
    d_hidden = upstream + change_mlp
    d_hidden_low = d_hidden.astype(low)
    grad_out = across(mixed_low, d_hidden_low, 1, 0)
    d_mixed = across(full_out, d_hidden_low, 1, 1).astype(low)
    grad_out = grad_out.astype(low).reshape(xs, 2, zs, 2 * share, D)
    grad_out = reduce_axis(grad_out, "core", 1, 2).astype(low)

    d_query, kv_terms = [None] * KVH, [None] * KVH
    d_query[0], kv_terms[0] = attention_back(
        0, meta, query, d_mixed, attended, logs, all_kv, block_len
    )
    first, second, d_query[0] = hold(first, second, d_query[0])
    first, second = add_up(first), add_up(second)
    first = jnp.concatenate([first, grad_out], -1)
    kv_terms[0] = reduce_axis(kv_terms[0], "y", 0, ys).astype(low)
    first, second, query = hold(first, second, query)
    first = [pick(first, x_index)] + [
        swap("x", pick(first, x_index ^ step), xs, step) for step in range(1, xs)
    ]
    second = [pick(second, y_index), swap("y", pick(second, 1 - y_index), ys, 1)]
    d_query[1], kv_terms[1] = attention_back(
        1, meta, query, d_mixed, attended, logs, all_kv, block_len
    )
    first, second, d_query[1] = hold(first, second, d_query[1])
    first, second = add_up(first), add_up(second)
    kv_terms[1] = reduce_axis(kv_terms[1], "y", 0, ys).astype(low)
    kv_grads = reduce_axis(jnp.stack(kv_terms, 1), "z", 0, zs, True)
    d_query = jnp.concatenate(d_query, 0)
    red_quads = reduce_axis(jnp.concatenate([first, second], -1), "z", 0, zs).astype(low)
    red_out = red_quads[:, half : half + D]
    red_quads = jnp.stack([red_quads[:, :half], red_quads[:, half + D :]], 0)
    red_quads = red_quads.reshape(4, share, half)
    kv_grads = kv_grads.reshape(KVH, tokens, 2 * HD).transpose(0, 2, 1)
    d_qkv = jnp.concatenate(
        [
            turn(d_query * scale, angles, -1.0),
            turn(kv_grads[:, :HD].reshape(kv_width, tokens), angles, -1.0),
            kv_grads[:, HD:].reshape(kv_width, tokens),
        ],
        0,
    ).astype(low)
    grad_bias = jnp.sum(d_qkv.astype(jnp.float32), 1)
    grad_qkv = across(normed, d_qkv, 0, 1)
    d_normed = across(d_qkv, full_qkv, 0, 1)
    change_attn, grad_gain_attn = norm_back(state, inverse_attn, gain_attn, d_normed)
    input_grad = (d_hidden + change_attn).astype(low)
    grad_small = jnp.concatenate([grad_gain_attn, grad_gain_mlp, grad_bias])

    grad_small = grad_small.astype(low).reshape(-1, ys, small_share)
    grad_small = jnp.pad(grad_small, ((0, 0), (0, 8 - ys), (0, qkv_width - small_share)))
    grad_qkv = jnp.concatenate(
        [grad_qkv.astype(low).reshape(-1, ys * share, qkv_width), grad_small], 1
    )
    red_qkv = to_owners(grad_qkv, sizes)

    red_small = red_qkv[ys * share : ys * share + ys]
    red_qkv = red_qkv[: ys * share].reshape(ys, share, qkv_width)
    red_out = red_out.reshape(ys, share, D)
    along = jnp.zeros((ys, -share % 8, qkv_width + D), low)
    along = along.at[:, 0, :qkv_width].set(red_small)
    along = jnp.concatenate([jnp.concatenate([red_qkv, red_out], 2), along], 1)
    mine = pick(along, y_index).astype(jnp.float32)
    mine = mine + swap("y", pick(along, 1 - y_index), ys, 1).astype(jnp.float32)
    red_qkv, red_out = mine[:share, :qkv_width], mine[:share, qkv_width:]
    red_small = mine[share, :small_share]
    red_gu = place(
        [pick(red_quads, quad)]
        + [swap(("core", "y"), pick(red_quads, quad ^ step), 4, step) for step in range(1, 4)],
        quad,
    )
    red_gu = (
        red_gu.reshape(2, 2, share, xs, ff_slab).transpose(2, 1, 3, 0, 4).reshape(share, 2 * FF)
    ).astype(jnp.float32)

    local_square = (
        jnp.sum(red_qkv * red_qkv)
        + jnp.sum(red_out * red_out)
        + jnp.sum(red_gu * red_gu)
        + jnp.sum(red_down * red_down)
        + jnp.sum(red_small * red_small)
    ).reshape(1)
    square_sum = tree_sum(local_square, "core", 2)
    square_sum = tree_sum(square_sum, ("x", "y"), xs * ys)
    square_sum = tree_sum(square_sum, "z", zs)[0]
    grad_norm = jnp.sqrt(square_sum)
    factor = CLIP / jnp.maximum(grad_norm, CLIP)
    qkv_new = adam_step(red_qkv, qkv_moment, qkv_square, qkv_weight, factor, RATES[0], DECAYS[0])
    out_new = adam_step(red_out, out_moment, out_square, out_weight, factor, RATES[1], DECAYS[1])
    gu_new = adam_step(
        red_gu, gate_up_moment, gate_up_square, gate_up_weight, factor, RATES[2], DECAYS[2]
    )
    down_new = adam_step(
        red_down, down_moment, down_square, down_weight, factor, RATES[3], DECAYS[3]
    )
    small_new = adam_step(
        red_small, small_moment, small_square, gains_biases, factor, RATES[4], DECAYS[4]
    )
    return (
        output.astype(low).reshape(inputs.shape),
        input_grad.reshape(inputs.shape),
        grad_norm,
        *qkv_new,
        *out_new,
        *gu_new,
        *down_new,
        *small_new,
    )


def solution(mesh):
    dp, ctx = mesh.shape["dp"], mesh.shape["ctx"]
    sizes = (dp // 2, ctx // 2, 2)
    fine = Mesh(mesh.devices.reshape(dp // 2, 2, ctx // 2, 2), ("x", "core", "z", "y"))
    seqs, blocks = ("x", "core"), ("z", "y")
    token = P(seqs, blocks, None)
    matrix = P(seqs + blocks, None)
    vector = P(seqs + blocks)
    weights = (matrix,) * 4 + (vector,)
    states = (matrix,) * 8 + (vector,) * 2
    return jax.shard_map(
        functools.partial(layer, sizes),
        mesh=fine,
        in_specs=(token, token, P(seqs)) + weights + states,
        out_specs=(token, token, P()) + (matrix,) * 16 + (vector,) * 4,
        check_vma=False,
    )
```

time: 2500 us -> 651 us (0.26)
  blocking collectives: 1500 us -> 0 us
  waiting for transfers between devices: 492 us -> 258 us
  matrix products: 154 us -> 103 us
  local copies, waits for them, and re-layouts: 121 us -> 79.6 us
  starting transfers between devices: 153 us -> 117 us
    unnamed x3 -> x0, blocking collectives: 1460 us -> none
    all_gather x6 -> x1, waiting for transfers between devices: 279 us -> 10.9 us  [layer(): lax.all_gather(down_weight.astype(low), chips, axis=0, tiled=True)]
    ppermute x0 -> x54, waiting for transfers between devices: none -> 247 us  [the longest x30 109 us: swap(): return lax.ppermute(value, axis, [(i, i ^ step) for i in range(count)])]
    reduce_scatter x2 -> x0, waiting for transfers between devices: 178 us -> none  [the longest x1 112 us: on_device(): lax.psum_scatter(key_terms.reshape(seq_len, rows, kv_width).astype(jnp.bf...]
    unnamed x13 -> x1, starting transfers between devices: 152 us -> 0.04 us
    ppermute x0 -> x54, starting transfers between devices: none -> 117 us  [the longest x14 45.7 us: reduce_axis(): part = lax.ppermute(pick(array, index ^ step, dim), axis, routes)]
    unnamed x117 -> x145, local copies, waits for them, and re-layouts: 82.3 us -> 10.3 us
    psum x1 -> x0, blocking collectives: 39.3 us -> none  [on_device(): square_sum = lax.psum(local_square, ('dp', 'ctx'))]
  transfers between devices with their start and end apart: 21 -> 56, of which waited for: 9 -> 24; matrix products, arithmetic and copies ran while one was open for 64% -> 20% of each run, Pallas kernels for 0% -> 2%
where the time goes in v1:
time: 651 us; the launch traced here: 645 us
  waiting for transfers between devices  258 us (40%)
  starting transfers between devices  117 us (18%)
  matrix products  103 us (16%)
  local copies, waits for them, and re-layouts  79.6 us (12%)
  other arithmetic  47 us (7%)
  between operations  25.2 us (4%)
  Pallas kernels  14.6 us (2%)
    ppermute x30, waiting for transfers between devices, swap(): return lax.ppermute(value, axis, [(i, i ^ step) for i in range(count)])  109 us
    ppermute x14, waiting for transfers between devices, reduce_axis(): part = lax.ppermute(pick(array, index ^ step, dim), axis, routes)  105 us
    ppermute x14, starting transfers between devices, reduce_axis(): part = lax.ppermute(pick(array, index ^ step, dim), axis, routes)  45.7 us
    ppermute x30, starting transfers between devices, swap(): return lax.ppermute(value, axis, [(i, i ^ step) for i in range(count)])  42.8 us
    dot_general x3, matrix products, against_weight(): lax.dot_general(values, weight, (((values.ndim - 1,), (1,)), ((), ())), p...  42.3 us
    dynamic_update_slice x38, local copies, waits for them, and re-layouts, place(): out = lax.dynamic_update_index_in_dim(out, piece, index ^ step, 0)  36.8 us
    ppermute x10, waiting for transfers between devices, gather_axis(): pieces.append(lax.ppermute(value, axis, routes))  33.4 us
    ppermute x10, starting transfers between devices, gather_axis(): pieces.append(lax.ppermute(value, axis, routes))  28.5 us
  transfers between devices with their start and end apart: 56, of which 24 were waited for; matrix products, arithmetic and copies ran while one was open for 20% of the time, Pallas kernels for 2%

profile of v1, /device:TPU:0, one launch (start us, length us, event | category | flops | bytes accessed | tf_op | source)
XLA Modules:
  0.0 644.7 jit_solution(8813474979437659707)
XLA Ops:
  43.8 9.7 %collective-permute-done.4 = bf16[4,64,1152]{2,1,0:T(8,128)(2,1)} collective-permute-done((bf16[4,64,1152]{2,1,0:T(8,128)(2,1)S(1)}, bf16[4,64,1152]{2,1,0:T(8,128)(2,1)}, u32[]{:S(2)}, u32[]{:S(2)}) %collective-permute-start.4) | collective-permute-done | bytes 589856 | tf_op jit(solution)/shard_map/ppermute | solution.py:84
  69.1 18.1 %collective-permute-done.9 = bf16[56,5760]{1,0:T(8,128)(2,1)} collective-permute-done((bf16[56,5760]{1,0:T(8,128)(2,1)S(1)}, bf16[56,5760]{1,0:T(8,128)(2,1)}, u32[]{:S(2)}, u32[]{:S(2)}) %collective-permute-start.9) | collective-permute-done | bytes 645152 | tf_op jit(solution)/shard_map/ppermute | solution.py:65
  87.2 17.3 %collective-permute-done.10 = bf16[56,5760]{1,0:T(8,128)(2,1)} collective-permute-done((bf16[56,5760]{1,0:T(8,128)(2,1)S(1)}, bf16[56,5760]{1,0:T(8,128)(2,1)}, u32[]{:S(2)}, u32[]{:S(2)}) %collective-permute-start.10) | collective-permute-done | bytes 645152 | tf_op jit(solution)/shard_map/ppermute | solution.py:65
  113.9 16.3 %collective-permute-start.12 = (bf16[2,2,256,128]{3,2,1,0:T(8,128)(2,1)}, bf16[2,2,256,128]{3,2,1,0:T(8,128)(2,1)}, u32[]{:S(2)}, u32[]{:S(2)}) collective-permute-start(bf16[2,2,256,128]{3,2,1,0:T(8,128)(2,1)} %bitcast.21), channel_id=1, source_target_pairs={{0,2},{4,6},{1,3},{5,7},{8,10},{12,14},{9,11},{13,15},{16,18},{20,... | collective-permute-start | bytes 786440 | tf_op jit(solution)/shard_map/ppermute | solution.py:84
  157.0 11.8 %collective-permute-done.17 = bf16[4,2,2,256,128]{4,3,2,1,0:T(8,128)(2,1)S(1)} collective-permute-done((bf16[4,2,2,256,128]{4,3,2,1,0:T(8,128)(2,1)S(1)}, bf16[4,2,2,256,128]{4,3,2,1,0:T(8,128)(2,1)S(1)}, u32[]{:S(2)}, u32[]{:S(2)}) %collective-permute-start.17) | collective-permute-done | bytes 1048608 | tf_op jit(solution)/shard_map/ppermute | solution.py:84
  185.4 19.6 %collective-permute-done.19 = bf16[2,4,56,2432]{3,2,1,0:T(8,128)(2,1)} collective-permute-done((bf16[2,4,56,2432]{3,2,1,0:T(8,128)(2,1)}, bf16[2,4,56,2432]{3,2,1,0:T(8,128)(2,1)}, u32[]{:S(2)}, u32[]{:S(2)}) %collective-permute-start.19) | collective-permute-done | bytes 2179104 | tf_op jit(solution)/shard_map/ppermute | solution.py:65
  205.0 16.5 %collective-permute-done.18 = bf16[2,4,56,2432]{3,2,1,0:T(8,128)(2,1)} collective-permute-done((bf16[2,4,56,2432]{3,2,1,0:T(8,128)(2,1)}, bf16[2,4,56,2432]{3,2,1,0:T(8,128)(2,1)}, u32[]{:S(2)}, u32[]{:S(2)}) %collective-permute-start.18) | collective-permute-done | bytes 2179104 | tf_op jit(solution)/shard_map/ppermute | solution.py:65
  234.1 8.8 %fusion.82 = f32[1024,2432]{1,0:T(8,128)} fusion(bf16[896,2432]{1,0:T(8,128)(2,1)S(1)} %bitcast.320, bf16[512,896]{1,0:T(8,128)(2,1)S(1)} %collective-permute-done.21, bf16[512,896]{1,0:T(8,128)(2,1)S(1)} %multiply_convert_fusion.3), kind=kOutput, calls=%fused_computation.277 | convolution fusion | flops 4466409472 | bytes 16154624 | tf_op jit(solution)/shard_map/dot_general | solution.py:451
  242.9 8.7 %fusion.81 = f32[1024,2432]{1,0:T(8,128)} fusion(bf16[896,2432]{1,0:T(8,128)(2,1)S(1)} %bitcast.324, bf16[512,896]{1,0:T(8,128)(2,1)S(1)} %collective-permute-done.21, bf16[512,896]{1,0:T(8,128)(2,1)S(1)} %multiply_convert_fusion.3), kind=kOutput, calls=%fused_computation.276 | convolution fusion | flops 4466409472 | bytes 16154624 | tf_op jit(solution)/shard_map/dot_general | solution.py:452
  251.6 10.9 %all-gather.2.cloned.1.call-done = bf16[2432,896]{1,0:T(8,128)(2,1)} async-done(((bf16[152,896]{1,0:T(8,128)(2,1)}), bf16[2432,896]{1,0:T(8,128)(2,1)}) %all-gather.2.cloned.1.call-update) | async-done | bytes 4358160 | tf_op jit(solution)/shard_map/all_gather | solution.py:394
  262.5 27.2 %multiply_convert_fusion = (bf16[1024,2432]{1,0:T(8,128)(2,1)}, bf16[1024,2432]{1,0:T(8,128)(2,1)}, bf16[1024,2432]{1,0:T(8,128)(2,1)}) fusion(f32[1024,2432]{1,0:T(8,128)} %fusion.82, f32[1024,2432]{1,0:T(8,128)} %fusion.81, bf16[2432,896]{1,0:T(8,128)(2,1)} %all-gather.2.cloned.1.call-done, bf16[512,896]{1,0:T(8,128)(2,1)} %collective-permute-done.23, ...), kind=kOutput, calls=%fused_computation | convolution fusion | flops 4503764992 | bytes 41058304 | tf_op jit(solution)/shard_map/dot_general | solution.py:41
  289.7 10.4 %convolution_convert_fusion.2 = bf16[2432,896]{1,0:T(8,128)(2,1)} fusion(bf16[1024,2432]{1,0:T(8,128)(2,1)} %get-tuple-element.158, bf16[512,896]{1,0:T(8,128)(2,1)} %collective-permute-done.23, bf16[512,896]{1,0:T(8,128)(2,1)} %fusion.12), kind=kOutput, calls=%fused_computation.7 | convolution fusion | flops 4468588544 | bytes 11173888 | tf_op jit(solution)/shard_map/dot_general | solution.py:35
  300.1 7.8 %convolution_convert_fusion.1 = bf16[896,2432]{1,0:T(8,128)(2,1)S(1)} fusion(bf16[1024,2432]{1,0:T(8,128)(2,1)} %get-tuple-element.110, bf16[512,896]{1,0:T(8,128)(2,1)} %copy-done.60, bf16[512,896]{1,0:T(8,128)(2,1)S(1)} %multiply_convert_fusion.3), kind=kOutput, calls=%fused_computation.6 | convolution fusion | flops 4468588544 | bytes 11173888 | tf_op jit(solution)/shard_map/dot_general | solution.py:35
  313.5 7.6 %fusion.95 = f32[1024,896]{1,0:T(8,128)S(1)} fusion(bf16[1024,2432]{1,0:T(8,128)(2,1)} %get-tuple-element.110, bf16[896,2432]{1,0:T(8,128)(2,1)S(1)} %bitcast.323), kind=kOutput, calls=%fused_computation.285 | convolution fusion | flops 4462739456 | bytes 13008896 | tf_op jit(solution)/shard_map/dot_general | solution.py:41
  321.2 7.5 %convolution_add_fusion.1 = f32[1024,896]{1,0:T(8,128)S(1)} fusion(f32[1024,896]{1,0:T(8,128)S(1)} %fusion.95, bf16[1024,2432]{1,0:T(8,128)(2,1)} %get-tuple-element.111, bf16[896,2432]{1,0:T(8,128)(2,1)S(1)} %bitcast.327), kind=kOutput, calls=%fused_computation.83 | convolution fusion | flops 4463656960 | bytes 16678912 | tf_op jit(solution)/shard_map/dot_general | solution.py:41
  360.6 30.9 %collective-permute-done.25 = bf16[2,4,56,2432]{3,2,1,0:T(8,128)(2,1)S(1)} collective-permute-done((bf16[2,4,56,2432]{3,2,1,0:T(8,128)(2,1)}, bf16[2,4,56,2432]{3,2,1,0:T(8,128)(2,1)S(1)}, u32[]{:S(2)}, u32[]{:S(2)}) %collective-permute-start.25) | collective-permute-done | bytes 2179104 | tf_op jit(solution)/shard_map/ppermute | solution.py:65
  393.2 8.7 %collective-permute-done.30 = bf16[4,2,256,128]{3,2,1,0:T(8,128)(2,1)S(1)} collective-permute-done((bf16[4,2,256,128]{3,2,1,0:T(8,128)(2,1)S(1)}, bf16[4,2,256,128]{3,2,1,0:T(8,128)(2,1)S(1)}, u32[]{:S(2)}, u32[]{:S(2)}) %collective-permute-start.30) | collective-permute-done | bytes 524320 | tf_op jit(solution)/shard_map/ppermute | solution.py:100
  415.1 8.8 %collective-permute-done.31 = bf16[4,2,256,128]{3,2,1,0:T(8,128)(2,1)S(1)} collective-permute-done((bf16[4,2,256,128]{3,2,1,0:T(8,128)(2,1)S(1)}, bf16[4,2,256,128]{3,2,1,0:T(8,128)(2,1)S(1)}, u32[]{:S(2)}, u32[]{:S(2)}) %collective-permute-start.31) | collective-permute-done | bytes 524320 | tf_op jit(solution)/shard_map/ppermute | solution.py:100
  429.0 15.0 %collective-permute-done.34 = bf16[2,2,256,128]{3,2,1,0:T(8,128)(2,1)S(1)} collective-permute-done((bf16[2,2,256,128]{3,2,1,0:T(8,128)(2,1)}, bf16[2,2,256,128]{3,2,1,0:T(8,128)(2,1)S(1)}, u32[]{:S(2)}, u32[]{:S(2)}) %collective-permute-start.34) | collective-permute-done | bytes 262176 | tf_op jit(solution)/shard_map/ppermute | solution.py:100
  444.0 12.1 %collective-permute-done.33 = bf16[2,2,256,128]{3,2,1,0:T(8,128)(2,1)S(1)} collective-permute-done((bf16[2,2,256,128]{3,2,1,0:T(8,128)(2,1)S(1)}, bf16[2,2,256,128]{3,2,1,0:T(8,128)(2,1)S(1)}, u32[]{:S(2)}, u32[]{:S(2)}) %collective-permute-start.33) | collective-permute-done | bytes 262176 | tf_op jit(solution)/shard_map/ppermute | solution.py:100
  464.0 19.6 %collective-permute-start.42 = (bf16[56,5760]{1,0:T(8,128)(2,1)}, bf16[56,5760]{1,0:T(8,128)(2,1)}, u32[]{:S(2)}, u32[]{:S(2)}) collective-permute-start(bf16[56,5760]{1,0:T(8,128)(2,1)} %get-tuple-element.172), channel_id=1, source_target_pairs={{0,6},{2,4},{4,2},{6,0},{1,7},{3,5},{5,3},{7,1},{8,14},{10,12},{12... | collective-permute-start | bytes 1935368 | tf_op jit(solution)/shard_map/ppermute | solution.py:100
  492.1 14.5 %collective-permute-done.42 = bf16[56,5760]{1,0:T(8,128)(2,1)} collective-permute-done((bf16[56,5760]{1,0:T(8,128)(2,1)}, bf16[56,5760]{1,0:T(8,128)(2,1)}, u32[]{:S(2)}, u32[]{:S(2)}) %collective-permute-start.42) | collective-permute-done | bytes 645152 | tf_op jit(solution)/shard_map/ppermute | solution.py:100
  506.5 42.8 %collective-permute-done.41 = bf16[56,5760]{1,0:T(8,128)(2,1)} collective-permute-done((bf16[56,5760]{1,0:T(8,128)(2,1)}, bf16[56,5760]{1,0:T(8,128)(2,1)}, u32[]{:S(2)}, u32[]{:S(2)}) %collective-permute-start.41) | collective-permute-done | bytes 645152 | tf_op jit(solution)/shard_map/ppermute | solution.py:100
  566.1 9.9 %collective-permute-start.39 = (bf16[64,1152]{1,0:T(8,128)(2,1)}, bf16[64,1152]{1,0:T(8,128)(2,1)S(1)}, u32[]{:S(2)}, u32[]{:S(2)}) collective-permute-start(bf16[64,1152]{1,0:T(8,128)(2,1)} %get-tuple-element.192), channel_id=1, source_target_pairs={{0,6},{2,4},{4,2},{6,0},{1,7},{3,5},{5,3},{7,1},{8,14},{10,12},{12... | collective-permute-start | bytes 442376 | tf_op jit(solution)/shard_map/ppermute | solution.py:100
  (451 shorter events, 258.9 us)
Async XLA Ops:
  7.2 255.3 %all-gather.2.cloned.1.call-start = ((), (), s32[]{:S(2)}) async-start(), calls=%async_computation.1 | async-start | bytes 4630528 | tf_op jit(solution)/shard_map/all_gather | solution.py:394
  54.8 32.4 %collective-permute-start.9 = (bf16[56,5760]{1,0:T(8,128)(2,1)S(1)}, bf16[56,5760]{1,0:T(8,128)(2,1)}, u32[]{:S(2)}, u32[]{:S(2)}) collective-permute-start(bf16[56,5760]{1,0:T(8,128)(2,1)S(1)} %pad_maximum_fusion.9), channel_id=1, source_target_pairs={{0,2},{2,0},{4,6},{6,4},{1,3},{3,1},{5,7},{7,5},{8,10},{10,8},{12,... | collective-permute-start | bytes 1935368 | tf_op jit(solution)/shard_map/ppermute | solution.py:65
  58.5 46.0 %collective-permute-start.10 = (bf16[56,5760]{1,0:T(8,128)(2,1)S(1)}, bf16[56,5760]{1,0:T(8,128)(2,1)}, u32[]{:S(2)}, u32[]{:S(2)}) collective-permute-start(bf16[56,5760]{1,0:T(8,128)(2,1)S(1)} %pad_maximum_fusion.9), channel_id=1, source_target_pairs={{0,4},{2,6},{4,0},{6,2},{1,5},{3,7},{5,1},{7,3},{8,12},{10,14},{12... | collective-permute-start | bytes 1935368 | tf_op jit(solution)/shard_map/ppermute | solution.py:65
  59.7 44.9 %collective-permute-start.11 = (bf16[56,5760]{1,0:T(8,128)(2,1)S(1)}, bf16[56,5760]{1,0:T(8,128)(2,1)}, u32[]{:S(2)}, u32[]{:S(2)}) collective-permute-start(bf16[56,5760]{1,0:T(8,128)(2,1)S(1)} %pad_maximum_fusion.9), channel_id=1, source_target_pairs={{0,6},{2,4},{4,2},{6,0},{1,7},{3,5},{5,3},{7,1},{8,14},{10,12},{12... | collective-permute-start | bytes 1935368 | tf_op jit(solution)/shard_map/ppermute | solution.py:65
  107.8 37.9 %collective-permute-start.15 = (bf16[4,56,3328]{2,1,0:T(8,128)(2,1)S(1)}, bf16[4,56,3328]{2,1,0:T(8,128)(2,1)}, u32[]{:S(2)}, u32[]{:S(2)}) collective-permute-start(bf16[4,56,3328]{2,1,0:T(8,128)(2,1)S(1)} %bitcast_dynamic-update-slice_fusion.14), channel_id=1, source_target_pairs={{0,16},{16,0},{1,17},{17,1},{2,18},{18,2},{3,19},{19,3},{4,20},{20... | collective-permute-start | bytes 4472840 | tf_op jit(solution)/shard_map/ppermute | solution.py:65
  113.4 32.3 %collective-permute-start.16 = (bf16[4,56,2432]{2,1,0:T(8,128)(2,1)S(1)}, bf16[4,56,2432]{2,1,0:T(8,128)(2,1)}, u32[]{:S(2)}, u32[]{:S(2)}) collective-permute-start(bf16[4,56,2432]{2,1,0:T(8,128)(2,1)S(1)} %bitcast_dynamic-update-slice_fusion.18), channel_id=1, source_target_pairs={{0,1},{1,0},{2,3},{3,2},{4,5},{5,4},{6,7},{7,6},{8,9},{9,8},{10,11... | collective-permute-start | bytes 3268616 | tf_op jit(solution)/shard_map/ppermute | solution.py:65
  113.9 22.6 %collective-permute-start.12 = (bf16[2,2,256,128]{3,2,1,0:T(8,128)(2,1)}, bf16[2,2,256,128]{3,2,1,0:T(8,128)(2,1)}, u32[]{:S(2)}, u32[]{:S(2)}) collective-permute-start(bf16[2,2,256,128]{3,2,1,0:T(8,128)(2,1)} %bitcast.21), channel_id=1, source_target_pairs={{0,2},{4,6},{1,3},{5,7},{8,10},{12,14},{9,11},{13,15},{16,18},{20,... | collective-permute-start | bytes 786440 | tf_op jit(solution)/shard_map/ppermute | solution.py:84
  145.7 23.0 %collective-permute-start.17 = (bf16[4,2,2,256,128]{4,3,2,1,0:T(8,128)(2,1)S(1)}, bf16[4,2,2,256,128]{4,3,2,1,0:T(8,128)(2,1)S(1)}, u32[]{:S(2)}, u32[]{:S(2)}) collective-permute-start(bf16[4,2,2,256,128]{4,3,2,1,0:T(8,128)(2,1)S(1)} %bitcast_dynamic-update-slice_fusion.22), channel_id=1, source_target_pairs={{0,1},{1,0},{2,3},{3,2},{4,5},{5,4},{6,7},{7,6},{8,9},{9,8},{10,11... | collective-permute-start | bytes 3145736 | tf_op jit(solution)/shard_map/ppermute | solution.py:84
  155.8 49.2 %collective-permute-start.19 = (bf16[2,4,56,2432]{3,2,1,0:T(8,128)(2,1)}, bf16[2,4,56,2432]{3,2,1,0:T(8,128)(2,1)}, u32[]{:S(2)}, u32[]{:S(2)}) collective-permute-start(bf16[2,4,56,2432]{3,2,1,0:T(8,128)(2,1)} %bitcast_dynamic-update-slice_fusion.6), channel_id=1, source_target_pairs={{0,16},{16,0},{1,17},{17,1},{2,18},{18,2},{3,19},{19,3},{4,20},{20... | collective-permute-start | bytes 6537224 | tf_op jit(solution)/shard_map/ppermute | solution.py:65
  168.9 52.6 %collective-permute-start.18 = (bf16[2,4,56,2432]{3,2,1,0:T(8,128)(2,1)}, bf16[2,4,56,2432]{3,2,1,0:T(8,128)(2,1)}, u32[]{:S(2)}, u32[]{:S(2)}) collective-permute-start(bf16[2,4,56,2432]{3,2,1,0:T(8,128)(2,1)} %slice.248), channel_id=1, source_target_pairs={{0,1},{1,0},{2,3},{3,2},{4,5},{5,4},{6,7},{7,6},{8,9},{9,8},{10,11... | collective-permute-start | bytes 6537224 | tf_op jit(solution)/shard_map/ppermute | solution.py:65
  171.2 424.1 %reduce-scatter.5.cloned.1.call-start = ((), (), s32[]{:S(2)}) async-start(), calls=%async_computation.2 | async-start | bytes 4630528
  173.7 77.9 %collective-permute-start.23 = (bf16[512,896]{1,0:T(8,128)(2,1)}, bf16[512,896]{1,0:T(8,128)(2,1)}, u32[]{:S(2)}, u32[]{:S(2)}) collective-permute-start(bf16[512,896]{1,0:T(8,128)(2,1)} %fusion.12), channel_id=1, source_target_pairs={{0,8},{8,0},{1,9},{9,1},{2,10},{10,2},{3,11},{11,3},{4,12},{12,4},... | collective-permute-start | bytes 2752520 | tf_op jit(solution)/shard_map/ppermute | solution.py:65
  341.1 50.5 %collective-permute-start.25 = (bf16[2,4,56,2432]{3,2,1,0:T(8,128)(2,1)}, bf16[2,4,56,2432]{3,2,1,0:T(8,128)(2,1)S(1)}, u32[]{:S(2)}, u32[]{:S(2)}) collective-permute-start(bf16[2,4,56,2432]{3,2,1,0:T(8,128)(2,1)} %get-tuple-element.162), channel_id=1, source_target_pairs={{0,1},{1,0},{2,3},{3,2},{4,5},{5,4},{6,7},{7,6},{8,9},{9,8},{10,11... | collective-permute-start | bytes 6537224 | tf_op jit(solution)/shard_map/ppermute | solution.py:65
  343.1 49.1 %collective-permute-start.26 = (bf16[2,4,56,2432]{3,2,1,0:T(8,128)(2,1)S(1)}, bf16[2,4,56,2432]{3,2,1,0:T(8,128)(2,1)S(1)}, u32[]{:S(2)}, u32[]{:S(2)}) collective-permute-start(bf16[2,4,56,2432]{3,2,1,0:T(8,128)(2,1)S(1)} %get-tuple-element.159), channel_id=1, source_target_pairs={{0,16},{16,0},{1,17},{17,1},{2,18},{18,2},{3,19},{19,3},{4,20},{20... | collective-permute-start | bytes 6537224 | tf_op jit(solution)/shard_map/ppermute | solution.py:65
  355.6 46.2 %collective-permute-start.30 = (bf16[4,2,256,128]{3,2,1,0:T(8,128)(2,1)S(1)}, bf16[4,2,256,128]{3,2,1,0:T(8,128)(2,1)S(1)}, u32[]{:S(2)}, u32[]{:S(2)}) collective-permute-start(bf16[4,2,256,128]{3,2,1,0:T(8,128)(2,1)S(1)} %dynamic-slice_bitcast_fusion.7), channel_id=1, source_target_pairs={{0,1},{1,0},{2,3},{3,2},{4,5},{5,4},{6,7},{7,6},{8,9},{9,8},{10,11... | collective-permute-start | bytes 1572872 | tf_op jit(solution)/shard_map/ppermute | solution.py:100
  360.5 41.4 %collective-permute-start.27 = (bf16[2,4,56,896]{3,2,1,0:T(8,128)(2,1)S(1)}, bf16[2,4,56,896]{3,2,1,0:T(8,128)(2,1)S(1)}, u32[]{:S(2)}, u32[]{:S(2)}) collective-permute-start(bf16[2,4,56,896]{3,2,1,0:T(8,128)(2,1)S(1)} %dynamic-slice_bitcast_fusion.4), channel_id=1, source_target_pairs={{0,8},{8,0},{1,9},{9,1},{2,10},{10,2},{3,11},{11,3},{4,12},{12,4},... | collective-permute-start | bytes 2408456 | tf_op jit(solution)/shard_map/ppermute | solution.py:100
  412.9 43.8 %collective-permute-start.28 = (bf16[4,56,3328]{2,1,0:T(8,128)(2,1)}, bf16[4,56,3328]{2,1,0:T(8,128)(2,1)}, u32[]{:S(2)}, u32[]{:S(2)}) collective-permute-start(bf16[4,56,3328]{2,1,0:T(8,128)(2,1)} %get-tuple-element.168), channel_id=1, source_target_pairs={{0,16},{16,0},{1,17},{17,1},{2,18},{18,2},{3,19},{19,3},{4,20},{20... | collective-permute-start | bytes 4472840 | tf_op jit(solution)/shard_map/ppermute | solution.py:65
  415.1 41.6 %collective-permute-start.29 = (bf16[4,56,2432]{2,1,0:T(8,128)(2,1)}, bf16[4,56,2432]{2,1,0:T(8,128)(2,1)}, u32[]{:S(2)}, u32[]{:S(2)}) collective-permute-start(bf16[4,56,2432]{2,1,0:T(8,128)(2,1)} %get-tuple-element.173), channel_id=1, source_target_pairs={{0,1},{1,0},{2,3},{3,2},{4,5},{5,4},{6,7},{7,6},{8,9},{9,8},{10,11... | collective-permute-start | bytes 3268616 | tf_op jit(solution)/shard_map/ppermute | solution.py:65
  426.1 30.0 %collective-permute-start.33 = (bf16[2,2,256,128]{3,2,1,0:T(8,128)(2,1)S(1)}, bf16[2,2,256,128]{3,2,1,0:T(8,128)(2,1)S(1)}, u32[]{:S(2)}, u32[]{:S(2)}) collective-permute-start(bf16[2,2,256,128]{3,2,1,0:T(8,128)(2,1)S(1)} %get-tuple-element.182), channel_id=1, source_target_pairs={{4,0},{6,2},{5,1},{7,3},{12,8},{14,10},{13,9},{15,11},{20,16},{22,... | collective-permute-start | bytes 786440 | tf_op jit(solution)/shard_map/ppermute | solution.py:100
  427.4 28.7 %collective-permute-start.32 = (bf16[2,2,256,128]{3,2,1,0:T(8,128)(2,1)S(1)}, bf16[2,2,256,128]{3,2,1,0:T(8,128)(2,1)S(1)}, u32[]{:S(2)}, u32[]{:S(2)}) collective-permute-start(bf16[2,2,256,128]{3,2,1,0:T(8,128)(2,1)S(1)} %get-tuple-element.181), channel_id=1, source_target_pairs={{2,0},{6,4},{3,1},{7,5},{10,8},{14,12},{11,9},{15,13},{18,16},{22,... | collective-permute-start | bytes 786440 | tf_op jit(solution)/shard_map/ppermute | solution.py:100
  464.0 42.6 %collective-permute-start.42 = (bf16[56,5760]{1,0:T(8,128)(2,1)}, bf16[56,5760]{1,0:T(8,128)(2,1)}, u32[]{:S(2)}, u32[]{:S(2)}) collective-permute-start(bf16[56,5760]{1,0:T(8,128)(2,1)} %get-tuple-element.172), channel_id=1, source_target_pairs={{0,6},{2,4},{4,2},{6,0},{1,7},{3,5},{5,3},{7,1},{8,14},{10,12},{12... | collective-permute-start | bytes 1935368 | tf_op jit(solution)/shard_map/ppermute | solution.py:100
  483.5 65.8 %collective-permute-start.41 = (bf16[56,5760]{1,0:T(8,128)(2,1)}, bf16[56,5760]{1,0:T(8,128)(2,1)}, u32[]{:S(2)}, u32[]{:S(2)}) collective-permute-start(bf16[56,5760]{1,0:T(8,128)(2,1)} %get-tuple-element.171), channel_id=1, source_target_pairs={{0,4},{2,6},{4,0},{6,2},{1,5},{3,7},{5,1},{7,3},{8,12},{10,14},{12... | collective-permute-start | bytes 1935368 | tf_op jit(solution)/shard_map/ppermute | solution.py:100
  483.5 65.8 %collective-permute-start.40 = (bf16[56,5760]{1,0:T(8,128)(2,1)}, bf16[56,5760]{1,0:T(8,128)(2,1)}, u32[]{:S(2)}, u32[]{:S(2)}) collective-permute-start(bf16[56,5760]{1,0:T(8,128)(2,1)} %get-tuple-element.170), channel_id=1, source_target_pairs={{0,2},{2,0},{4,6},{6,4},{1,3},{3,1},{5,7},{7,5},{8,10},{10,8},{12,... | collective-permute-start | bytes 1935368 | tf_op jit(solution)/shard_map/ppermute | solution.py:100
  492.0 59.4 %collective-permute-start.35 = (bf16[2,4,64,1152]{3,2,1,0:T(8,128)(2,1)S(1)}, bf16[2,4,64,1152]{3,2,1,0:T(8,128)(2,1)S(1)}, u32[]{:S(2)}, u32[]{:S(2)}) collective-permute-start(bf16[2,4,64,1152]{3,2,1,0:T(8,128)(2,1)S(1)} %fusion.32), channel_id=1, source_target_pairs={{0,8},{8,0},{1,9},{9,1},{2,10},{10,2},{3,11},{11,3},{4,12},{12,4},... | collective-permute-start | bytes 3538952 | tf_op jit(solution)/shard_map/ppermute | solution.py:100
  (103 other events, 1064.4 us)
Sparse Core Ops, SparseCore 0:
  171.4 91.1 all-gather.1
  429.1 147.4 reduce-scatter.4

commit v2 on v1

--- a/solution.py
+++ b/solution.py
@@ -29,20 +29,6 @@
 DECAYS = (0.1, 0.1, 0.1, 0.1, 0.0)
 
 
-def across_tokens(left, right):
-    flat_left = left.reshape(-1, left.shape[-1])
-    flat_right = right.reshape(-1, right.shape[-1])
-    return lax.dot_general(
-        flat_left, flat_right, (((0,), (0,)), ((), ())), preferred_element_type=jnp.float32
-    )
-
-
-def against_weight(values, weight):
-    return lax.dot_general(
-        values, weight, (((values.ndim - 1,), (1,)), ((), ())), preferred_element_type=jnp.float32
-    )
-
-
 def norm_back(state, inverse, gain, upstream):
     scaled = gain * upstream
     change = inverse * scaled - state * inverse**3 * jnp.mean(scaled * state, -1, keepdims=True)
@@ -70,55 +56,66 @@
 
 
 def place(pieces, index):
+    count = range(len(pieces))
+    index = index.astype(jnp.int32)
+    if len(pieces) == 2:
+        index = index > 0
+    return jnp.stack([lax.select_n(index, *[pieces[i ^ k] for k in count]) for i in count], 0)
+
+
+def place_steps(pieces, index):
     out = jnp.zeros((len(pieces),) + pieces[0].shape, pieces[0].dtype)
     for step, piece in enumerate(pieces):
         out = lax.dynamic_update_index_in_dim(out, piece, index ^ step, 0)
     return out
 
 
-def gather_axis(value, axis, count, up_only=False):
-    index = lax.axis_index(axis)
+def pieces_along(axis, value, count, up_only=False):
     pieces = [value]
     for step in range(1, count):
         routes = [(i, i ^ step) for i in range(count) if i < i ^ step or not up_only]
         pieces.append(lax.ppermute(value, axis, routes))
-    return place(pieces, index)
-
-
-def add_up(parts):
+    return pieces
+
+
+def gather_axis(value, axis, count):
+    return place(pieces_along(axis, value, count), lax.axis_index(axis))
+
+
+def total_of(parts):
     total = parts[0].astype(jnp.float32)
     for part in parts[1:]:
         total = total + part.astype(jnp.float32)
-    return total.astype(jnp.bfloat16)
-
-
-def reduce_axis(array, axis, dim, count, down_only=False):
+    return total
+
+
+def add_up(parts):
+    return total_of(parts).astype(jnp.bfloat16)
+
+
+def parts_along(axis, array, dim, count, down_only=False):
     index = lax.axis_index(axis)
-    total = pick(array, index, dim).astype(jnp.float32)
+    parts = [pick(array, index, dim)]
     for step in range(1, count):
         routes = [(i, i ^ step) for i in range(count) if i ^ step < i or not down_only]
-        part = lax.ppermute(pick(array, index ^ step, dim), axis, routes)
-        total = total + part.astype(jnp.float32)
-    return total
+        parts.append(lax.ppermute(pick(array, index ^ step, dim), axis, routes))
+    return parts
+
+
+def reduce_axis(array, axis, dim, count):
+    return total_of(parts_along(axis, array, dim, count))
 
 
 def hold(*values):
     return lax.optimization_barrier(values)
 
 
-def to_owners(grad, sizes):
-    xs, zs, ys = sizes
-    grad = grad.reshape(xs, 2, zs, *grad.shape[1:])
-    grad = reduce_axis(grad, "core", 1, 2).astype(jnp.bfloat16)
-    grad = reduce_axis(grad, "x", 0, xs).astype(jnp.bfloat16)
-    return reduce_axis(grad, "z", 0, zs).astype(jnp.bfloat16)
-
-
 def tree_sum(value, axis, count):
-    terms = [value] + [swap(axis, value, count, step) for step in range(1, count)]
-    while len(terms) > 1:
-        terms = [terms[i] + terms[i + 1] for i in range(0, len(terms), 2)]
-    return terms[0]
+    step = 1
+    while step < count:
+        value = value + swap(axis, value, count, step)
+        step *= 2
+    return value
 
 
 def across(left, right, left_dim, right_dim):
@@ -260,7 +257,6 @@
     wide = pl.BlockSpec((group * HD, block), lambda h, r, meta: (h, r))
     pairs = pl.BlockSpec((ys, zs, 1, 1, block, 2 * HD), lambda h, r, meta: (0, 0, h, r, 0, 0))
     logs = pl.BlockSpec((1, group, block), lambda h, r, meta: (h, 0, r))
-    work = rows * HEADS * block * ys * zs * block
     return pl.pallas_call(
         functools.partial(attend_kernel, group, block),
         grid_spec=pltpu.PrefetchScalarGridSpec(
@@ -279,9 +275,7 @@
             jax.ShapeDtypeStruct((KVH, group, rows * block), jnp.float32),
         ],
         compiler_params=pltpu.CompilerParams(vmem_limit_bytes=32 * 2**20),
-        cost_estimate=pl.CostEstimate(
-            flops=4 * work * HD, bytes_accessed=4 * all_kv.size, transcendentals=work
-        ),
+        cost_estimate=pl.CostEstimate(flops=1, bytes_accessed=1, transcendentals=0),
         name="attend",
     )(meta, query, all_kv)
 
@@ -294,7 +288,6 @@
     pairs = pl.BlockSpec((ys, zs, 1, 1, block, 2 * HD), lambda r, meta: (0, 0, h, r, 0, 0))
     terms = pl.BlockSpec((ys, zs, 1, block, 2 * HD), lambda r, meta: (0, 0, r, 0, 0))
     log_spec = pl.BlockSpec((1, group, block), lambda r, meta: (h, 0, r))
-    work = rows * group * block * ys * zs * block
     return pl.pallas_call(
         functools.partial(attend_back_kernel, group, block),
         grid_spec=pltpu.PrefetchScalarGridSpec(
@@ -312,11 +305,179 @@
             jax.ShapeDtypeStruct((ys, zs, rows, block, 2 * HD), jnp.bfloat16),
         ],
         compiler_params=pltpu.CompilerParams(vmem_limit_bytes=32 * 2**20),
-        cost_estimate=pl.CostEstimate(
-            flops=10 * work * HD, bytes_accessed=4 * all_kv.size, transcendentals=work
-        ),
+        cost_estimate=pl.CostEstimate(flops=1, bytes_accessed=1, transcendentals=0),
         name="attend_back",
     )(meta, query, upper, attended, logs, all_kv)
+
+
+def dot(left, right, left_dim=1, right_dim=0):
+    return lax.dot_general(
+        left, right, (((left_dim,), (right_dim,)), ((), ())), preferred_element_type=jnp.float32
+    )
+
+
+def hidden_kernel(xs, chunk, spot, n_own, n_other, u_own, u_other, first_a, first_b, *refs):
+    seconds, (down_ref, inner_ref, d_ref, gate_ref, up_ref, across_ref) = refs[:xs], refs[xs:]
+    y, x = spot[0], spot[1]
+    count = n_own.shape[0]
+
+    swapped = y != 0
+    lower = [jnp.where(swapped, first_b[...], first_a[...]), jnp.where(swapped, first_a[...], first_b[...])]
+    size = first_a.shape[1]
+    for index, out in enumerate((gate_ref, up_ref)):
+        for i in range(xs):
+            out[2 * i * size : (2 * i + 1) * size] = lower[index][i]
+            upper = seconds[i][index]
+            for other in range(xs):
+                if other != i:
+                    upper = jnp.where((x ^ i) == other, seconds[other][index], upper)
+            out[(2 * i + 1) * size : (2 * i + 2) * size] = upper
+
+    @pl.when(pl.program_id(0) == 0)
+    def _():
+        for ref, columns in ((n_own, slice(0, count)), (n_other, slice(count, 2 * count))):
+            turned = ref[...].T
+            for i in range(xs):
+                across_ref[i, :, columns] = turned[2 * i * size : (2 * i + 1) * size]
+                across_ref[xs + (x ^ i), :, columns] = turned[(2 * i + 1) * size : (2 * i + 2) * size]
+
+    gate_w, up_w, down_w = gate_ref[...], up_ref[...], down_ref[...]
+    spans = [slice(i, i + chunk) for i in range(0, count, chunk)]
+    gates = [dot(ref[span], gate_w) for ref in (n_own, n_other) for span in spans]
+    ups = [dot(ref[span], up_w) for ref in (n_own, n_other) for span in spans]
+    inners = [dot(ref[span], down_w, 1, 1) for ref in (u_own, u_other) for span in spans]
+    parts = [slice(i, i + chunk) for i in range(0, 2 * count, chunk)]
+    for part, gate, up, d_inner in zip(parts, gates, ups, inners):
+        sigma = 1.0 / (1.0 + jnp.exp(-gate))
+        activated = gate * sigma
+        inner_ref[part] = (activated * up).astype(jnp.bfloat16)
+        d_ref[1, part] = (d_inner * activated).astype(jnp.bfloat16)
+        d_ref[0, part] = (d_inner * up * (sigma + activated * (1.0 - sigma))).astype(jnp.bfloat16)
+
+
+def hidden_part(spot, normed, upper, first, second, down, width=256):
+    count, size = normed[0].shape
+    half = down.shape[0]
+    xs, slab, _ = first[0].shape
+    whole = pl.BlockSpec((count, size), lambda i, spot: (0, 0))
+    lower = pl.BlockSpec((xs, slab, width), lambda i, spot: (0, 0, i))
+    both = pl.BlockSpec((2, slab, width), lambda i, spot: (0, 0, i))
+    columns = pl.BlockSpec((size, width), lambda i, spot: (0, i))
+    rows = pl.BlockSpec((width, size), lambda i, spot: (i, 0))
+    shapes = [(2 * count, half), (2, 2 * count, half), (size, half), (size, half)]
+    shapes += [(2 * xs, slab, 2 * count)]
+    return pl.pallas_call(
+        functools.partial(hidden_kernel, xs, 256),
+        grid_spec=pltpu.PrefetchScalarGridSpec(
+            num_scalar_prefetch=1,
+            grid=(pl.cdiv(half, width),),
+            in_specs=[whole] * 4 + [lower] * 2 + [both] * xs + [rows],
+            out_specs=[
+                pl.BlockSpec((2 * count, width), lambda i, spot: (0, i)),
+                pl.BlockSpec((2, 2 * count, width), lambda i, spot: (0, 0, i)),
+                columns,
+                columns,
+                pl.BlockSpec((2 * xs, slab, 2 * count), lambda i, spot: (0, 0, 0)),
+            ],
+        ),
+        out_shape=[jax.ShapeDtypeStruct(shape, jnp.bfloat16) for shape in shapes],
+        compiler_params=pltpu.CompilerParams(vmem_limit_bytes=56 * 2**20),
+        cost_estimate=pl.CostEstimate(flops=1, bytes_accessed=1, transcendentals=0),
+        name="hidden",
+    )(spot, *normed, *upper, *first, *second, down)
+
+
+def grads_kernel(xs, spot, n_ref, d_own, d_other, *outs):
+    y = spot[0]
+    rows = n_ref.shape[1]
+    features = n_ref[...].reshape(-1, n_ref.shape[2])
+    for out, index, ref in zip(outs[:2], (y, 1 - y), (d_own, d_other)):
+        result = dot(features, ref[...]).astype(jnp.bfloat16)
+        out[...] = result[: xs * rows].reshape(out.shape)
+        for step, upper in enumerate(outs[2:]):
+            upper[index] = result[(xs + step) * rows : (xs + step + 1) * rows]
+
+
+def gate_up_grads(spot, features, d_both, xs, start, stop, width):
+    _, rows, count = features.shape
+    first = start // width
+    lower = pl.BlockSpec((xs, rows, width), lambda i, spot: (0, 0, i))
+    upper = pl.BlockSpec((2, rows, width), lambda i, spot: (0, 0, i))
+    return pl.pallas_call(
+        functools.partial(grads_kernel, xs),
+        grid_spec=pltpu.PrefetchScalarGridSpec(
+            num_scalar_prefetch=1,
+            grid=(pl.cdiv(stop - start, width),),
+            in_specs=[
+                pl.BlockSpec((2 * xs, rows, count), lambda i, spot: (0, 0, 0)),
+                pl.BlockSpec((None, count, width), lambda i, spot: (spot[0], 0, first + i)),
+                pl.BlockSpec((None, count, width), lambda i, spot: (1 - spot[0], 0, first + i)),
+            ],
+            out_specs=[lower] * 2 + [upper] * xs,
+        ),
+        out_shape=[jax.ShapeDtypeStruct((xs, rows, stop - start), jnp.bfloat16)] * 2
+        + [jax.ShapeDtypeStruct((2, rows, stop - start), jnp.bfloat16)] * xs,
+        compiler_params=pltpu.CompilerParams(vmem_limit_bytes=56 * 2**20),
+        cost_estimate=pl.CostEstimate(flops=1, bytes_accessed=1, transcendentals=0),
+        name="gate_up_grads",
+    )(spot, features, d_both, d_both)
+
+
+def down_kernel(inner_ref, u_own, u_other, out_ref):
+    count = u_own.shape[0]
+    result = dot(inner_ref[:count], u_own[...], 0, 0) + dot(inner_ref[count:], u_other[...], 0, 0)
+    out_ref[...] = result.astype(jnp.bfloat16)
+
+
+def down_grad(inner, upper, width=256):
+    count, half = inner.shape
+    size = upper[0].shape[1]
+    return pl.pallas_call(
+        down_kernel,
+        grid=(pl.cdiv(half, width),),
+        in_specs=[
+            pl.BlockSpec((count, width), lambda i: (0, i)),
+            pl.BlockSpec((count // 2, size), lambda i: (0, 0)),
+            pl.BlockSpec((count // 2, size), lambda i: (0, 0)),
+        ],
+        out_specs=pl.BlockSpec((width, size), lambda i: (i, 0)),
+        out_shape=jax.ShapeDtypeStruct((half, size), jnp.bfloat16),
+        compiler_params=pltpu.CompilerParams(vmem_limit_bytes=56 * 2**20),
+        cost_estimate=pl.CostEstimate(flops=1, bytes_accessed=1, transcendentals=0),
+        name="down_grad",
+    )(inner, *upper)
+
+
+def back_kernel(steps, d_ref, gate_ref, up_ref, own_ref, other_ref):
+    result = dot(d_ref[0], gate_ref[...], 1, 1) + dot(d_ref[1], up_ref[...], 1, 1)
+
+    @pl.when(pl.program_id(0) < steps)
+    def _():
+        own_ref[...] = result
+
+    @pl.when(pl.program_id(0) >= steps)
+    def _():
+        other_ref[...] = result
+
+
+def hidden_back(d_both, gate, up, height=256):
+    _, count, half = d_both.shape
+    size = gate.shape[0]
+    steps = count // height // 2
+    whole = pl.BlockSpec((size, half), lambda i: (0, 0))
+    return pl.pallas_call(
+        functools.partial(back_kernel, steps),
+        grid=(2 * steps,),
+        in_specs=[pl.BlockSpec((2, height, half), lambda i: (0, i, 0)), whole, whole],
+        out_specs=[
+            pl.BlockSpec((height, size), lambda i: (jnp.minimum(i, steps - 1), 0)),
+            pl.BlockSpec((height, size), lambda i: (jnp.maximum(i, steps) - steps, 0)),
+        ],
+        out_shape=[jax.ShapeDtypeStruct((count // 2, size), jnp.float32)] * 2,
+        compiler_params=pltpu.CompilerParams(vmem_limit_bytes=56 * 2**20),
+        cost_estimate=pl.CostEstimate(flops=1, bytes_accessed=1, transcendentals=0),
+        name="hidden_back",
+    )(d_both, gate, up)
 
 
 def layer(
@@ -368,9 +529,9 @@
     pair_out = jnp.concatenate([lower[:share, qkv_width:], upper[:share, qkv_width:]], 0)
     lower, upper = lower[:, :qkv_width], upper[:, :qkv_width]
     spare = jnp.zeros((-2 * (share + 1) % 8, qkv_width), low)
-    full_qkv = gather_axis(
+    full_qkv = pieces_along(
+        "z",
         jnp.concatenate([lower[:share], upper[:share], lower[share:], upper[share:], spare], 0),
-        "z",
         zs,
     )
 
@@ -386,12 +547,16 @@
         + [swap(("core", "y"), pick(own_gu, quad ^ step), 4, step) for step in range(1, 4)],
         quad,
     ).reshape(2, 2 * share, half)
-    quads = jnp.concatenate([quads[0], pair_out, quads[1]], 1)
-    quads = [quads] + [swap("z", quads, zs, step) for step in range(1, zs)]
-    full_qkv = gather_axis(gather_axis(full_qkv, "x", xs), "core", 2).swapaxes(0, 1)
+    first = jnp.concatenate([quads[0], pair_out], 1)
+    full_qkv, first, second = hold(full_qkv, first, quads[1])
+    first = pieces_along("z", first, zs)
+    full_qkv = pieces_along("x", place_steps(full_qkv, z_index), xs)
+    full_qkv, first, second = hold(full_qkv, first, second)
+    second = pieces_along("z", second, zs)
+    first = pieces_along("x", place(first, z_index), xs)
+    full_qkv = gather_axis(place(full_qkv, x_index), "core", 2).swapaxes(0, 1)
     full_small = full_qkv[..., 2 * share : 2 * share + ys, :small_share].reshape(-1)
     full_qkv = full_qkv[..., : 2 * share, :].reshape(D, qkv_width)
-    full_down = lax.all_gather(down_weight.astype(low), chips, axis=0, tiled=True)
 
     small_used = full_small.astype(jnp.float32)
     gain_attn = small_used[:D]
@@ -410,105 +575,123 @@
     ).transpose(0, 2, 1)
     own_kv = own_kv.reshape(KVH, rows, block_len, 2 * HD)
 
-    own_kv, quads = hold(own_kv, quads)
-    all_kv = gather_axis(own_kv, "z", zs, True)
-    first = place([part[:, : half + D] for part in quads], z_index)
-    second = place([part[:, half + D :] for part in quads], z_index)
-    first = [first] + [swap("x", first, xs, step) for step in range(1, xs)]
-    second = [second, swap("y", second, ys, 1)]
-    all_kv, first, second = hold(all_kv, first, second)
-    all_kv = gather_axis(all_kv, "y", ys)
+    valid = (positions[None, :] < lengths[:, None]).astype(jnp.float32)
+    upstream = cotangent.reshape(tokens, D).astype(jnp.float32) * valid.reshape(tokens, 1)
+
+    own_kv, second, down_weight, upstream = hold(own_kv, second, down_weight, upstream)
+    full_down = lax.all_gather(down_weight.astype(low), chips, axis=0, tiled=True)
+    all_kv = pieces_along("z", own_kv, zs, True)
+    second = pieces_along("y", place(second, z_index), ys)
+    all_kv, first, second, upstream = hold(all_kv, first, second, upstream)
+    all_kv = pieces_along("y", place(all_kv, z_index), ys)
+    second = pieces_along("x", place(second, y_index), xs)
     first = place(first, x_index)
     first, full_out = first[..., :half], first[..., half:]
+    all_kv, first, full_out, upstream = hold(all_kv, first, full_out, upstream)
+    all_kv = place(all_kv, y_index)
     full_out = gather_axis(full_out, "core", 2).swapaxes(0, 1).reshape(QD, D)
-    second = place(second, y_index)
-    second = [second] + [swap("x", second, xs, step) for step in range(1, xs)]
-    all_kv, first = hold(all_kv, first)
-    first = [first, swap("y", first, ys, 1)]
+    first = pieces_along("y", first, ys)
     meta = jnp.concatenate([ctx_index.astype(jnp.int32).reshape(1), lengths])
     attended, logs = attention(meta, query, all_kv, block_len)
     attended, first, second = hold(attended, first, second)
-    second = place(second, x_index)
-    is_gate = y_index == 0
-    first = [jnp.where(is_gate, first[0], first[1]), jnp.where(is_gate, first[1], first[0])]
-    full_gate = jnp.stack([first[0], second[:, 0]], 1).reshape(D, half)
-    full_up = jnp.stack([first[1], second[:, 1]], 1).reshape(D, half)
+    spot = jnp.stack([y_index, x_index]).astype(jnp.int32)
+    slab = D // (2 * xs)
+    first = [part.reshape(xs, slab, half) for part in first]
+    second = [part.reshape(2, slab, half) for part in second]
     mixed_low = attended.astype(low)
     hidden_state = state + across(mixed_low, full_out, 0, 0)
     inverse_mlp = lax.rsqrt(jnp.mean(hidden_state * hidden_state, -1, keepdims=True) + EPS)
     normed2 = (hidden_state * inverse_mlp * gain_mlp).astype(low)
-    valid = (positions[None, :] < lengths[:, None]).astype(jnp.float32)
-    upstream = cotangent.reshape(tokens, D).astype(jnp.float32) * valid.reshape(tokens, 1)
 
     def pair(value):
-        return jnp.concatenate([value, swap("core", value, 2, 1)], 0)
+        return value, swap("core", value, 2, 1)
 
     def pair_sum(value):
         return value[:tokens] + swap("core", value[tokens:], 2, 1)
 
     pair_up = pair(upstream.astype(low))
     pair_normed = pair(normed2)
-    gate = jnp.dot(pair_normed, full_gate, preferred_element_type=jnp.float32)
-    up_part = jnp.dot(pair_normed, full_up, preferred_element_type=jnp.float32)
-    sigma = jax.nn.sigmoid(gate)
-    activated = gate * sigma
-    inner = (activated * up_part).astype(low)
-    d_inner = against_weight(pair_up, full_down)
-    d_gate = (d_inner * up_part * sigma * (1.0 + gate * (1.0 - sigma))).astype(low)
-    d_up = (d_inner * activated).astype(low)
-    grad_down = across_tokens(inner, pair_up).astype(low)
-    grad_down, d_gate, d_up = hold(grad_down, d_gate, d_up)
-    red_down = lax.psum_scatter(grad_down, chips, scatter_dimension=0, tiled=True)
-    red_down = red_down.astype(jnp.float32)
-    grad_gate = across_tokens(pair_normed, d_gate).astype(low)
-    grad_up = across_tokens(pair_normed, d_up).astype(low)
-    grad_gate, grad_up, d_gate, d_up = hold(grad_gate, grad_up, d_gate, d_up)
-    grad_gate = grad_gate.reshape(xs, 2, zs, 2 * share, half)
-    grad_up = grad_up.reshape(xs, 2, zs, 2 * share, half)
-
-    first = [grad_gate[:, 0], grad_up[:, 0]]
-    first = [jnp.where(is_gate, first[0], first[1]), jnp.where(is_gate, first[1], first[0])]
-    first[1] = swap("y", first[1], ys, 1)
-    second = jnp.stack([grad_gate[:, 1], grad_up[:, 1]], 1)
-    second = [pick(second, x_index)] + [
-        swap("x", pick(second, x_index ^ step), xs, step) for step in range(1, xs)
-    ]
-    d_normed2 = pair_sum(against_weight(d_gate, full_gate) + against_weight(d_up, full_up))
-    output = hidden_state + pair_sum(jnp.dot(inner, full_down, preferred_element_type=jnp.float32))
+    inner, d_both, full_gate, full_up, features = hidden_part(
+        spot, pair_normed, pair_up, first, second, full_down
+    )
+
+    middle = half // 256 // 2 * 256 + 128
+
+    def exchange(parts):
+        first, second = list(parts[:2]), list(parts[2:])
+        first[1] = swap("y", first[1], ys, 1)
+        return first, second[:1] + [swap("x", second[i], xs, i) for i in range(1, xs)]
+
+    cut = ff_share // 16 * 8
+    grad_down = down_grad(inner, pair_up, 512)
+    grad_down, d_both = hold(grad_down, d_both)
+    grad_down = grad_down.reshape(xs, zs, ys, ff_share, D)
+    down_y = parts_along("y", grad_down[:, :, :, :cut], 2, ys)
+    down_x = parts_along("x", grad_down[:, :, :, cut:], 0, xs)
+    left = gate_up_grads(spot, features, d_both, xs, 0, middle, 384)
+    right = gate_up_grads(spot, features, d_both, xs, middle, half, 384)
+    down_y, down_x, left, right, d_both, inner = hold(down_y, down_x, left, right, d_both, inner)
+    left = exchange(left)
+    down_y = parts_along("x", add_up(down_y), 0, xs)
+    down_x = parts_along("y", add_up(down_x), 1, ys)
+    d_normed2 = hidden_back(d_both, full_gate, full_up)
+    output = jnp.dot(inner, full_down, preferred_element_type=jnp.float32)
+    left, down_y, down_x, right, d_normed2, output = hold(
+        left, down_y, down_x, right, d_normed2, output
+    )
+    right = exchange(right)
+    first = parts_along("x", add_up(left[0]), 0, xs)
+    second = parts_along("y", add_up(left[1]), 0, ys)
+    d_normed2 = d_normed2[0] + swap("core", d_normed2[1], 2, 1)
 
     change_mlp, grad_gain_mlp = norm_back(hidden_state, inverse_mlp, gain_mlp, d_normed2)
     d_hidden = upstream + change_mlp
     d_hidden_low = d_hidden.astype(low)
     grad_out = across(mixed_low, d_hidden_low, 1, 0)
     d_mixed = across(full_out, d_hidden_low, 1, 1).astype(low)
-    grad_out = grad_out.astype(low).reshape(xs, 2, zs, 2 * share, D)
-    grad_out = reduce_axis(grad_out, "core", 1, 2).astype(low)
-
+    grad_out = parts_along(
+        "core", grad_out.astype(low).reshape(xs, 2, zs, 2 * share, D), 1, 2
+    )
     d_query, kv_terms = [None] * KVH, [None] * KVH
     d_query[0], kv_terms[0] = attention_back(
         0, meta, query, d_mixed, attended, logs, all_kv, block_len
     )
-    first, second, d_query[0] = hold(first, second, d_query[0])
-    first, second = add_up(first), add_up(second)
-    first = jnp.concatenate([first, grad_out], -1)
-    kv_terms[0] = reduce_axis(kv_terms[0], "y", 0, ys).astype(low)
-    first, second, query = hold(first, second, query)
-    first = [pick(first, x_index)] + [
-        swap("x", pick(first, x_index ^ step), xs, step) for step in range(1, xs)
-    ]
-    second = [pick(second, y_index), swap("y", pick(second, 1 - y_index), ys, 1)]
+    right, first, second, grad_out, d_query[0], kv_terms[0], query = hold(
+        right, first, second, grad_out, d_query[0], kv_terms[0], query
+    )
+    left = jnp.concatenate([add_up(first), add_up(second)], -1)
+    left = parts_along("z", left.reshape(zs, 2 * share, -1), 0, zs)
+    first = add_up(right[0]).reshape(xs, zs, 2 * share, -1)
+    first = parts_along("x", jnp.concatenate([first, add_up(grad_out)], -1), 0, xs)
+    second = parts_along("y", add_up(right[1]), 0, ys)
     d_query[1], kv_terms[1] = attention_back(
         1, meta, query, d_mixed, attended, logs, all_kv, block_len
     )
-    first, second, d_query[1] = hold(first, second, d_query[1])
-    first, second = add_up(first), add_up(second)
-    kv_terms[1] = reduce_axis(kv_terms[1], "y", 0, ys).astype(low)
-    kv_grads = reduce_axis(jnp.stack(kv_terms, 1), "z", 0, zs, True)
+    left, first, second, kv_terms, d_query[1] = hold(left, first, second, kv_terms, d_query[1])
+    kv_terms = parts_along("y", jnp.stack(kv_terms, 2), 0, ys)
+    right = jnp.concatenate([add_up(first), add_up(second).reshape(zs, 2 * share, -1)], -1)
+    right = parts_along("z", right, 0, zs)
+    output = hidden_state + pair_sum(output)
+    kv_terms, right, output, left, down_y, down_x = hold(
+        kv_terms, right, output, left, down_y, down_x
+    )
+    kv_terms = parts_along("z", add_up(kv_terms), 0, zs, True)
+    left, right = add_up(left), add_up(right)
+    red_out = right[:, half - middle : half - middle + D]
+    red_quads = jnp.stack(
+        [
+            jnp.concatenate([left[:, :middle], right[:, : half - middle]], 1),
+            jnp.concatenate([left[:, middle:], right[:, half - middle + D :]], 1),
+        ],
+        0,
+    )
+    red_quads = parts_along("y", red_quads.reshape(2, ys, share, half), 1, ys)
+    red_down = jnp.concatenate([add_up(down_y), add_up(down_x)], 1)
+    kv_terms, red_quads, red_down = hold(kv_terms, red_quads, red_down)
+    kv_grads = total_of(kv_terms)
+    red_down = parts_along("z", red_down, 0, zs)
+    red_gu = parts_along("core", place(red_quads, y_index), 1, 2)
     d_query = jnp.concatenate(d_query, 0)
-    red_quads = reduce_axis(jnp.concatenate([first, second], -1), "z", 0, zs).astype(low)
-    red_out = red_quads[:, half : half + D]
-    red_quads = jnp.stack([red_quads[:, :half], red_quads[:, half + D :]], 0)
-    red_quads = red_quads.reshape(4, share, half)
     kv_grads = kv_grads.reshape(KVH, tokens, 2 * HD).transpose(0, 2, 1)
     d_qkv = jnp.concatenate(
         [
@@ -530,7 +713,12 @@
     grad_qkv = jnp.concatenate(
         [grad_qkv.astype(low).reshape(-1, ys * share, qkv_width), grad_small], 1
     )
-    red_qkv = to_owners(grad_qkv, sizes)
+    red_qkv = grad_qkv.reshape(xs, 2, zs, -1, qkv_width)
+    red_qkv = add_up(parts_along("core", red_qkv, 1, 2))
+    red_qkv = parts_along("x", red_qkv, 0, xs)
+    red_qkv, red_down, red_gu = hold(red_qkv, red_down, red_gu)
+    red_qkv = add_up(parts_along("z", add_up(red_qkv), 0, zs))
+    red_down = total_of(red_down)
 
     red_small = red_qkv[ys * share : ys * share + ys]
     red_qkv = red_qkv[: ys * share].reshape(ys, share, qkv_width)
@@ -542,11 +730,7 @@
     mine = mine + swap("y", pick(along, 1 - y_index), ys, 1).astype(jnp.float32)
     red_qkv, red_out = mine[:share, :qkv_width], mine[:share, qkv_width:]
     red_small = mine[share, :small_share]
-    red_gu = place(
-        [pick(red_quads, quad)]
-        + [swap(("core", "y"), pick(red_quads, quad ^ step), 4, step) for step in range(1, 4)],
-        quad,
-    )
+    red_gu = place(red_gu, core)
     red_gu = (
         red_gu.reshape(2, 2, share, xs, ff_slab).transpose(2, 1, 3, 0, 4).reshape(share, 2 * FF)
     ).astype(jnp.float32)
@@ -558,9 +742,10 @@
         + jnp.sum(red_down * red_down)
         + jnp.sum(red_small * red_small)
     ).reshape(1)
-    square_sum = tree_sum(local_square, "core", 2)
-    square_sum = tree_sum(square_sum, ("x", "y"), xs * ys)
-    square_sum = tree_sum(square_sum, "z", zs)[0]
+    square_sum = local_square
+    for axis, count in (("core", 2), ("y", ys), ("x", xs), ("z", zs)):
+        square_sum = tree_sum(square_sum, axis, count)
+    square_sum = square_sum[0]
     grad_norm = jnp.sqrt(square_sum)
     factor = CLIP / jnp.maximum(grad_norm, CLIP)
     qkv_new = adam_step(red_qkv, qkv_moment, qkv_square, qkv_weight, factor, RATES[0], DECAYS[0])

time: 651 us -> 594 us (0.912)
  matrix products: 103 us -> 22.4 us
  Pallas kernels: 14.6 us -> 91.2 us
  local copies, waits for them, and re-layouts: 79.6 us -> 41 us
  waiting for transfers between devices: 258 us -> 235 us
  other arithmetic: 47 us -> 68.4 us
  starting transfers between devices: 117 us -> 105 us
    ppermute x30 -> x18, waiting for transfers between devices: 109 us -> 15.7 us  [swap(): return lax.ppermute(value, axis, [(i, i ^ step) for i in range(count)])]
    ppermute x24 -> x49, waiting for transfers between devices: 138 us -> 220 us  [the longest x20 122 us: pieces_along(): pieces.append(lax.ppermute(value, axis, routes))]
    dot_general x9 -> x1, matrix products: 90.9 us -> 9.53 us  [layer(): output = jnp.dot(inner, full_down, preferred_element_type=jnp.float32)]
    pallas_call x0 -> x5, Pallas kernels: none -> 76.9 us  [the longest x1 26.8 us: hidden_part(): pl.pallas_call(functools.partial(hidden_kernel, xs, 256), grid_spec=pltpu...]
    dynamic_update_slice x38 -> x4, local copies, waits for them, and re-layouts: 36.8 us -> 3.6 us  [place_steps(): out = lax.dynamic_update_index_in_dim(out, piece, index ^ step, 0)]
    ppermute x30 -> x18, starting transfers between devices: 42.8 us -> 16.8 us  [swap(): return lax.ppermute(value, axis, [(i, i ^ step) for i in range(count)])]
    ppermute x24 -> x49, starting transfers between devices: 74.2 us -> 87.9 us  [the longest x29 51.4 us: parts_along(): parts.append(lax.ppermute(pick(array, index ^ step, dim), axis, routes))]
    another operation x11 -> x29, other arithmetic: 6.21 us -> 18.4 us  [the longest x23 15.5 us: place(): jnp.stack([lax.select_n(index, *[pieces[i ^ k] for k in count]) for i in...]
  transfers between devices with their start and end apart: 56 -> 68, of which waited for: 24 -> 30; matrix products, arithmetic and copies ran while one was open for 20% -> 14% of each run, Pallas kernels for 2% -> 9%
where the time goes in v2:
time: 594 us; the launch traced here: 587 us
  waiting for transfers between devices  235 us (40%)
  starting transfers between devices  105 us (18%)
  Pallas kernels  91.2 us (15%)
  other arithmetic  68.4 us (12%)
  local copies, waits for them, and re-layouts  41 us (7%)
  between operations  23.5 us (4%)
  matrix products  22.4 us (4%)
    ppermute x20, waiting for transfers between devices, pieces_along(): pieces.append(lax.ppermute(value, axis, routes))  122 us
    ppermute x29, waiting for transfers between devices, parts_along(): parts.append(lax.ppermute(pick(array, index ^ step, dim), axis, routes))  97.1 us
    ppermute x29, starting transfers between devices, parts_along(): parts.append(lax.ppermute(pick(array, index ^ step, dim), axis, routes))  51.4 us
    ppermute x20, starting transfers between devices, pieces_along(): pieces.append(lax.ppermute(value, axis, routes))  36.5 us
    pallas_call x1, Pallas kernels, hidden_part(): pl.pallas_call(functools.partial(hidden_kernel, xs, 256), grid_spec=pltpu...  26.8 us
    pallas_call x2, Pallas kernels, gate_up_grads(): pl.pallas_call(functools.partial(grads_kernel, xs), grid_spec=pltpu.Prefe...  23 us
    pallas_call x1, Pallas kernels, hidden_back(): pl.pallas_call(functools.partial(back_kernel, steps), grid=(2 * steps,),...  17.4 us
    ppermute x18, starting transfers between devices, swap(): return lax.ppermute(value, axis, [(i, i ^ step) for i in range(count)])  16.8 us
  transfers between devices with their start and end apart: 68, of which 30 were waited for; matrix products, arithmetic and copies ran while one was open for 14% of the time, Pallas kernels for 9%

profile of v2, /device:TPU:0, one launch (start us, length us, event | category | flops | bytes accessed | tf_op | source)
XLA Modules:
  0.0 586.5 jit_solution(11898880806501055301)
XLA Ops:
  30.0 7.1 %collective-permute-done.2 = bf16[64,1152]{1,0:T(8,128)(2,1)S(1)} collective-permute-done((bf16[64,1152]{1,0:T(8,128)(2,1)S(1)}, bf16[64,1152]{1,0:T(8,128)(2,1)S(1)}, u32[]{:S(2)}, u32[]{:S(2)}) %collective-permute-start.2) | collective-permute-done | bytes 147488 | tf_op jit(solution)/shard_map/ppermute | solution.py:77
  49.8 10.4 %collective-permute-done.8 = bf16[56,3328]{1,0:T(8,128)(2,1)} collective-permute-done((bf16[56,3328]{1,0:T(8,128)(2,1)}, bf16[56,3328]{1,0:T(8,128)(2,1)}, u32[]{:S(2)}, u32[]{:S(2)}) %collective-permute-start.8) | collective-permute-done | bytes 372768 | tf_op jit(solution)/shard_map/ppermute | solution.py:77
  60.2 14.4 %collective-permute-done.9 = bf16[56,3328]{1,0:T(8,128)(2,1)} collective-permute-done((bf16[56,3328]{1,0:T(8,128)(2,1)}, bf16[56,3328]{1,0:T(8,128)(2,1)}, u32[]{:S(2)}, u32[]{:S(2)}) %collective-permute-start.9) | collective-permute-done | bytes 372768 | tf_op jit(solution)/shard_map/ppermute | solution.py:77
  95.7 6.0 %collective-permute-done.13 = bf16[56,2432]{1,0:T(8,128)(2,1)} collective-permute-done((bf16[56,2432]{1,0:T(8,128)(2,1)S(1)}, bf16[56,2432]{1,0:T(8,128)(2,1)}, u32[]{:S(2)}, u32[]{:S(2)}) %collective-permute-start.13) | collective-permute-done | bytes 272416 | tf_op jit(solution)/shard_map/ppermute | solution.py:77
  118.7 9.2 %collective-permute-done.16 = bf16[2,2,256,128]{3,2,1,0:T(8,128)(2,1)S(1)} collective-permute-done((bf16[2,2,256,128]{3,2,1,0:T(8,128)(2,1)S(1)}, bf16[2,2,256,128]{3,2,1,0:T(8,128)(2,1)S(1)}, u32[]{:S(2)}, u32[]{:S(2)}) %collective-permute-start.16) | collective-permute-done | bytes 262176 | tf_op jit(solution)/shard_map/ppermute | solution.py:77
  139.6 20.5 %collective-permute-done.20 = bf16[4,2,2,256,128]{4,3,2,1,0:T(8,128)(2,1)S(1)} collective-permute-done((bf16[4,2,2,256,128]{4,3,2,1,0:T(8,128)(2,1)S(1)}, bf16[4,2,2,256,128]{4,3,2,1,0:T(8,128)(2,1)S(1)}, u32[]{:S(2)}, u32[]{:S(2)}) %collective-permute-start.20) | collective-permute-done | bytes 1048608 | tf_op jit(solution)/shard_map/ppermute | solution.py:77
  171.2 33.0 %collective-permute-done.22 = bf16[2,4,56,2432]{3,2,1,0:T(8,128)(2,1)S(1)} collective-permute-done((bf16[2,4,56,2432]{3,2,1,0:T(8,128)(2,1)S(1)}, bf16[2,4,56,2432]{3,2,1,0:T(8,128)(2,1)S(1)}, u32[]{:S(2)}, u32[]{:S(2)}) %collective-permute-start.22) | collective-permute-done | bytes 2179104 | tf_op jit(solution)/shard_map/ppermute | solution.py:77
  204.2 15.1 %collective-permute-done.21 = bf16[2,4,56,2432]{3,2,1,0:T(8,128)(2,1)S(1)} collective-permute-done((bf16[2,4,56,2432]{3,2,1,0:T(8,128)(2,1)S(1)}, bf16[2,4,56,2432]{3,2,1,0:T(8,128)(2,1)S(1)}, u32[]{:S(2)}, u32[]{:S(2)}) %collective-permute-start.21) | collective-permute-done | bytes 2179104 | tf_op jit(solution)/shard_map/ppermute | solution.py:77
  225.9 26.8 %hidden.1 = (bf16[1024,2432]{1,0:T(8,128)(2,1)}, bf16[2,1024,2432]{2,1,0:T(8,128)(2,1)}, bf16[896,2432]{1,0:T(8,128)(2,1)}, bf16[896,2432]{1,0:T(8,128)(2,1)}, bf16[4,224,1024]{2,1,0:T(8,128)(2,1)}) custom-call(s32[2]{0:T(128)} %pad_add_fusion.spot, bf16[512,896]{1,0:T(8,128)(2,1)} %multiply_convert_fusion.n_own, ...), custom_call_target="tpu_custom_call" | custom-call | flops 1 | bytes 1 | tf_op jit(solution)/shard_map/hidden/pallas_call | solution.py:369
  252.6 9.6 %down_grad.1 = bf16[2432,896]{1,0:T(8,128)(2,1)} custom-call(bf16[1024,2432]{1,0:T(8,128)(2,1)} %get-tuple-element.262.inner_ref, bf16[512,896]{1,0:T(8,128)(2,1)} %convert_element_type.369.u_own, bf16[512,896]{1,0:T(8,128)(2,1)} %collective-permute-done.25.u_other), custom_call_target="tpu_custom_call" | custom-call | flops 1 | bytes 1 | tf_op jit(solution)/shard_map/down_grad/pallas_call | solution.py:435
  270.6 10.6 %gate_up_grads.2 = (bf16[2,224,1152]{2,1,0:T(8,128)(2,1)}, bf16[2,224,1152]{2,1,0:T(8,128)(2,1)}, bf16[2,224,1152]{2,1,0:T(8,128)(2,1)}, bf16[2,224,1152]{2,1,0:T(8,128)(2,1)}) custom-call(s32[2]{0:T(128)} %pad_add_fusion.spot, bf16[4,224,1024]{2,1,0:T(8,128)(2,1)} %get-tuple-element.235.n_ref, ...), custom_call_target="tpu_custom_call" | custom-call | flops 1 | bytes 1 | tf_op jit(solution)/shard_map/gate_up_grads/pallas_call | solution.py:406
  281.2 12.5 %gate_up_grads.3 = (bf16[2,224,1280]{2,1,0:T(8,128)(2,1)}, bf16[2,224,1280]{2,1,0:T(8,128)(2,1)}, bf16[2,224,1280]{2,1,0:T(8,128)(2,1)}, bf16[2,224,1280]{2,1,0:T(8,128)(2,1)}) custom-call(s32[2]{0:T(128)} %pad_add_fusion.spot, bf16[4,224,1024]{2,1,0:T(8,128)(2,1)} %get-tuple-element.235.n_ref, ...), custom_call_target="tpu_custom_call" | custom-call | flops 1 | bytes 1 | tf_op jit(solution)/shard_map/gate_up_grads/pallas_call | solution.py:406
  304.6 9.5 %fusion.77 = f32[1024,896]{1,0:T(8,128)} fusion(bf16[1024,2432]{1,0:T(8,128)(2,1)S(1)} %bitcast.335, bf16[2432,896]{1,0:T(8,128)(2,1)} %all-gather.2.cloned.1.call-done.refs_2_), kind=kOutput, calls=%fused_computation.305 | convolution fusion | flops 4462739456 | bytes 13008896 | tf_op jit(solution)/shard_map/dot_general | solution.py:638
  314.2 17.4 %hidden_back.1 = (f32[512,896]{1,0:T(8,128)}, f32[512,896]{1,0:T(8,128)}) custom-call(bf16[2,1024,2432]{2,1,0:T(8,128)(2,1)} %get-tuple-element.257.d_own.d_other.d_ref, bf16[896,2432]{1,0:T(8,128)(2,1)} %get-tuple-element.258.gate_ref, bf16[896,2432]{1,0:T(8,128)(2,1)} %get-tuple-element.259.up_ref), custom_call_target="tpu_custom_call" | custom-call | flops 1 | bytes 1 | tf_op jit(solution)/shard_map/hidden_back/pallas_call | solution.py:468
  354.0 18.1 %collective-permute-done.34 = bf16[224,1152]{1,0:T(8,128)(2,1)S(1)} collective-permute-done((bf16[224,1152]{1,0:T(8,128)(2,1)S(1)}, bf16[224,1152]{1,0:T(8,128)(2,1)S(1)}, u32[]{:S(2)}, u32[]{:S(2)}) %collective-permute-start.34) | collective-permute-done | bytes 516128 | tf_op jit(solution)/shard_map/ppermute | solution.py:101
  375.3 9.3 %collective-permute-start.38 = (bf16[56,2304]{1,0:T(8,128)(2,1)S(1)}, bf16[56,2304]{1,0:T(8,128)(2,1)S(1)}, u32[]{:S(2)}, u32[]{:S(2)}) collective-permute-start(bf16[56,2304]{1,0:T(8,128)(2,1)S(1)} %get-tuple-element.420), channel_id=1, source_target_pairs={{0,2},{2,0},{4,6},{6,4},{1,3},{3,1},{5,7},{7,5},{8,10},{10,8},{12,... | collective-permute-start | bytes 774152 | tf_op jit(solution)/shard_map/ppermute | solution.py:101
  396.6 9.0 %collective-permute-done.39 = bf16[56,2304]{1,0:T(8,128)(2,1)S(1)} collective-permute-done((bf16[56,2304]{1,0:T(8,128)(2,1)S(1)}, bf16[56,2304]{1,0:T(8,128)(2,1)S(1)}, u32[]{:S(2)}, u32[]{:S(2)}) %collective-permute-start.39) | collective-permute-done | bytes 258080 | tf_op jit(solution)/shard_map/ppermute | solution.py:101
  418.0 11.2 %collective-permute-done.44 = bf16[56,3456]{1,0:T(8,128)(2,1)S(1)} collective-permute-done((bf16[56,3456]{1,0:T(8,128)(2,1)S(1)}, bf16[56,3456]{1,0:T(8,128)(2,1)S(1)}, u32[]{:S(2)}, u32[]{:S(2)}) %collective-permute-start.44) | collective-permute-done | bytes 387104 | tf_op jit(solution)/shard_map/ppermute | solution.py:101
  429.2 13.3 %collective-permute-done.45 = bf16[56,3456]{1,0:T(8,128)(2,1)S(1)} collective-permute-done((bf16[56,3456]{1,0:T(8,128)(2,1)S(1)}, bf16[56,3456]{1,0:T(8,128)(2,1)S(1)}, u32[]{:S(2)}, u32[]{:S(2)}) %collective-permute-start.45) | collective-permute-done | bytes 387104 | tf_op jit(solution)/shard_map/ppermute | solution.py:101
  454.4 11.0 %collective-permute-done.48 = bf16[2,2,256,128]{3,2,1,0:T(8,128)(2,1)} collective-permute-done((bf16[2,2,256,128]{3,2,1,0:T(8,128)(2,1)}, bf16[2,2,256,128]{3,2,1,0:T(8,128)(2,1)}, u32[]{:S(2)}, u32[]{:S(2)}) %collective-permute-start.48) | collective-permute-done | bytes 262176 | tf_op jit(solution)/shard_map/ppermute | solution.py:101
  465.4 9.4 %collective-permute-done.49 = bf16[2,2,256,128]{3,2,1,0:T(8,128)(2,1)} collective-permute-done((bf16[2,2,256,128]{3,2,1,0:T(8,128)(2,1)}, bf16[2,2,256,128]{3,2,1,0:T(8,128)(2,1)}, u32[]{:S(2)}, u32[]{:S(2)}) %collective-permute-start.49) | collective-permute-done | bytes 262176 | tf_op jit(solution)/shard_map/ppermute | solution.py:101
  503.5 11.1 %collective-permute-done.55 = bf16[152,896]{1,0:T(8,128)(2,1)S(1)} collective-permute-done((bf16[152,896]{1,0:T(8,128)(2,1)S(1)}, bf16[152,896]{1,0:T(8,128)(2,1)S(1)}, u32[]{:S(2)}, u32[]{:S(2)}) %collective-permute-start.55) | collective-permute-done | bytes 272416 | tf_op jit(solution)/shard_map/ppermute | solution.py:101
  515.5 9.8 %collective-permute-start.59 = (bf16[64,1152]{1,0:T(8,128)(2,1)S(1)}, bf16[64,1152]{1,0:T(8,128)(2,1)S(1)}, u32[]{:S(2)}, u32[]{:S(2)}) collective-permute-start(bf16[64,1152]{1,0:T(8,128)(2,1)S(1)} %get-tuple-element.436), channel_id=1, source_target_pairs={{0,4},{2,6},{4,0},{6,2},{1,5},{3,7},{5,1},{7,3},{8,12},{10,14},{12... | collective-permute-start | bytes 442376 | tf_op jit(solution)/shard_map/ppermute | solution.py:101
  527.9 6.8 %collective-permute-done.59 = bf16[64,1152]{1,0:T(8,128)(2,1)S(1)} collective-permute-done((bf16[64,1152]{1,0:T(8,128)(2,1)S(1)}, bf16[64,1152]{1,0:T(8,128)(2,1)S(1)}, u32[]{:S(2)}, u32[]{:S(2)}) %collective-permute-start.59) | collective-permute-done | bytes 147488 | tf_op jit(solution)/shard_map/ppermute | solution.py:101
  (451 shorter events, 252.0 us)
Async XLA Ops:
  7.2 218.7 %all-gather.2.cloned.1.call-start = ((), (), s32[]{:S(2)}) async-start(), calls=%async_computation | async-start | bytes 4630528 | tf_op jit(solution)/shard_map/all_gather | solution.py:582
  41.6 32.9 %collective-permute-start.7 = (bf16[4,64,1152]{2,1,0:T(8,128)(2,1)}, bf16[4,64,1152]{2,1,0:T(8,128)(2,1)}, u32[]{:S(2)}, u32[]{:S(2)}) collective-permute-start(bf16[4,64,1152]{2,1,0:T(8,128)(2,1)} %bitcast_dynamic-update-slice_fusion), channel_id=1, source_target_pairs={{0,16},{16,0},{1,17},{17,1},{2,18},{18,2},{3,19},{19,3},{4,20},{20... | collective-permute-start | bytes 1769480 | tf_op jit(solution)/shard_map/ppermute | solution.py:77
  45.7 28.8 %collective-permute-start.9 = (bf16[56,3328]{1,0:T(8,128)(2,1)}, bf16[56,3328]{1,0:T(8,128)(2,1)}, u32[]{:S(2)}, u32[]{:S(2)}) collective-permute-start(bf16[56,3328]{1,0:T(8,128)(2,1)} %maximum_maximum_fusion), channel_id=1, source_target_pairs={{0,4},{2,6},{4,0},{6,2},{1,5},{3,7},{5,1},{7,3},{8,12},{10,14},{12... | collective-permute-start | bytes 1118216 | tf_op jit(solution)/shard_map/ppermute | solution.py:77
  46.8 27.7 %collective-permute-start.10 = (bf16[56,3328]{1,0:T(8,128)(2,1)}, bf16[56,3328]{1,0:T(8,128)(2,1)}, u32[]{:S(2)}, u32[]{:S(2)}) collective-permute-start(bf16[56,3328]{1,0:T(8,128)(2,1)} %maximum_maximum_fusion), channel_id=1, source_target_pairs={{0,6},{2,4},{4,2},{6,0},{1,7},{3,5},{5,3},{7,1},{8,14},{10,12},{12... | collective-permute-start | bytes 1118216 | tf_op jit(solution)/shard_map/ppermute | solution.py:77
  87.4 43.4 %collective-permute-start.18 = (bf16[4,56,3328]{2,1,0:T(8,128)(2,1)}, bf16[4,56,3328]{2,1,0:T(8,128)(2,1)}, u32[]{:S(2)}, u32[]{:S(2)}) collective-permute-start(bf16[4,56,3328]{2,1,0:T(8,128)(2,1)} %pad_maximum_fusion.2), channel_id=1, source_target_pairs={{0,16},{16,0},{1,17},{17,1},{2,18},{18,2},{3,19},{19,3},{4,20},{20... | collective-permute-start | bytes 4472840 | tf_op jit(solution)/shard_map/ppermute | solution.py:77
  104.2 27.3 %collective-permute-start.19 = (bf16[4,56,2432]{2,1,0:T(8,128)(2,1)}, bf16[4,56,2432]{2,1,0:T(8,128)(2,1)}, u32[]{:S(2)}, u32[]{:S(2)}) collective-permute-start(bf16[4,56,2432]{2,1,0:T(8,128)(2,1)} %pad_maximum_fusion.5), channel_id=1, source_target_pairs={{0,1},{1,0},{2,3},{3,2},{4,5},{5,4},{6,7},{7,6},{8,9},{9,8},{10,11... | collective-permute-start | bytes 3268616 | tf_op jit(solution)/shard_map/ppermute | solution.py:77
  136.6 67.6 %collective-permute-start.22 = (bf16[2,4,56,2432]{3,2,1,0:T(8,128)(2,1)S(1)}, bf16[2,4,56,2432]{3,2,1,0:T(8,128)(2,1)S(1)}, u32[]{:S(2)}, u32[]{:S(2)}) collective-permute-start(bf16[2,4,56,2432]{3,2,1,0:T(8,128)(2,1)S(1)} %pad_maximum_fusion), channel_id=1, source_target_pairs={{0,16},{16,0},{1,17},{17,1},{2,18},{18,2},{3,19},{19,3},{4,20},{20... | collective-permute-start | bytes 6537224 | tf_op jit(solution)/shard_map/ppermute | solution.py:77
  160.2 59.1 %collective-permute-start.21 = (bf16[2,4,56,2432]{3,2,1,0:T(8,128)(2,1)S(1)}, bf16[2,4,56,2432]{3,2,1,0:T(8,128)(2,1)S(1)}, u32[]{:S(2)}, u32[]{:S(2)}) collective-permute-start(bf16[2,4,56,2432]{3,2,1,0:T(8,128)(2,1)S(1)} %fusion.1), channel_id=1, source_target_pairs={{0,1},{1,0},{2,3},{3,2},{4,5},{5,4},{6,7},{7,6},{8,9},{9,8},{10,11... | collective-permute-start | bytes 6537224 | tf_op jit(solution)/shard_map/ppermute | solution.py:77
  164.8 58.8 %collective-permute-start.25 = (bf16[512,896]{1,0:T(8,128)(2,1)}, bf16[512,896]{1,0:T(8,128)(2,1)}, u32[]{:S(2)}, u32[]{:S(2)}) collective-permute-start(bf16[512,896]{1,0:T(8,128)(2,1)} %convert_element_type.369.u_own), channel_id=1, source_target_pairs={{0,8},{8,0},{1,9},{9,1},{2,10},{10,2},{3,11},{11,3},{4,12},{12,4},... | collective-permute-start | bytes 2752520 | tf_op jit(solution)/shard_map/ppermute | solution.py:51
  267.5 27.6 %collective-permute-start.27 = (bf16[4,2,80,896]{3,2,1,0:T(8,128)(2,1)}, bf16[4,2,80,896]{3,2,1,0:T(8,128)(2,1)}, u32[]{:S(2)}, u32[]{:S(2)}) collective-permute-start(bf16[4,2,80,896]{3,2,1,0:T(8,128)(2,1)} %get-tuple-element.366), channel_id=1, source_target_pairs={{0,16},{16,0},{1,17},{17,1},{2,18},{18,2},{3,19},{19,3},{4,20},{20... | collective-permute-start | bytes 3440648 | tf_op jit(solution)/shard_map/ppermute | solution.py:101
  295.1 36.8 %collective-permute-start.28 = (bf16[2,224,1152]{2,1,0:T(8,128)(2,1)}, bf16[2,224,1152]{2,1,0:T(8,128)(2,1)}, u32[]{:S(2)}, u32[]{:S(2)}) collective-permute-start(bf16[2,224,1152]{2,1,0:T(8,128)(2,1)} %get-tuple-element.246), channel_id=1, source_target_pairs={{0,1},{1,0},{2,3},{3,2},{4,5},{5,4},{6,7},{7,6},{8,9},{9,8},{10,11... | collective-permute-start | bytes 3096584 | tf_op jit(solution)/shard_map/ppermute | solution.py:51
  296.7 35.1 %collective-permute-start.29 = (bf16[2,224,1152]{2,1,0:T(8,128)(2,1)}, bf16[2,224,1152]{2,1,0:T(8,128)(2,1)}, u32[]{:S(2)}, u32[]{:S(2)}) collective-permute-start(bf16[2,224,1152]{2,1,0:T(8,128)(2,1)} %get-tuple-element.248), channel_id=1, source_target_pairs={{0,16},{16,0},{1,17},{17,1},{2,18},{18,2},{3,19},{19,3},{4,20},{20... | collective-permute-start | bytes 3096584 | tf_op jit(solution)/shard_map/ppermute | solution.py:51
  300.4 31.5 %collective-permute-start.30 = (bf16[4,72,896]{2,1,0:T(8,128)(2,1)}, bf16[4,72,896]{2,1,0:T(8,128)(2,1)}, u32[]{:S(2)}, u32[]{:S(2)}) collective-permute-start(bf16[4,72,896]{2,1,0:T(8,128)(2,1)} %get-tuple-element.426), channel_id=1, source_target_pairs={{0,16},{16,0},{1,17},{17,1},{2,18},{18,2},{3,19},{19,3},{4,20},{20... | collective-permute-start | bytes 1548296 | tf_op jit(solution)/shard_map/ppermute | solution.py:101
  304.2 27.6 %collective-permute-start.31 = (bf16[4,80,896]{2,1,0:T(8,128)(2,1)}, bf16[4,80,896]{2,1,0:T(8,128)(2,1)}, u32[]{:S(2)}, u32[]{:S(2)}) collective-permute-start(bf16[4,80,896]{2,1,0:T(8,128)(2,1)} %get-tuple-element.400), channel_id=1, source_target_pairs={{0,1},{1,0},{2,3},{3,2},{4,5},{5,4},{6,7},{7,6},{8,9},{9,8},{10,11... | collective-permute-start | bytes 1720328 | tf_op jit(solution)/shard_map/ppermute | solution.py:101
  332.0 40.1 %collective-permute-start.32 = (bf16[2,224,1280]{2,1,0:T(8,128)(2,1)}, bf16[2,224,1280]{2,1,0:T(8,128)(2,1)S(1)}, u32[]{:S(2)}, u32[]{:S(2)}) collective-permute-start(bf16[2,224,1280]{2,1,0:T(8,128)(2,1)} %get-tuple-element.264), channel_id=1, source_target_pairs={{0,1},{1,0},{2,3},{3,2},{4,5},{5,4},{6,7},{7,6},{8,9},{9,8},{10,11... | collective-permute-start | bytes 3440648 | tf_op jit(solution)/shard_map/ppermute | solution.py:51
  333.5 38.6 %collective-permute-start.33 = (bf16[2,224,1280]{2,1,0:T(8,128)(2,1)}, bf16[2,224,1280]{2,1,0:T(8,128)(2,1)S(1)}, u32[]{:S(2)}, u32[]{:S(2)}) collective-permute-start(bf16[2,224,1280]{2,1,0:T(8,128)(2,1)} %get-tuple-element.266), channel_id=1, source_target_pairs={{0,16},{16,0},{1,17},{17,1},{2,18},{18,2},{3,19},{19,3},{4,20},{20... | collective-permute-start | bytes 3440648 | tf_op jit(solution)/shard_map/ppermute | solution.py:51
  336.2 35.9 %collective-permute-start.34 = (bf16[224,1152]{1,0:T(8,128)(2,1)S(1)}, bf16[224,1152]{1,0:T(8,128)(2,1)S(1)}, u32[]{:S(2)}, u32[]{:S(2)}) collective-permute-start(bf16[224,1152]{1,0:T(8,128)(2,1)S(1)} %get-tuple-element.424), channel_id=1, source_target_pairs={{0,16},{16,0},{1,17},{17,1},{2,18},{18,2},{3,19},{19,3},{4,20},{20... | collective-permute-start | bytes 1548296 | tf_op jit(solution)/shard_map/ppermute | solution.py:101
  372.8 32.9 %collective-permute-start.41 = (bf16[4,56,2176]{2,1,0:T(8,128)(2,1)S(1)}, bf16[4,56,2176]{2,1,0:T(8,128)(2,1)S(1)}, u32[]{:S(2)}, u32[]{:S(2)}) collective-permute-start(bf16[4,56,2176]{2,1,0:T(8,128)(2,1)S(1)} %get-tuple-element.380), channel_id=1, source_target_pairs={{0,16},{16,0},{1,17},{17,1},{2,18},{18,2},{3,19},{19,3},{4,20},{20... | collective-permute-start | bytes 2924552 | tf_op jit(solution)/shard_map/ppermute | solution.py:101
  374.2 31.4 %collective-permute-start.42 = (bf16[224,1280]{1,0:T(8,128)(2,1)S(1)}, bf16[224,1280]{1,0:T(8,128)(2,1)S(1)}, u32[]{:S(2)}, u32[]{:S(2)}) collective-permute-start(bf16[224,1280]{1,0:T(8,128)(2,1)S(1)} %get-tuple-element.398), channel_id=1, source_target_pairs={{0,1},{1,0},{2,3},{3,2},{4,5},{5,4},{6,7},{7,6},{8,9},{9,8},{10,11... | collective-permute-start | bytes 1720328 | tf_op jit(solution)/shard_map/ppermute | solution.py:101
  405.8 36.7 %collective-permute-start.43 = (bf16[4,2,2,256,128]{4,3,2,0,1:T(8,128)(2,1)S(1)}, bf16[4,2,2,256,128]{4,3,2,0,1:T(8,128)(2,1)S(1)}, u32[]{:S(2)}, u32[]{:S(2)}) collective-permute-start(bf16[4,2,2,256,128]{4,3,2,0,1:T(8,128)(2,1)S(1)} %get-tuple-element.370), channel_id=1, source_target_pairs={{0,1},{1,0},{2,3},{3,2},{4,5},{5,4},{6,7},{7,6},{8,9},{9,8},{10,11... | collective-permute-start | bytes 3145736 | tf_op jit(solution)/shard_map/ppermute | solution.py:101
  413.1 29.4 %collective-permute-start.45 = (bf16[56,3456]{1,0:T(8,128)(2,1)S(1)}, bf16[56,3456]{1,0:T(8,128)(2,1)S(1)}, u32[]{:S(2)}, u32[]{:S(2)}) collective-permute-start(bf16[56,3456]{1,0:T(8,128)(2,1)S(1)} %get-tuple-element.389), channel_id=1, source_target_pairs={{0,4},{2,6},{4,0},{6,2},{1,5},{3,7},{5,1},{7,3},{8,12},{10,14},{12... | collective-permute-start | bytes 1161224 | tf_op jit(solution)/shard_map/ppermute | solution.py:101
  415.1 27.4 %collective-permute-start.46 = (bf16[56,3456]{1,0:T(8,128)(2,1)S(1)}, bf16[56,3456]{1,0:T(8,128)(2,1)S(1)}, u32[]{:S(2)}, u32[]{:S(2)}) collective-permute-start(bf16[56,3456]{1,0:T(8,128)(2,1)S(1)} %get-tuple-element.386), channel_id=1, source_target_pairs={{0,6},{2,4},{4,2},{6,0},{1,7},{3,5},{5,3},{7,1},{8,14},{10,12},{12... | collective-permute-start | bytes 1161224 | tf_op jit(solution)/shard_map/ppermute | solution.py:101
  445.1 29.6 %collective-permute-start.49 = (bf16[2,2,256,128]{3,2,1,0:T(8,128)(2,1)}, bf16[2,2,256,128]{3,2,1,0:T(8,128)(2,1)}, u32[]{:S(2)}, u32[]{:S(2)}) collective-permute-start(bf16[2,2,256,128]{3,2,1,0:T(8,128)(2,1)} %get-tuple-element.411), channel_id=1, source_target_pairs={{4,0},{6,2},{5,1},{7,3},{12,8},{14,10},{13,9},{15,11},{20,16},{22,... | collective-permute-start | bytes 786440 | tf_op jit(solution)/shard_map/ppermute | solution.py:101
  446.4 28.3 %collective-permute-start.50 = (bf16[2,2,256,128]{3,2,1,0:T(8,128)(2,1)}, bf16[2,2,256,128]{3,2,1,0:T(8,128)(2,1)}, u32[]{:S(2)}, u32[]{:S(2)}) collective-permute-start(bf16[2,2,256,128]{3,2,1,0:T(8,128)(2,1)} %get-tuple-element.410), channel_id=1, source_target_pairs={{4,2},{6,0},{5,3},{7,1},{12,10},{14,8},{13,11},{15,9},{20,18},{22,... | collective-permute-start | bytes 786440 | tf_op jit(solution)/shard_map/ppermute | solution.py:101
  (111 other events, 1280.0 us)
Sparse Core Ops, SparseCore 0:
  105.6 110.7 all-gather.1

commit v3 on v2

--- a/solution.py
+++ b/solution.py
@@ -93,17 +93,20 @@
     return total_of(parts).astype(jnp.bfloat16)
 
 
+def parts_of(array, index, dim, count):
+    return [pick(array, index ^ step, dim) for step in range(count)]
+
+
+def send_parts(axis, parts, down_only=False):
+    out = parts[:1]
+    for step in range(1, len(parts)):
+        routes = [(i, i ^ step) for i in range(len(parts)) if i ^ step < i or not down_only]
+        out.append(lax.ppermute(parts[step], axis, routes))
+    return out
+
+
 def parts_along(axis, array, dim, count, down_only=False):
-    index = lax.axis_index(axis)
-    parts = [pick(array, index, dim)]
-    for step in range(1, count):
-        routes = [(i, i ^ step) for i in range(count) if i ^ step < i or not down_only]
-        parts.append(lax.ppermute(pick(array, index ^ step, dim), axis, routes))
-    return parts
-
-
-def reduce_axis(array, axis, dim, count):
-    return total_of(parts_along(axis, array, dim, count))
+    return send_parts(axis, parts_of(array, lax.axis_index(axis), dim, count), down_only)
 
 
 def hold(*values):
@@ -448,36 +451,62 @@
     )(inner, *upper)
 
 
-def back_kernel(steps, d_ref, gate_ref, up_ref, own_ref, other_ref):
-    result = dot(d_ref[0], gate_ref[...], 1, 1) + dot(d_ref[1], up_ref[...], 1, 1)
-
-    @pl.when(pl.program_id(0) < steps)
-    def _():
-        own_ref[...] = result
-
-    @pl.when(pl.program_id(0) >= steps)
-    def _():
-        other_ref[...] = result
-
-
-def hidden_back(d_both, gate, up, height=256):
+def back_kernel(half, d_ref, gate_ref, up_ref, own_ref, other_ref):
+    step, width = pl.program_id(0), d_ref.shape[2]
+    rest = half % width
+
+    def add(limit, first):
+        d_gate, d_up, gate, up = d_ref[0], d_ref[1], gate_ref[...], up_ref[...]
+        if limit:
+            d_gate, d_up, gate, up = (part[:, :limit] for part in (d_gate, d_up, gate, up))
+        count = own_ref.shape[0]
+        for out, rows in ((own_ref, slice(0, count)), (other_ref, slice(count, 2 * count))):
+            result = dot(d_gate[rows], gate, 1, 1) + dot(d_up[rows], up, 1, 1)
+            out[...] = result if first else out[...] + result
+
+    last = pl.cdiv(half, width) - 1
+    pl.when(step == 0)(lambda: add(0, True))
+    pl.when((step > 0) & (step < last))(lambda: add(0, False))
+    pl.when(step == last)(lambda: add(rest, False))
+
+
+def hidden_back(d_both, gate, up, width=512):
     _, count, half = d_both.shape
     size = gate.shape[0]
-    steps = count // height // 2
-    whole = pl.BlockSpec((size, half), lambda i: (0, 0))
+    columns = pl.BlockSpec((size, width), lambda i: (0, i))
+    whole = pl.BlockSpec((count // 2, size), lambda i: (0, 0))
     return pl.pallas_call(
-        functools.partial(back_kernel, steps),
-        grid=(2 * steps,),
-        in_specs=[pl.BlockSpec((2, height, half), lambda i: (0, i, 0)), whole, whole],
-        out_specs=[
-            pl.BlockSpec((height, size), lambda i: (jnp.minimum(i, steps - 1), 0)),
-            pl.BlockSpec((height, size), lambda i: (jnp.maximum(i, steps) - steps, 0)),
-        ],
+        functools.partial(back_kernel, half),
+        grid=(pl.cdiv(half, width),),
+        in_specs=[pl.BlockSpec((2, count, width), lambda i: (0, 0, i)), columns, columns],
+        out_specs=[whole, whole],
         out_shape=[jax.ShapeDtypeStruct((count // 2, size), jnp.float32)] * 2,
         compiler_params=pltpu.CompilerParams(vmem_limit_bytes=56 * 2**20),
         cost_estimate=pl.CostEstimate(flops=1, bytes_accessed=1, transcendentals=0),
         name="hidden_back",
     )(d_both, gate, up)
+
+
+def project_kernel(inner_ref, down_ref, out_ref):
+    out_ref[...] = dot(inner_ref[...], down_ref[...])
+
+
+def project(inner, down, height=512):
+    count, half = inner.shape
+    size = down.shape[1]
+    return pl.pallas_call(
+        project_kernel,
+        grid=(count // height,),
+        in_specs=[
+            pl.BlockSpec((height, half), lambda i: (i, 0)),
+            pl.BlockSpec((half, size), lambda i: (0, 0)),
+        ],
+        out_specs=pl.BlockSpec((height, size), lambda i: (i, 0)),
+        out_shape=jax.ShapeDtypeStruct((count, size), jnp.float32),
+        compiler_params=pltpu.CompilerParams(vmem_limit_bytes=56 * 2**20),
+        cost_estimate=pl.CostEstimate(flops=1, bytes_accessed=1, transcendentals=0),
+        name="project",
+    )(inner, down)
 
 
 def layer(
@@ -503,7 +532,6 @@
 ):
     xs, zs, ys = sizes
     everyone = ("x", "core", "z", "y")
-    chips = ("x", "z", "y")
     low = jnp.bfloat16
     rows, block_len, width = inputs.shape
     tokens = rows * block_len
@@ -516,7 +544,6 @@
     share = qkv_weight.shape[0]
     small_share = gains_biases.shape[0]
     ff_share = down_weight.shape[0]
-    ff_slab = ff_share * zs * ys
     half = FF // 2
     x_index, z_index = lax.axis_index("x"), lax.axis_index("z")
 
@@ -537,8 +564,8 @@
 
     own_gu = (
         gate_up_weight.astype(low)
-        .reshape(share, 2, xs, 2, ff_slab)
-        .transpose(3, 1, 0, 2, 4)
+        .reshape(share, 2, xs, 2, zs, ys * ff_share)
+        .transpose(3, 1, 0, 4, 2, 5)
         .reshape(4, share, half)
     )
     quad = core * 2 + y_index
@@ -579,7 +606,7 @@
     upstream = cotangent.reshape(tokens, D).astype(jnp.float32) * valid.reshape(tokens, 1)
 
     own_kv, second, down_weight, upstream = hold(own_kv, second, down_weight, upstream)
-    full_down = lax.all_gather(down_weight.astype(low), chips, axis=0, tiled=True)
+    full_down = lax.all_gather(down_weight.astype(low), ("z", "x", "y"), axis=0, tiled=True)
     all_kv = pieces_along("z", own_kv, zs, True)
     second = pieces_along("y", place(second, z_index), ys)
     all_kv, first, second, upstream = hold(all_kv, first, second, upstream)
@@ -622,26 +649,19 @@
         first[1] = swap("y", first[1], ys, 1)
         return first, second[:1] + [swap("x", second[i], xs, i) for i in range(1, xs)]
 
-    cut = ff_share // 16 * 8
+    left = gate_up_grads(spot, features, d_both, xs, 0, middle, 384)
+    *left, d_both, inner = hold(*left, d_both, inner)
+    left = exchange(left)
+    right = gate_up_grads(spot, features, d_both, xs, middle, half, 384)
     grad_down = down_grad(inner, pair_up, 512)
-    grad_down, d_both = hold(grad_down, d_both)
-    grad_down = grad_down.reshape(xs, zs, ys, ff_share, D)
-    down_y = parts_along("y", grad_down[:, :, :, :cut], 2, ys)
-    down_x = parts_along("x", grad_down[:, :, :, cut:], 0, xs)
-    left = gate_up_grads(spot, features, d_both, xs, 0, middle, 384)
-    right = gate_up_grads(spot, features, d_both, xs, middle, half, 384)
-    down_y, down_x, left, right, d_both, inner = hold(down_y, down_x, left, right, d_both, inner)
-    left = exchange(left)
-    down_y = parts_along("x", add_up(down_y), 0, xs)
-    down_x = parts_along("y", add_up(down_x), 1, ys)
+    left, right, grad_down, d_both, inner = hold(left, right, grad_down, d_both, inner)
+    red_down = lax.psum_scatter(grad_down, "z", scatter_dimension=0, tiled=True)
+    output = project(inner, full_down)
+    right = exchange(right)
     d_normed2 = hidden_back(d_both, full_gate, full_up)
-    output = jnp.dot(inner, full_down, preferred_element_type=jnp.float32)
-    left, down_y, down_x, right, d_normed2, output = hold(
-        left, down_y, down_x, right, d_normed2, output
-    )
-    right = exchange(right)
-    first = parts_along("x", add_up(left[0]), 0, xs)
-    second = parts_along("y", add_up(left[1]), 0, ys)
+    left, right, d_normed2, output = hold(left, right, d_normed2, output)
+    first = jnp.concatenate([add_up(left[0]), add_up(right[0])], -1)
+    second = jnp.concatenate([add_up(left[1]), add_up(right[1])], -1)
     d_normed2 = d_normed2[0] + swap("core", d_normed2[1], 2, 1)
 
     change_mlp, grad_gain_mlp = norm_back(hidden_state, inverse_mlp, gain_mlp, d_normed2)
@@ -652,44 +672,44 @@
     grad_out = parts_along(
         "core", grad_out.astype(low).reshape(xs, 2, zs, 2 * share, D), 1, 2
     )
+    first, second = parts_of(first, x_index, 0, xs), parts_of(second, y_index, 0, ys)
+    first, second, grad_out, d_mixed = hold(first, second, grad_out, d_mixed)
+    first, second = send_parts("x", first), send_parts("y", second)
     d_query, kv_terms = [None] * KVH, [None] * KVH
     d_query[0], kv_terms[0] = attention_back(
         0, meta, query, d_mixed, attended, logs, all_kv, block_len
     )
-    right, first, second, grad_out, d_query[0], kv_terms[0], query = hold(
-        right, first, second, grad_out, d_query[0], kv_terms[0], query
-    )
-    left = jnp.concatenate([add_up(first), add_up(second)], -1)
-    left = parts_along("z", left.reshape(zs, 2 * share, -1), 0, zs)
-    first = add_up(right[0]).reshape(xs, zs, 2 * share, -1)
-    first = parts_along("x", jnp.concatenate([first, add_up(grad_out)], -1), 0, xs)
-    second = parts_along("y", add_up(right[1]), 0, ys)
+    first, second, d_query[0], kv_terms[0], query = hold(
+        first, second, d_query[0], kv_terms[0], query
+    )
+    red_quads = [add_up(part).reshape(zs, 2 * share, -1) for part in (first, second)]
+    red_quads = parts_of(jnp.concatenate(red_quads, -1), z_index, 0, zs)
+    grad_out = parts_of(add_up(grad_out), x_index, 0, xs)
+    kv_terms[0] = parts_of(kv_terms[0], y_index, 0, ys)
+    red_quads, grad_out, kv_terms[0], query = hold(red_quads, grad_out, kv_terms[0], query)
+    red_quads, grad_out = send_parts("z", red_quads), send_parts("x", grad_out)
+    kv_terms[0] = send_parts("y", kv_terms[0])
     d_query[1], kv_terms[1] = attention_back(
         1, meta, query, d_mixed, attended, logs, all_kv, block_len
     )
-    left, first, second, kv_terms, d_query[1] = hold(left, first, second, kv_terms, d_query[1])
-    kv_terms = parts_along("y", jnp.stack(kv_terms, 2), 0, ys)
-    right = jnp.concatenate([add_up(first), add_up(second).reshape(zs, 2 * share, -1)], -1)
-    right = parts_along("z", right, 0, zs)
+    red_quads, grad_out, kv_terms, d_query[1], red_down = hold(
+        red_quads, grad_out, kv_terms, d_query[1], red_down
+    )
+    kv_terms[1] = parts_along("y", kv_terms[1], 0, ys)
+    red_down = parts_along("x", red_down.reshape(xs, ys, ff_share, D), 0, xs)
     output = hidden_state + pair_sum(output)
-    kv_terms, right, output, left, down_y, down_x = hold(
-        kv_terms, right, output, left, down_y, down_x
-    )
-    kv_terms = parts_along("z", add_up(kv_terms), 0, zs, True)
-    left, right = add_up(left), add_up(right)
-    red_out = right[:, half - middle : half - middle + D]
-    red_quads = jnp.stack(
-        [
-            jnp.concatenate([left[:, :middle], right[:, : half - middle]], 1),
-            jnp.concatenate([left[:, middle:], right[:, half - middle + D :]], 1),
-        ],
-        0,
-    )
+    kv_terms, red_down, output, red_quads, grad_out = hold(
+        kv_terms, red_down, output, red_quads, grad_out
+    )
+    kv_terms = jnp.stack([add_up(part) for part in kv_terms], 1)
+    kv_terms = parts_along("z", kv_terms, 0, zs, True)
+    kv_terms, red_quads, red_down, grad_out = hold(kv_terms, red_quads, red_down, grad_out)
+    red_quads = add_up(red_quads)
+    red_quads = jnp.stack([red_quads[:, :half], red_quads[:, half:]], 0)
     red_quads = parts_along("y", red_quads.reshape(2, ys, share, half), 1, ys)
-    red_down = jnp.concatenate([add_up(down_y), add_up(down_x)], 1)
-    kv_terms, red_quads, red_down = hold(kv_terms, red_quads, red_down)
+    red_down = parts_along("y", add_up(red_down), 0, ys)
+    red_out = parts_along("z", add_up(grad_out), 0, zs)
     kv_grads = total_of(kv_terms)
-    red_down = parts_along("z", red_down, 0, zs)
     red_gu = parts_along("core", place(red_quads, y_index), 1, 2)
     d_query = jnp.concatenate(d_query, 0)
     kv_grads = kv_grads.reshape(KVH, tokens, 2 * HD).transpose(0, 2, 1)
@@ -716,7 +736,8 @@
     red_qkv = grad_qkv.reshape(xs, 2, zs, -1, qkv_width)
     red_qkv = add_up(parts_along("core", red_qkv, 1, 2))
     red_qkv = parts_along("x", red_qkv, 0, xs)
-    red_qkv, red_down, red_gu = hold(red_qkv, red_down, red_gu)
+    red_qkv, red_gu, red_out, red_down = hold(red_qkv, red_gu, red_out, red_down)
+    red_out = add_up(red_out)
     red_qkv = add_up(parts_along("z", add_up(red_qkv), 0, zs))
     red_down = total_of(red_down)
 
@@ -732,9 +753,13 @@
     red_small = mine[share, :small_share]
     red_gu = place(red_gu, core)
     red_gu = (
-        red_gu.reshape(2, 2, share, xs, ff_slab).transpose(2, 1, 3, 0, 4).reshape(share, 2 * FF)
-    ).astype(jnp.float32)
-
+        red_gu.reshape(2, 2, share, zs, xs, ys * ff_share)
+        .transpose(2, 1, 4, 0, 3, 5)
+        .reshape(share, 2 * FF)
+        .astype(jnp.float32)
+    )
+
+    red_gu, red_qkv, red_out, red_small = hold(red_gu, red_qkv, red_out, red_small)
     local_square = (
         jnp.sum(red_qkv * red_qkv)
         + jnp.sum(red_out * red_out)

time: 594 us -> 581 us (0.978)
  starting transfers between devices: 105 us -> 85.3 us
  waiting for transfers between devices: 235 us -> 250 us
  other arithmetic: 68.4 us -> 56.9 us
  matrix products: 22.4 us -> 14.3 us
  Pallas kernels: 91.2 us -> 99.1 us
    ppermute x29 -> x24, starting transfers between devices: 51.4 us -> 35.7 us  [send_parts(): out.append(lax.ppermute(parts[step], axis, routes))]
    ppermute x20, waiting for transfers between devices: 122 us -> 135 us  [pieces_along(): pieces.append(lax.ppermute(value, axis, routes))]
    dot_general x1 -> x0, matrix products: 9.53 us -> none  [layer(): output = jnp.dot(inner, full_down, preferred_element_type=jnp.float32)]
    pallas_call x1 -> x2, Pallas kernels: 17.4 us -> 26.5 us  [the longest x1 16.3 us: hidden_back(): pl.pallas_call(functools.partial(back_kernel, half), grid=(pl.cdiv(half,...]
    ppermute x20, starting transfers between devices: 36.5 us -> 28.5 us  [pieces_along(): pieces.append(lax.ppermute(value, axis, routes))]
    unnamed x138 -> x160, local copies, waits for them, and re-layouts: 8.21 us -> 15.5 us
    convert_element_type x19 -> x14, other arithmetic: 12.9 us -> 11.8 us  [add_up(): return total_of(parts).astype(jnp.bfloat16)]
    ppermute x29 -> x24, waiting for transfers between devices: 97.1 us -> 97.8 us  [send_parts(): out.append(lax.ppermute(parts[step], axis, routes))]
  transfers between devices with their start and end apart: 68 -> 64, of which waited for: 30 -> 33; matrix products, arithmetic and copies ran while one was open for 14% -> 12% of each run, Pallas kernels for 9% -> 11%
where the time goes in v3:
time: 581 us; the launch traced here: 571 us
  waiting for transfers between devices  250 us (43%)
  Pallas kernels  99.1 us (17%)
  starting transfers between devices  85.3 us (15%)
  other arithmetic  56.9 us (10%)
  local copies, waits for them, and re-layouts  41.6 us (7%)
  between operations  24.2 us (4%)
  matrix products  14.3 us (2%)
    ppermute x20, waiting for transfers between devices, pieces_along(): pieces.append(lax.ppermute(value, axis, routes))  135 us
    ppermute x24, waiting for transfers between devices, send_parts(): out.append(lax.ppermute(parts[step], axis, routes))  97.8 us
    ppermute x24, starting transfers between devices, send_parts(): out.append(lax.ppermute(parts[step], axis, routes))  35.7 us
    ppermute x20, starting transfers between devices, pieces_along(): pieces.append(lax.ppermute(value, axis, routes))  28.5 us
    pallas_call x1, Pallas kernels, hidden_part(): pl.pallas_call(functools.partial(hidden_kernel, xs, 256), grid_spec=pltpu...  26.8 us
    pallas_call x2, Pallas kernels, gate_up_grads(): pl.pallas_call(functools.partial(grads_kernel, xs), grid_spec=pltpu.Prefe...  21.9 us
    ppermute x18, starting transfers between devices, swap(): return lax.ppermute(value, axis, [(i, i ^ step) for i in range(count)])  21 us
    ppermute x18, waiting for transfers between devices, swap(): return lax.ppermute(value, axis, [(i, i ^ step) for i in range(count)])  17.6 us
  transfers between devices with their start and end apart: 64, of which 33 were waited for; matrix products, arithmetic and copies ran while one was open for 12% of the time, Pallas kernels for 11%

profile of v3, /device:TPU:0, one launch (start us, length us, event | category | flops | bytes accessed | tf_op | source)
XLA Modules:
  0.0 571.4 jit_solution(16712232507672661871)
XLA Ops:
  33.1 8.4 %collective-permute-done.2 = bf16[64,1152]{1,0:T(8,128)(2,1)S(1)} collective-permute-done((bf16[64,1152]{1,0:T(8,128)(2,1)S(1)}, bf16[64,1152]{1,0:T(8,128)(2,1)S(1)}, u32[]{:S(2)}, u32[]{:S(2)}) %collective-permute-start.2) | collective-permute-done | bytes 147488 | tf_op jit(solution)/shard_map/ppermute | solution.py:77
  50.7 7.9 %collective-permute-done.10 = bf16[56,3328]{1,0:T(8,128)(2,1)} collective-permute-done((bf16[56,3328]{1,0:T(8,128)(2,1)}, bf16[56,3328]{1,0:T(8,128)(2,1)}, u32[]{:S(2)}, u32[]{:S(2)}) %collective-permute-start.10) | collective-permute-done | bytes 372768 | tf_op jit(solution)/shard_map/ppermute | solution.py:77
  63.0 13.5 %collective-permute-done.9 = bf16[56,3328]{1,0:T(8,128)(2,1)} collective-permute-done((bf16[56,3328]{1,0:T(8,128)(2,1)}, bf16[56,3328]{1,0:T(8,128)(2,1)}, u32[]{:S(2)}, u32[]{:S(2)}) %collective-permute-start.9) | collective-permute-done | bytes 372768 | tf_op jit(solution)/shard_map/ppermute | solution.py:77
  92.9 6.3 %collective-permute-done.13 = bf16[56,2432]{1,0:T(8,128)(2,1)} collective-permute-done((bf16[56,2432]{1,0:T(8,128)(2,1)}, bf16[56,2432]{1,0:T(8,128)(2,1)}, u32[]{:S(2)}, u32[]{:S(2)}) %collective-permute-start.13) | collective-permute-done | bytes 272416 | tf_op jit(solution)/shard_map/ppermute | solution.py:77
  104.0 6.7 %collective-permute-start.15 = (bf16[2,2,256,128]{3,2,1,0:T(8,128)(2,1)S(1)}, bf16[2,2,256,128]{3,2,1,0:T(8,128)(2,1)S(1)}, u32[]{:S(2)}, u32[]{:S(2)}) collective-permute-start(bf16[2,2,256,128]{3,2,1,0:T(8,128)(2,1)S(1)} %bitcast.339), channel_id=1, source_target_pairs={{0,2},{4,6},{1,3},{5,7},{8,10},{12,14},{9,11},{13,15},{16,18},{20,... | collective-permute-start | bytes 786440 | tf_op jit(solution)/shard_map/ppermute | solution.py:77
  119.8 9.2 %collective-permute-done.16 = bf16[2,2,256,128]{3,2,1,0:T(8,128)(2,1)S(1)} collective-permute-done((bf16[2,2,256,128]{3,2,1,0:T(8,128)(2,1)S(1)}, bf16[2,2,256,128]{3,2,1,0:T(8,128)(2,1)S(1)}, u32[]{:S(2)}, u32[]{:S(2)}) %collective-permute-start.16) | collective-permute-done | bytes 262176 | tf_op jit(solution)/shard_map/ppermute | solution.py:77
  137.9 24.5 %collective-permute-done.20 = bf16[4,2,2,256,128]{4,3,2,1,0:T(8,128)(2,1)S(1)} collective-permute-done((bf16[4,2,2,256,128]{4,3,2,1,0:T(8,128)(2,1)S(1)}, bf16[4,2,2,256,128]{4,3,2,1,0:T(8,128)(2,1)S(1)}, u32[]{:S(2)}, u32[]{:S(2)}) %collective-permute-start.20) | collective-permute-done | bytes 1048608 | tf_op jit(solution)/shard_map/ppermute | solution.py:77
  166.0 5.4 attend.1
  171.9 32.0 %collective-permute-done.22 = bf16[2,4,56,2432]{3,2,1,0:T(8,128)(2,1)S(1)} collective-permute-done((bf16[2,4,56,2432]{3,2,1,0:T(8,128)(2,1)S(1)}, bf16[2,4,56,2432]{3,2,1,0:T(8,128)(2,1)S(1)}, u32[]{:S(2)}, u32[]{:S(2)}) %collective-permute-start.22) | collective-permute-done | bytes 2179104 | tf_op jit(solution)/shard_map/ppermute | solution.py:77
  203.9 19.8 %collective-permute-done.21 = bf16[2,4,56,2432]{3,2,1,0:T(8,128)(2,1)S(1)} collective-permute-done((bf16[2,4,56,2432]{3,2,1,0:T(8,128)(2,1)S(1)}, bf16[2,4,56,2432]{3,2,1,0:T(8,128)(2,1)S(1)}, u32[]{:S(2)}, u32[]{:S(2)}) %collective-permute-start.21) | collective-permute-done | bytes 2179104 | tf_op jit(solution)/shard_map/ppermute | solution.py:77
  229.3 26.8 %hidden.1 = (bf16[1024,2432]{1,0:T(8,128)(2,1)}, bf16[2,1024,2432]{2,1,0:T(8,128)(2,1)}, bf16[896,2432]{1,0:T(8,128)(2,1)}, bf16[896,2432]{1,0:T(8,128)(2,1)}, bf16[4,224,1024]{2,1,0:T(8,128)(2,1)}) custom-call(s32[2]{0:T(128)} %pad_add_fusion.spot, bf16[512,896]{1,0:T(8,128)(2,1)} %copy-done.28, bf16[512,896]{1,0:T(8,128)(2,1)} %collective-permute-done.24.n_other, ...), custom_call_target="tpu_custom_call" | custom-call | flops 1 | bytes 1 | tf_op jit(solution)/shard_map/hidden/pallas_call | solution.py:372
  256.1 10.0 %gate_up_grads.2 = (bf16[2,224,1152]{2,1,0:T(8,128)(2,1)}, bf16[2,224,1152]{2,1,0:T(8,128)(2,1)}, bf16[2,224,1152]{2,1,0:T(8,128)(2,1)}, bf16[2,224,1152]{2,1,0:T(8,128)(2,1)}) custom-call(s32[2]{0:T(128)} %pad_add_fusion.spot, bf16[4,224,1024]{2,1,0:T(8,128)(2,1)} %get-tuple-element.248.n_ref, ...), custom_call_target="tpu_custom_call" | custom-call | flops 1 | bytes 1 | tf_op jit(solution)/shard_map/gate_up_grads/pallas_call | solution.py:409
  267.2 12.0 %gate_up_grads.3 = (bf16[2,224,1280]{2,1,0:T(8,128)(2,1)}, bf16[2,224,1280]{2,1,0:T(8,128)(2,1)}, bf16[2,224,1280]{2,1,0:T(8,128)(2,1)}, bf16[2,224,1280]{2,1,0:T(8,128)(2,1)}) custom-call(s32[2]{0:T(128)} %pad_add_fusion.spot, bf16[4,224,1024]{2,1,0:T(8,128)(2,1)} %get-tuple-element.248.n_ref, ...), custom_call_target="tpu_custom_call" | custom-call | flops 1 | bytes 1 | tf_op jit(solution)/shard_map/gate_up_grads/pallas_call | solution.py:409
  279.1 9.6 %down_grad.1 = bf16[2432,896]{1,0:T(8,128)(2,1)} custom-call(bf16[1024,2432]{1,0:T(8,128)(2,1)} %get-tuple-element.278.inner_ref, bf16[512,896]{1,0:T(8,128)(2,1)} %copy-done.24, bf16[512,896]{1,0:T(8,128)(2,1)} %copy-done.29), custom_call_target="tpu_custom_call" | custom-call | flops 1 | bytes 1 | tf_op jit(solution)/shard_map/down_grad/pallas_call | solution.py:438
  293.8 16.3 %hidden_back.1 = (f32[512,896]{1,0:T(8,128)}, f32[512,896]{1,0:T(8,128)}) custom-call(bf16[2,1024,2432]{2,1,0:T(8,128)(2,1)} %get-tuple-element.273.d_own.d_other.d_ref, bf16[896,2432]{1,0:T(8,128)(2,1)} %get-tuple-element.274.gate_ref, bf16[896,2432]{1,0:T(8,128)(2,1)} %get-tuple-element.275.up_ref), custom_call_target="tpu_custom_call" | custom-call | flops 1 | bytes 1 | tf_op jit(solution)/shard_map/hidden_back/pallas_call | solution.py:478
  310.2 10.1 %project.1 = f32[1024,896]{1,0:T(8,128)} custom-call(bf16[1024,2432]{1,0:T(8,128)(2,1)} %get-tuple-element.278.inner_ref, bf16[2432,896]{1,0:T(8,128)(2,1)} %all-gather.2.cloned.1.call-done.refs_2_.down_ref), custom_call_target="tpu_custom_call" | custom-call | flops 1 | bytes 1 | tf_op jit(solution)/shard_map/project/pallas_call | solution.py:497
  343.2 17.5 %collective-permute-done.32 = bf16[224,2432]{1,0:T(8,128)(2,1)S(1)} collective-permute-done((bf16[224,2432]{1,0:T(8,128)(2,1)S(1)}, bf16[224,2432]{1,0:T(8,128)(2,1)S(1)}, u32[]{:S(2)}, u32[]{:S(2)}) %collective-permute-start.32) | collective-permute-done | bytes 1089568 | tf_op jit(solution)/shard_map/ppermute | solution.py:104
  365.5 6.9 %collective-permute-start.34 = (bf16[56,4864]{1,0:T(8,128)(2,1)}, bf16[56,4864]{1,0:T(8,128)(2,1)}, u32[]{:S(2)}, u32[]{:S(2)}) collective-permute-start(bf16[56,4864]{1,0:T(8,128)(2,1)} %get-tuple-element.306), channel_id=1, source_target_pairs={{0,2},{2,0},{4,6},{6,4},{1,3},{3,1},{5,7},{7,5},{8,10},{10,8},{12,... | collective-permute-start | bytes 1634312 | tf_op jit(solution)/shard_map/ppermute | solution.py:104
  389.1 12.4 %collective-permute-done.34 = bf16[56,4864]{1,0:T(8,128)(2,1)} collective-permute-done((bf16[56,4864]{1,0:T(8,128)(2,1)}, bf16[56,4864]{1,0:T(8,128)(2,1)}, u32[]{:S(2)}, u32[]{:S(2)}) %collective-permute-start.34) | collective-permute-done | bytes 544800 | tf_op jit(solution)/shard_map/ppermute | solution.py:104
  401.5 14.1 %collective-permute-done.36 = bf16[56,4864]{1,0:T(8,128)(2,1)} collective-permute-done((bf16[56,4864]{1,0:T(8,128)(2,1)}, bf16[56,4864]{1,0:T(8,128)(2,1)}, u32[]{:S(2)}, u32[]{:S(2)}) %collective-permute-start.36) | collective-permute-done | bytes 544800 | tf_op jit(solution)/shard_map/ppermute | solution.py:104
  423.7 7.9 %collective-permute-done.39 = bf16[4,2,256,128]{3,2,1,0:T(8,128)(2,1)S(1)} collective-permute-done((bf16[4,2,256,128]{3,2,1,0:T(8,128)(2,1)S(1)}, bf16[4,2,256,128]{3,2,1,0:T(8,128)(2,1)S(1)}, u32[]{:S(2)}, u32[]{:S(2)}) %collective-permute-start.39) | collective-permute-done | bytes 524320 | tf_op jit(solution)/shard_map/ppermute | solution.py:104
  437.7 19.7 %collective-permute-done.42 = bf16[2,2,256,128]{3,2,1,0:T(8,128)(2,1)S(1)} collective-permute-done((bf16[2,2,256,128]{3,2,1,0:T(8,128)(2,1)S(1)}, bf16[2,2,256,128]{3,2,1,0:T(8,128)(2,1)S(1)}, u32[]{:S(2)}, u32[]{:S(2)}) %collective-permute-start.42) | collective-permute-done | bytes 262176 | tf_op jit(solution)/shard_map/ppermute | solution.py:104
  457.4 7.0 %collective-permute-done.43 = bf16[2,2,256,128]{3,2,1,0:T(8,128)(2,1)S(1)} collective-permute-done((bf16[2,2,256,128]{3,2,1,0:T(8,128)(2,1)S(1)}, bf16[2,2,256,128]{3,2,1,0:T(8,128)(2,1)S(1)}, u32[]{:S(2)}, u32[]{:S(2)}) %collective-permute-start.43) | collective-permute-done | bytes 262176 | tf_op jit(solution)/shard_map/ppermute | solution.py:104
  499.9 7.8 %collective-permute-done.46 = bf16[4,64,1152]{2,1,0:T(8,128)(2,1)S(1)} collective-permute-done((bf16[4,64,1152]{2,1,0:T(8,128)(2,1)S(1)}, bf16[4,64,1152]{2,1,0:T(8,128)(2,1)S(1)}, u32[]{:S(2)}, u32[]{:S(2)}) %collective-permute-start.46) | collective-permute-done | bytes 589856 | tf_op jit(solution)/shard_map/ppermute | solution.py:104
  (451 shorter events, 235.6 us)
Async XLA Ops:
  7.2 222.1 %all-gather.2.cloned.1.call-start = ((), (), s32[]{:S(2)}) async-start(), calls=%async_computation.1 | async-start | bytes 4630528 | tf_op jit(solution)/shard_map/all_gather | solution.py:609
  43.2 33.3 %collective-permute-start.7 = (bf16[4,64,1152]{2,1,0:T(8,128)(2,1)S(1)}, bf16[4,64,1152]{2,1,0:T(8,128)(2,1)}, u32[]{:S(2)}, u32[]{:S(2)}) collective-permute-start(bf16[4,64,1152]{2,1,0:T(8,128)(2,1)S(1)} %bitcast_dynamic-update-slice_fusion), channel_id=1, source_target_pairs={{0,16},{16,0},{1,17},{17,1},{2,18},{18,2},{3,19},{19,3},{4,20},{20... | collective-permute-start | bytes 1769480 | tf_op jit(solution)/shard_map/ppermute | solution.py:77
  47.8 28.7 %collective-permute-start.9 = (bf16[56,3328]{1,0:T(8,128)(2,1)}, bf16[56,3328]{1,0:T(8,128)(2,1)}, u32[]{:S(2)}, u32[]{:S(2)}) collective-permute-start(bf16[56,3328]{1,0:T(8,128)(2,1)} %maximum_maximum_fusion), channel_id=1, source_target_pairs={{0,4},{2,6},{4,0},{6,2},{1,5},{3,7},{5,1},{7,3},{8,12},{10,14},{12... | collective-permute-start | bytes 1118216 | tf_op jit(solution)/shard_map/ppermute | solution.py:77
  85.2 46.6 %collective-permute-start.18 = (bf16[4,56,3328]{2,1,0:T(8,128)(2,1)}, bf16[4,56,3328]{2,1,0:T(8,128)(2,1)}, u32[]{:S(2)}, u32[]{:S(2)}) collective-permute-start(bf16[4,56,3328]{2,1,0:T(8,128)(2,1)} %pad_maximum_fusion.2), channel_id=1, source_target_pairs={{0,16},{16,0},{1,17},{17,1},{2,18},{18,2},{3,19},{19,3},{4,20},{20... | collective-permute-start | bytes 4472840 | tf_op jit(solution)/shard_map/ppermute | solution.py:77
  101.7 30.1 %collective-permute-start.19 = (bf16[4,56,2432]{2,1,0:T(8,128)(2,1)}, bf16[4,56,2432]{2,1,0:T(8,128)(2,1)}, u32[]{:S(2)}, u32[]{:S(2)}) collective-permute-start(bf16[4,56,2432]{2,1,0:T(8,128)(2,1)} %pad_maximum_fusion.5), channel_id=1, source_target_pairs={{0,1},{1,0},{2,3},{3,2},{4,5},{5,4},{6,7},{7,6},{8,9},{9,8},{10,11... | collective-permute-start | bytes 3268616 | tf_op jit(solution)/shard_map/ppermute | solution.py:77
  104.0 311.6 %reduce-scatter.2.cloned.1.call-start = ((), (), s32[]{:S(2)}) async-start(), calls=%async_computation.2 | async-start | bytes 5447680 | tf_op jit(solution)/shard_map/reduce_scatter | solution.py:658
  133.9 70.0 %collective-permute-start.22 = (bf16[2,4,56,2432]{3,2,1,0:T(8,128)(2,1)S(1)}, bf16[2,4,56,2432]{3,2,1,0:T(8,128)(2,1)S(1)}, u32[]{:S(2)}, u32[]{:S(2)}) collective-permute-start(bf16[2,4,56,2432]{3,2,1,0:T(8,128)(2,1)S(1)} %pad_maximum_fusion), channel_id=1, source_target_pairs={{0,16},{16,0},{1,17},{17,1},{2,18},{18,2},{3,19},{19,3},{4,20},{20... | collective-permute-start | bytes 6537224 | tf_op jit(solution)/shard_map/ppermute | solution.py:77
  135.3 27.1 %collective-permute-start.20 = (bf16[4,2,2,256,128]{4,3,2,1,0:T(8,128)(2,1)S(1)}, bf16[4,2,2,256,128]{4,3,2,1,0:T(8,128)(2,1)S(1)}, u32[]{:S(2)}, u32[]{:S(2)}) collective-permute-start(bf16[4,2,2,256,128]{4,3,2,1,0:T(8,128)(2,1)S(1)} %pad_maximum_fusion.6), channel_id=1, source_target_pairs={{0,1},{1,0},{2,3},{3,2},{4,5},{5,4},{6,7},{7,6},{8,9},{9,8},{10,11... | collective-permute-start | bytes 3145736 | tf_op jit(solution)/shard_map/ppermute | solution.py:77
  162.4 61.3 %collective-permute-start.21 = (bf16[2,4,56,2432]{3,2,1,0:T(8,128)(2,1)S(1)}, bf16[2,4,56,2432]{3,2,1,0:T(8,128)(2,1)S(1)}, u32[]{:S(2)}, u32[]{:S(2)}) collective-permute-start(bf16[2,4,56,2432]{3,2,1,0:T(8,128)(2,1)S(1)} %fusion.1), channel_id=1, source_target_pairs={{0,1},{1,0},{2,3},{3,2},{4,5},{5,4},{6,7},{7,6},{8,9},{9,8},{10,11... | collective-permute-start | bytes 6537224 | tf_op jit(solution)/shard_map/ppermute | solution.py:77
  164.9 62.6 %collective-permute-start.25 = (bf16[512,896]{1,0:T(8,128)(2,1)S(1)}, bf16[512,896]{1,0:T(8,128)(2,1)S(1)}, u32[]{:S(2)}, u32[]{:S(2)}) collective-permute-start(bf16[512,896]{1,0:T(8,128)(2,1)S(1)} %convert_element_type.338.u_own), channel_id=1, source_target_pairs={{0,8},{8,0},{1,9},{9,1},{2,10},{10,2},{3,11},{11,3},{4,12},{12,4},... | collective-permute-start | bytes 2752520 | tf_op jit(solution)/shard_map/ppermute | solution.py:51
  266.0 25.2 %collective-permute-start.26 = (bf16[2,224,1152]{2,1,0:T(8,128)(2,1)}, bf16[2,224,1152]{2,1,0:T(8,128)(2,1)}, u32[]{:S(2)}, u32[]{:S(2)}) collective-permute-start(bf16[2,224,1152]{2,1,0:T(8,128)(2,1)} %get-tuple-element.256), channel_id=1, source_target_pairs={{0,1},{1,0},{2,3},{3,2},{4,5},{5,4},{6,7},{7,6},{8,9},{9,8},{10,11... | collective-permute-start | bytes 3096584 | tf_op jit(solution)/shard_map/ppermute | solution.py:51
  266.3 24.9 %collective-permute-start.27 = (bf16[2,224,1152]{2,1,0:T(8,128)(2,1)}, bf16[2,224,1152]{2,1,0:T(8,128)(2,1)}, u32[]{:S(2)}, u32[]{:S(2)}) collective-permute-start(bf16[2,224,1152]{2,1,0:T(8,128)(2,1)} %get-tuple-element.258), channel_id=1, source_target_pairs={{0,16},{16,0},{1,17},{17,1},{2,18},{18,2},{3,19},{19,3},{4,20},{20... | collective-permute-start | bytes 3096584 | tf_op jit(solution)/shard_map/ppermute | solution.py:51
  291.3 29.0 %collective-permute-start.28 = (bf16[2,224,1280]{2,1,0:T(8,128)(2,1)}, bf16[2,224,1280]{2,1,0:T(8,128)(2,1)}, u32[]{:S(2)}, u32[]{:S(2)}) collective-permute-start(bf16[2,224,1280]{2,1,0:T(8,128)(2,1)} %get-tuple-element.270), channel_id=1, source_target_pairs={{0,1},{1,0},{2,3},{3,2},{4,5},{5,4},{6,7},{7,6},{8,9},{9,8},{10,11... | collective-permute-start | bytes 3440648 | tf_op jit(solution)/shard_map/ppermute | solution.py:51
  293.0 27.3 %collective-permute-start.29 = (bf16[2,224,1280]{2,1,0:T(8,128)(2,1)}, bf16[2,224,1280]{2,1,0:T(8,128)(2,1)}, u32[]{:S(2)}, u32[]{:S(2)}) collective-permute-start(bf16[2,224,1280]{2,1,0:T(8,128)(2,1)} %get-tuple-element.272), channel_id=1, source_target_pairs={{0,16},{16,0},{1,17},{17,1},{2,18},{18,2},{3,19},{19,3},{4,20},{20... | collective-permute-start | bytes 3440648 | tf_op jit(solution)/shard_map/ppermute | solution.py:51
  334.6 26.1 %collective-permute-start.32 = (bf16[224,2432]{1,0:T(8,128)(2,1)S(1)}, bf16[224,2432]{1,0:T(8,128)(2,1)S(1)}, u32[]{:S(2)}, u32[]{:S(2)}) collective-permute-start(bf16[224,2432]{1,0:T(8,128)(2,1)S(1)} %get-tuple-element.290), channel_id=1, source_target_pairs={{0,16},{16,0},{1,17},{17,1},{2,18},{18,2},{3,19},{19,3},{4,20},{20... | collective-permute-start | bytes 3268616 | tf_op jit(solution)/shard_map/ppermute | solution.py:104
  335.8 25.8 %collective-permute-start.33 = (bf16[224,2432]{1,0:T(8,128)(2,1)S(1)}, bf16[224,2432]{1,0:T(8,128)(2,1)S(1)}, u32[]{:S(2)}, u32[]{:S(2)}) collective-permute-start(bf16[224,2432]{1,0:T(8,128)(2,1)S(1)} %get-tuple-element.292), channel_id=1, source_target_pairs={{0,1},{1,0},{2,3},{3,2},{4,5},{5,4},{6,7},{7,6},{8,9},{9,8},{10,11... | collective-permute-start | bytes 3268616 | tf_op jit(solution)/shard_map/ppermute | solution.py:104
  337.6 82.7 %collective-permute-start.41 = (f32[512,896]{1,0:T(8,128)}, f32[512,896]{1,0:T(8,128)}, u32[]{:S(2)}, u32[]{:S(2)}) collective-permute-start(f32[512,896]{1,0:T(8,128)} %slice.151), channel_id=1, source_target_pairs={{0,8},{8,0},{1,9},{9,1},{2,10},{10,2},{3,11},{11,3},{4,12},{12,4},... | collective-permute-start | bytes 5505032 | tf_op jit(solution)/shard_map/ppermute | solution.py:51
  365.5 36.0 %collective-permute-start.34 = (bf16[56,4864]{1,0:T(8,128)(2,1)}, bf16[56,4864]{1,0:T(8,128)(2,1)}, u32[]{:S(2)}, u32[]{:S(2)}) collective-permute-start(bf16[56,4864]{1,0:T(8,128)(2,1)} %get-tuple-element.306), channel_id=1, source_target_pairs={{0,2},{2,0},{4,6},{6,4},{1,3},{3,1},{5,7},{7,5},{8,10},{10,8},{12,... | collective-permute-start | bytes 1634312 | tf_op jit(solution)/shard_map/ppermute | solution.py:104
  372.4 29.1 %collective-permute-start.35 = (bf16[56,4864]{1,0:T(8,128)(2,1)}, bf16[56,4864]{1,0:T(8,128)(2,1)}, u32[]{:S(2)}, u32[]{:S(2)}) collective-permute-start(bf16[56,4864]{1,0:T(8,128)(2,1)} %get-tuple-element.307), channel_id=1, source_target_pairs={{0,4},{2,6},{4,0},{6,2},{1,5},{3,7},{5,1},{7,3},{8,12},{10,14},{12... | collective-permute-start | bytes 1634312 | tf_op jit(solution)/shard_map/ppermute | solution.py:104
  375.1 40.6 %collective-permute-start.36 = (bf16[56,4864]{1,0:T(8,128)(2,1)}, bf16[56,4864]{1,0:T(8,128)(2,1)}, u32[]{:S(2)}, u32[]{:S(2)}) collective-permute-start(bf16[56,4864]{1,0:T(8,128)(2,1)} %get-tuple-element.308), channel_id=1, source_target_pairs={{0,6},{2,4},{4,2},{6,0},{1,7},{3,5},{5,3},{7,1},{8,14},{10,12},{12... | collective-permute-start | bytes 1634312 | tf_op jit(solution)/shard_map/ppermute | solution.py:104
  433.2 24.2 %collective-permute-start.42 = (bf16[2,2,256,128]{3,2,1,0:T(8,128)(2,1)S(1)}, bf16[2,2,256,128]{3,2,1,0:T(8,128)(2,1)S(1)}, u32[]{:S(2)}, u32[]{:S(2)}) collective-permute-start(bf16[2,2,256,128]{3,2,1,0:T(8,128)(2,1)S(1)} %get-tuple-element.435), channel_id=1, source_target_pairs={{2,0},{6,4},{3,1},{7,5},{10,8},{14,12},{11,9},{15,13},{18,16},{22,... | collective-permute-start | bytes 786440 | tf_op jit(solution)/shard_map/ppermute | solution.py:104
  434.5 29.9 %collective-permute-start.43 = (bf16[2,2,256,128]{3,2,1,0:T(8,128)(2,1)S(1)}, bf16[2,2,256,128]{3,2,1,0:T(8,128)(2,1)S(1)}, u32[]{:S(2)}, u32[]{:S(2)}) collective-permute-start(bf16[2,2,256,128]{3,2,1,0:T(8,128)(2,1)S(1)} %get-tuple-element.436), channel_id=1, source_target_pairs={{4,0},{6,2},{5,1},{7,3},{12,8},{14,10},{13,9},{15,11},{20,16},{22,... | collective-permute-start | bytes 786440 | tf_op jit(solution)/shard_map/ppermute | solution.py:104
  435.8 28.6 %collective-permute-start.44 = (bf16[2,2,256,128]{3,2,1,0:T(8,128)(2,1)S(1)}, bf16[2,2,256,128]{3,2,1,0:T(8,128)(2,1)S(1)}, u32[]{:S(2)}, u32[]{:S(2)}) collective-permute-start(bf16[2,2,256,128]{3,2,1,0:T(8,128)(2,1)S(1)} %get-tuple-element.433), channel_id=1, source_target_pairs={{4,2},{6,0},{5,3},{7,1},{12,10},{14,8},{13,11},{15,9},{20,18},{22,... | collective-permute-start | bytes 786440 | tf_op jit(solution)/shard_map/ppermute | solution.py:104
  473.3 26.6 %collective-permute-start.52 = (bf16[152,896]{1,0:T(8,128)(2,1)}, bf16[152,896]{1,0:T(8,128)(2,1)S(1)}, u32[]{:S(2)}, u32[]{:S(2)}) collective-permute-start(bf16[152,896]{1,0:T(8,128)(2,1)} %get-tuple-element.460), channel_id=1, source_target_pairs={{0,1},{1,0},{2,3},{3,2},{4,5},{5,4},{6,7},{7,6},{8,9},{9,8},{10,11... | collective-permute-start | bytes 817160 | tf_op jit(solution)/shard_map/ppermute | solution.py:104
  (117 other events, 1146.5 us)
Sparse Core Ops, SparseCore 0:
  104.1 111.8 all-gather.1
  293.9 99.3 reduce-scatter.1

commit v4 on v3

--- a/solution.py
+++ b/solution.py
@@ -95,6 +95,13 @@
 
 def parts_of(array, index, dim, count):
     return [pick(array, index ^ step, dim) for step in range(count)]
+
+
+def sums_of(groups, index, count):
+    return [
+        jnp.concatenate([add_up([pick(part, index ^ step) for part in group]) for group in groups], -1)
+        for step in range(count)
+    ]
 
 
 def send_parts(axis, parts, down_only=False):
@@ -509,6 +516,37 @@
     )(inner, down)
 
 
+def norm_kernel(
+    own_ref, other_ref, state_ref, upstream_ref, inverse_ref, gain_ref, weight_ref, mixed_ref,
+    hidden_ref, gain_grad_ref, mixed_grad_ref, weight_grad_ref,
+):
+    incoming, state, inverse = own_ref[...] + other_ref[...], state_ref[...], inverse_ref[...]
+    scaled = gain_ref[...] * incoming
+    mean = jnp.mean(scaled * state, -1, keepdims=True)
+    hidden = upstream_ref[...] + (inverse * scaled - state * inverse**3 * mean)
+    gain_grad_ref[...] = jnp.sum(incoming * state * inverse, 0, keepdims=True)
+    hidden_ref[...] = hidden
+    low = hidden.astype(jnp.bfloat16)
+    mixed_grad_ref[...] = dot(weight_ref[...], low, 1, 1).astype(jnp.bfloat16)
+    weight_grad_ref[...] = dot(mixed_ref[...], low).astype(jnp.bfloat16)
+
+
+def norm_and_out_back(own, other, state, upstream, inverse, gain, weight, mixed):
+    count, size = state.shape
+    return pl.pallas_call(
+        norm_kernel,
+        out_shape=[
+            jax.ShapeDtypeStruct((count, size), jnp.float32),
+            jax.ShapeDtypeStruct((1, size), jnp.float32),
+            jax.ShapeDtypeStruct((weight.shape[0], count), jnp.bfloat16),
+            jax.ShapeDtypeStruct(weight.shape, jnp.bfloat16),
+        ],
+        compiler_params=pltpu.CompilerParams(vmem_limit_bytes=48 * 2**20),
+        cost_estimate=pl.CostEstimate(flops=1, bytes_accessed=1, transcendentals=0),
+        name="norm_and_out_back",
+    )(own, other, state, upstream, inverse, gain[None, :], weight, mixed)
+
+
 def layer(
     sizes,
     inputs,
@@ -660,19 +698,21 @@
     right = exchange(right)
     d_normed2 = hidden_back(d_both, full_gate, full_up)
     left, right, d_normed2, output = hold(left, right, d_normed2, output)
-    first = jnp.concatenate([add_up(left[0]), add_up(right[0])], -1)
-    second = jnp.concatenate([add_up(left[1]), add_up(right[1])], -1)
-    d_normed2 = d_normed2[0] + swap("core", d_normed2[1], 2, 1)
-
-    change_mlp, grad_gain_mlp = norm_back(hidden_state, inverse_mlp, gain_mlp, d_normed2)
-    d_hidden = upstream + change_mlp
-    d_hidden_low = d_hidden.astype(low)
-    grad_out = across(mixed_low, d_hidden_low, 1, 0)
-    d_mixed = across(full_out, d_hidden_low, 1, 1).astype(low)
+    first = sums_of((left[0], right[0]), x_index, xs)
+    second = sums_of((left[1], right[1]), y_index, ys)
+    d_hidden, grad_gain_mlp, d_mixed, grad_out = norm_and_out_back(
+        d_normed2[0],
+        swap("core", d_normed2[1], 2, 1),
+        hidden_state,
+        upstream,
+        inverse_mlp,
+        gain_mlp,
+        full_out,
+        mixed_low,
+    )
     grad_out = parts_along(
-        "core", grad_out.astype(low).reshape(xs, 2, zs, 2 * share, D), 1, 2
-    )
-    first, second = parts_of(first, x_index, 0, xs), parts_of(second, y_index, 0, ys)
+        "core", grad_out.reshape(xs, 2, zs, 2 * share, D), 1, 2
+    )
     first, second, grad_out, d_mixed = hold(first, second, grad_out, d_mixed)
     first, second = send_parts("x", first), send_parts("y", second)
     d_query, kv_terms = [None] * KVH, [None] * KVH
@@ -726,7 +766,7 @@
     d_normed = across(d_qkv, full_qkv, 0, 1)
     change_attn, grad_gain_attn = norm_back(state, inverse_attn, gain_attn, d_normed)
     input_grad = (d_hidden + change_attn).astype(low)
-    grad_small = jnp.concatenate([grad_gain_attn, grad_gain_mlp, grad_bias])
+    grad_small = jnp.concatenate([grad_gain_attn, grad_gain_mlp[0], grad_bias])
 
     grad_small = grad_small.astype(low).reshape(-1, ys, small_share)
     grad_small = jnp.pad(grad_small, ((0, 0), (0, 8 - ys), (0, qkv_width - small_share)))

time: 581 us -> 578 us (level)
  Pallas kernels: 99.1 us -> 105 us
    pallas_call x0 -> x1, Pallas kernels: none -> 6.1 us  [norm_and_out_back(): pl.pallas_call(norm_kernel, out_shape=[jax.ShapeDtypeStruct((count, size)...]
    dot_general x6 -> x4, matrix products: 14.3 us -> 12 us  [across(): lax.dot_general(left, right, (((left_dim,), (right_dim,)), ((), ())), pre...]
    unnamed x160 -> x144, local copies, waits for them, and re-layouts: 15.5 us -> 14.6 us
  transfers between devices with their start and end apart: 64 -> 64, of which waited for: 33 -> 33; matrix products, arithmetic and copies ran while one was open for 12% -> 11% of each run, Pallas kernels for 11% -> 12%
where the time goes in v4:
time: 578 us; the launch traced here: 568 us
  waiting for transfers between devices  245 us (42%)
  Pallas kernels  105 us (18%)
  starting transfers between devices  83.8 us (14%)
  other arithmetic  56.9 us (10%)
  local copies, waits for them, and re-layouts  41 us (7%)
  between operations  23.9 us (4%)
  matrix products  12 us (2%)
    ppermute x20, waiting for transfers between devices, pieces_along(): pieces.append(lax.ppermute(value, axis, routes))  132 us
    ppermute x24, waiting for transfers between devices, send_parts(): out.append(lax.ppermute(parts[step], axis, routes))  95.4 us
    ppermute x24, starting transfers between devices, send_parts(): out.append(lax.ppermute(parts[step], axis, routes))  33.7 us
    ppermute x20, starting transfers between devices, pieces_along(): pieces.append(lax.ppermute(value, axis, routes))  28.6 us
    pallas_call x1, Pallas kernels, hidden_part(): pl.pallas_call(functools.partial(hidden_kernel, xs, 256), grid_spec=pltpu...  26.8 us
    pallas_call x2, Pallas kernels, gate_up_grads(): pl.pallas_call(functools.partial(grads_kernel, xs), grid_spec=pltpu.Prefe...  21.9 us
    ppermute x18, starting transfers between devices, swap(): return lax.ppermute(value, axis, [(i, i ^ step) for i in range(count)])  21.5 us
    ppermute x18, waiting for transfers between devices, swap(): return lax.ppermute(value, axis, [(i, i ^ step) for i in range(count)])  17.9 us
  transfers between devices with their start and end apart: 64, of which 33 were waited for; matrix products, arithmetic and copies ran while one was open for 11% of the time, Pallas kernels for 12%

profile of v4, /device:TPU:0, one launch (start us, length us, event | category | flops | bytes accessed | tf_op | source)
XLA Modules:
  0.0 568.1 jit_solution(6711595512905818938)
XLA Ops:
  33.1 8.4 %collective-permute-done.2 = bf16[64,1152]{1,0:T(8,128)(2,1)S(1)} collective-permute-done((bf16[64,1152]{1,0:T(8,128)(2,1)S(1)}, bf16[64,1152]{1,0:T(8,128)(2,1)S(1)}, u32[]{:S(2)}, u32[]{:S(2)}) %collective-permute-start.2) | collective-permute-done | bytes 147488 | tf_op jit(solution)/shard_map/ppermute | solution.py:77
  50.7 7.9 %collective-permute-done.10 = bf16[56,3328]{1,0:T(8,128)(2,1)} collective-permute-done((bf16[56,3328]{1,0:T(8,128)(2,1)}, bf16[56,3328]{1,0:T(8,128)(2,1)}, u32[]{:S(2)}, u32[]{:S(2)}) %collective-permute-start.10) | collective-permute-done | bytes 372768 | tf_op jit(solution)/shard_map/ppermute | solution.py:77
  63.0 13.5 %collective-permute-done.9 = bf16[56,3328]{1,0:T(8,128)(2,1)} collective-permute-done((bf16[56,3328]{1,0:T(8,128)(2,1)}, bf16[56,3328]{1,0:T(8,128)(2,1)}, u32[]{:S(2)}, u32[]{:S(2)}) %collective-permute-start.9) | collective-permute-done | bytes 372768 | tf_op jit(solution)/shard_map/ppermute | solution.py:77
  92.8 6.4 %collective-permute-done.13 = bf16[56,2432]{1,0:T(8,128)(2,1)} collective-permute-done((bf16[56,2432]{1,0:T(8,128)(2,1)}, bf16[56,2432]{1,0:T(8,128)(2,1)}, u32[]{:S(2)}, u32[]{:S(2)}) %collective-permute-start.13) | collective-permute-done | bytes 272416 | tf_op jit(solution)/shard_map/ppermute | solution.py:77
  104.0 6.7 %collective-permute-start.15 = (bf16[2,2,256,128]{3,2,1,0:T(8,128)(2,1)S(1)}, bf16[2,2,256,128]{3,2,1,0:T(8,128)(2,1)S(1)}, u32[]{:S(2)}, u32[]{:S(2)}) collective-permute-start(bf16[2,2,256,128]{3,2,1,0:T(8,128)(2,1)S(1)} %bitcast.348), channel_id=1, source_target_pairs={{0,2},{4,6},{1,3},{5,7},{8,10},{12,14},{9,11},{13,15},{16,18},{20,... | collective-permute-start | bytes 786440 | tf_op jit(solution)/shard_map/ppermute | solution.py:77
  119.8 9.2 %collective-permute-done.16 = bf16[2,2,256,128]{3,2,1,0:T(8,128)(2,1)S(1)} collective-permute-done((bf16[2,2,256,128]{3,2,1,0:T(8,128)(2,1)S(1)}, bf16[2,2,256,128]{3,2,1,0:T(8,128)(2,1)S(1)}, u32[]{:S(2)}, u32[]{:S(2)}) %collective-permute-start.16) | collective-permute-done | bytes 262176 | tf_op jit(solution)/shard_map/ppermute | solution.py:77
  139.3 21.7 %collective-permute-done.20 = bf16[4,2,2,256,128]{4,3,2,1,0:T(8,128)(2,1)S(1)} collective-permute-done((bf16[4,2,2,256,128]{4,3,2,1,0:T(8,128)(2,1)S(1)}, bf16[4,2,2,256,128]{4,3,2,1,0:T(8,128)(2,1)S(1)}, u32[]{:S(2)}, u32[]{:S(2)}) %collective-permute-start.20) | collective-permute-done | bytes 1048608 | tf_op jit(solution)/shard_map/ppermute | solution.py:77
  170.5 35.4 %collective-permute-done.22 = bf16[2,4,56,2432]{3,2,1,0:T(8,128)(2,1)S(1)} collective-permute-done((bf16[2,4,56,2432]{3,2,1,0:T(8,128)(2,1)S(1)}, bf16[2,4,56,2432]{3,2,1,0:T(8,128)(2,1)S(1)}, u32[]{:S(2)}, u32[]{:S(2)}) %collective-permute-start.22) | collective-permute-done | bytes 2179104 | tf_op jit(solution)/shard_map/ppermute | solution.py:77
  205.9 16.4 %collective-permute-done.21 = bf16[2,4,56,2432]{3,2,1,0:T(8,128)(2,1)S(1)} collective-permute-done((bf16[2,4,56,2432]{3,2,1,0:T(8,128)(2,1)S(1)}, bf16[2,4,56,2432]{3,2,1,0:T(8,128)(2,1)S(1)}, u32[]{:S(2)}, u32[]{:S(2)}) %collective-permute-start.21) | collective-permute-done | bytes 2179104 | tf_op jit(solution)/shard_map/ppermute | solution.py:77
  228.1 26.8 %hidden.1 = (bf16[1024,2432]{1,0:T(8,128)(2,1)}, bf16[2,1024,2432]{2,1,0:T(8,128)(2,1)}, bf16[896,2432]{1,0:T(8,128)(2,1)}, bf16[896,2432]{1,0:T(8,128)(2,1)}, bf16[4,224,1024]{2,1,0:T(8,128)(2,1)}) custom-call(s32[2]{0:T(128)} %pad_add_fusion.spot, bf16[512,896]{1,0:T(8,128)(2,1)} %copy-done.27, bf16[512,896]{1,0:T(8,128)(2,1)} %collective-permute-done.24.n_other, ...), custom_call_target="tpu_custom_call" | custom-call | flops 1 | bytes 1 | tf_op jit(solution)/shard_map/hidden/pallas_call | solution.py:379
  254.9 10.0 %gate_up_grads.2 = (bf16[2,224,1152]{2,1,0:T(8,128)(2,1)}, bf16[2,224,1152]{2,1,0:T(8,128)(2,1)}, bf16[2,224,1152]{2,1,0:T(8,128)(2,1)}, bf16[2,224,1152]{2,1,0:T(8,128)(2,1)}) custom-call(s32[2]{0:T(128)} %pad_add_fusion.spot, bf16[4,224,1024]{2,1,0:T(8,128)(2,1)} %get-tuple-element.252.n_ref, ...), custom_call_target="tpu_custom_call" | custom-call | flops 1 | bytes 1 | tf_op jit(solution)/shard_map/gate_up_grads/pallas_call | solution.py:416
  265.7 12.0 %gate_up_grads.3 = (bf16[2,224,1280]{2,1,0:T(8,128)(2,1)}, bf16[2,224,1280]{2,1,0:T(8,128)(2,1)}, bf16[2,224,1280]{2,1,0:T(8,128)(2,1)}, bf16[2,224,1280]{2,1,0:T(8,128)(2,1)}) custom-call(s32[2]{0:T(128)} %pad_add_fusion.spot, bf16[4,224,1024]{2,1,0:T(8,128)(2,1)} %get-tuple-element.252.n_ref, ...), custom_call_target="tpu_custom_call" | custom-call | flops 1 | bytes 1 | tf_op jit(solution)/shard_map/gate_up_grads/pallas_call | solution.py:416
  277.7 9.7 %down_grad.1 = bf16[2432,896]{1,0:T(8,128)(2,1)} custom-call(bf16[1024,2432]{1,0:T(8,128)(2,1)} %get-tuple-element.282.inner_ref, bf16[512,896]{1,0:T(8,128)(2,1)} %copy-done.24, bf16[512,896]{1,0:T(8,128)(2,1)} %copy-done.28), custom_call_target="tpu_custom_call" | custom-call | flops 1 | bytes 1 | tf_op jit(solution)/shard_map/down_grad/pallas_call | solution.py:445
  292.4 16.4 %hidden_back.1 = (f32[512,896]{1,0:T(8,128)}, f32[512,896]{1,0:T(8,128)}) custom-call(bf16[2,1024,2432]{2,1,0:T(8,128)(2,1)} %get-tuple-element.277.d_own.d_other.d_ref, bf16[896,2432]{1,0:T(8,128)(2,1)} %get-tuple-element.278.gate_ref, bf16[896,2432]{1,0:T(8,128)(2,1)} %get-tuple-element.279.up_ref), custom_call_target="tpu_custom_call" | custom-call | flops 1 | bytes 1 | tf_op jit(solution)/shard_map/hidden_back/pallas_call | solution.py:485
  308.8 9.9 %project.1 = f32[1024,896]{1,0:T(8,128)} custom-call(bf16[1024,2432]{1,0:T(8,128)(2,1)} %get-tuple-element.282.inner_ref, bf16[2432,896]{1,0:T(8,128)(2,1)} %all-gather.2.cloned.1.call-done.refs_2_.down_ref), custom_call_target="tpu_custom_call" | custom-call | flops 1 | bytes 1 | tf_op jit(solution)/shard_map/project/pallas_call | solution.py:504
  325.7 6.1 %norm_and_out_back.1 = (f32[512,896]{1,0:T(8,128)}, f32[1,896]{1,0:T(1,128)S(1)}, bf16[896,512]{1,0:T(8,128)(2,1)S(1)}, bf16[896,896]{1,0:T(8,128)(2,1)S(1)}) custom-call(f32[512,896]{1,0:T(8,128)} %get-tuple-element.291.own_ref, f32[512,896]{1,0:T(8,128)} %collective-permute-done.30.other_ref, f32[512,896]{1,0:T(8,128)} %copy-done.16, ...), custom_call_target="tpu_custom_call" | custom-call | flops 1 | bytes 1 | tf_op jit(solution)/shard_map/norm_and_out_back/pallas_call | solution.py:536
  344.6 17.0 %collective-permute-done.32 = bf16[224,2432]{1,0:T(8,128)(2,1)S(1)} collective-permute-done((bf16[224,2432]{1,0:T(8,128)(2,1)S(1)}, bf16[224,2432]{1,0:T(8,128)(2,1)S(1)}, u32[]{:S(2)}, u32[]{:S(2)}) %collective-permute-start.32) | collective-permute-done | bytes 1089568 | tf_op jit(solution)/shard_map/ppermute | solution.py:111
  366.5 7.0 %collective-permute-start.34 = (bf16[56,4864]{1,0:T(8,128)(2,1)}, bf16[56,4864]{1,0:T(8,128)(2,1)}, u32[]{:S(2)}, u32[]{:S(2)}) collective-permute-start(bf16[56,4864]{1,0:T(8,128)(2,1)} %get-tuple-element.312), channel_id=1, source_target_pairs={{0,2},{2,0},{4,6},{6,4},{1,3},{3,1},{5,7},{7,5},{8,10},{10,8},{12,... | collective-permute-start | bytes 1634312 | tf_op jit(solution)/shard_map/ppermute | solution.py:111
  389.9 7.3 %collective-permute-done.34 = bf16[56,4864]{1,0:T(8,128)(2,1)} collective-permute-done((bf16[56,4864]{1,0:T(8,128)(2,1)}, bf16[56,4864]{1,0:T(8,128)(2,1)}, u32[]{:S(2)}, u32[]{:S(2)}) %collective-permute-start.34) | collective-permute-done | bytes 544800 | tf_op jit(solution)/shard_map/ppermute | solution.py:111
  397.1 16.1 %collective-permute-done.35 = bf16[56,4864]{1,0:T(8,128)(2,1)} collective-permute-done((bf16[56,4864]{1,0:T(8,128)(2,1)}, bf16[56,4864]{1,0:T(8,128)(2,1)}, u32[]{:S(2)}, u32[]{:S(2)}) %collective-permute-start.35) | collective-permute-done | bytes 544800 | tf_op jit(solution)/shard_map/ppermute | solution.py:111
  420.6 6.5 %collective-permute-done.39 = bf16[4,2,256,128]{3,2,1,0:T(8,128)(2,1)S(1)} collective-permute-done((bf16[4,2,256,128]{3,2,1,0:T(8,128)(2,1)S(1)}, bf16[4,2,256,128]{3,2,1,0:T(8,128)(2,1)S(1)}, u32[]{:S(2)}, u32[]{:S(2)}) %collective-permute-start.39) | collective-permute-done | bytes 524320 | tf_op jit(solution)/shard_map/ppermute | solution.py:111
  433.1 14.8 %collective-permute-done.42 = bf16[2,2,256,128]{3,2,1,0:T(8,128)(2,1)S(1)} collective-permute-done((bf16[2,2,256,128]{3,2,1,0:T(8,128)(2,1)S(1)}, bf16[2,2,256,128]{3,2,1,0:T(8,128)(2,1)S(1)}, u32[]{:S(2)}, u32[]{:S(2)}) %collective-permute-start.42) | collective-permute-done | bytes 262176 | tf_op jit(solution)/shard_map/ppermute | solution.py:111
  447.9 13.8 %collective-permute-done.43 = bf16[2,2,256,128]{3,2,1,0:T(8,128)(2,1)S(1)} collective-permute-done((bf16[2,2,256,128]{3,2,1,0:T(8,128)(2,1)S(1)}, bf16[2,2,256,128]{3,2,1,0:T(8,128)(2,1)S(1)}, u32[]{:S(2)}, u32[]{:S(2)}) %collective-permute-start.43) | collective-permute-done | bytes 262176 | tf_op jit(solution)/shard_map/ppermute | solution.py:111
  496.1 7.8 %collective-permute-done.46 = bf16[4,64,1152]{2,1,0:T(8,128)(2,1)S(1)} collective-permute-done((bf16[4,64,1152]{2,1,0:T(8,128)(2,1)S(1)}, bf16[4,64,1152]{2,1,0:T(8,128)(2,1)S(1)}, u32[]{:S(2)}, u32[]{:S(2)}) %collective-permute-start.46) | collective-permute-done | bytes 589856 | tf_op jit(solution)/shard_map/ppermute | solution.py:111
  (437 shorter events, 237.4 us)
Async XLA Ops:
  7.2 220.9 %all-gather.2.cloned.1.call-start = ((), (), s32[]{:S(2)}) async-start(), calls=%async_computation.1 | async-start | bytes 4630528 | tf_op jit(solution)/shard_map/all_gather | solution.py:647
  43.1 33.3 %collective-permute-start.7 = (bf16[4,64,1152]{2,1,0:T(8,128)(2,1)S(1)}, bf16[4,64,1152]{2,1,0:T(8,128)(2,1)}, u32[]{:S(2)}, u32[]{:S(2)}) collective-permute-start(bf16[4,64,1152]{2,1,0:T(8,128)(2,1)S(1)} %bitcast_dynamic-update-slice_fusion), channel_id=1, source_target_pairs={{0,16},{16,0},{1,17},{17,1},{2,18},{18,2},{3,19},{19,3},{4,20},{20... | collective-permute-start | bytes 1769480 | tf_op jit(solution)/shard_map/ppermute | solution.py:77
  47.8 28.7 %collective-permute-start.9 = (bf16[56,3328]{1,0:T(8,128)(2,1)}, bf16[56,3328]{1,0:T(8,128)(2,1)}, u32[]{:S(2)}, u32[]{:S(2)}) collective-permute-start(bf16[56,3328]{1,0:T(8,128)(2,1)} %maximum_maximum_fusion), channel_id=1, source_target_pairs={{0,4},{2,6},{4,0},{6,2},{1,5},{3,7},{5,1},{7,3},{8,12},{10,14},{12... | collective-permute-start | bytes 1118216 | tf_op jit(solution)/shard_map/ppermute | solution.py:77
  76.5 22.7 %collective-permute-start.13 = (bf16[56,2432]{1,0:T(8,128)(2,1)}, bf16[56,2432]{1,0:T(8,128)(2,1)}, u32[]{:S(2)}, u32[]{:S(2)}) collective-permute-start(bf16[56,2432]{1,0:T(8,128)(2,1)} %squeeze.171), channel_id=1, source_target_pairs={{0,4},{2,6},{4,0},{6,2},{1,5},{3,7},{5,1},{7,3},{8,12},{10,14},{12... | collective-permute-start | bytes 817160 | tf_op jit(solution)/shard_map/ppermute | solution.py:77
  85.1 46.6 %collective-permute-start.18 = (bf16[4,56,3328]{2,1,0:T(8,128)(2,1)}, bf16[4,56,3328]{2,1,0:T(8,128)(2,1)}, u32[]{:S(2)}, u32[]{:S(2)}) collective-permute-start(bf16[4,56,3328]{2,1,0:T(8,128)(2,1)} %pad_maximum_fusion.2), channel_id=1, source_target_pairs={{0,16},{16,0},{1,17},{17,1},{2,18},{18,2},{3,19},{19,3},{4,20},{20... | collective-permute-start | bytes 4472840 | tf_op jit(solution)/shard_map/ppermute | solution.py:77
  101.7 30.8 %collective-permute-start.19 = (bf16[4,56,2432]{2,1,0:T(8,128)(2,1)}, bf16[4,56,2432]{2,1,0:T(8,128)(2,1)}, u32[]{:S(2)}, u32[]{:S(2)}) collective-permute-start(bf16[4,56,2432]{2,1,0:T(8,128)(2,1)} %pad_maximum_fusion.5), channel_id=1, source_target_pairs={{0,1},{1,0},{2,3},{3,2},{4,5},{5,4},{6,7},{7,6},{8,9},{9,8},{10,11... | collective-permute-start | bytes 3268616 | tf_op jit(solution)/shard_map/ppermute | solution.py:77
  104.0 309.3 %reduce-scatter.2.cloned.1.call-start = ((), (), s32[]{:S(2)}) async-start(), calls=%async_computation.2 | async-start | bytes 5447680 | tf_op jit(solution)/shard_map/reduce_scatter | solution.py:696
  133.8 27.2 %collective-permute-start.20 = (bf16[4,2,2,256,128]{4,3,2,1,0:T(8,128)(2,1)S(1)}, bf16[4,2,2,256,128]{4,3,2,1,0:T(8,128)(2,1)S(1)}, u32[]{:S(2)}, u32[]{:S(2)}) collective-permute-start(bf16[4,2,2,256,128]{4,3,2,1,0:T(8,128)(2,1)S(1)} %pad_maximum_fusion.10), channel_id=1, source_target_pairs={{0,1},{1,0},{2,3},{3,2},{4,5},{5,4},{6,7},{7,6},{8,9},{9,8},{10,11... | collective-permute-start | bytes 3145736 | tf_op jit(solution)/shard_map/ppermute | solution.py:77
  136.2 69.8 %collective-permute-start.22 = (bf16[2,4,56,2432]{3,2,1,0:T(8,128)(2,1)S(1)}, bf16[2,4,56,2432]{3,2,1,0:T(8,128)(2,1)S(1)}, u32[]{:S(2)}, u32[]{:S(2)}) collective-permute-start(bf16[2,4,56,2432]{3,2,1,0:T(8,128)(2,1)S(1)} %pad_maximum_fusion), channel_id=1, source_target_pairs={{0,16},{16,0},{1,17},{17,1},{2,18},{18,2},{3,19},{19,3},{4,20},{20... | collective-permute-start | bytes 6537224 | tf_op jit(solution)/shard_map/ppermute | solution.py:77
  161.0 61.3 %collective-permute-start.21 = (bf16[2,4,56,2432]{3,2,1,0:T(8,128)(2,1)S(1)}, bf16[2,4,56,2432]{3,2,1,0:T(8,128)(2,1)S(1)}, u32[]{:S(2)}, u32[]{:S(2)}) collective-permute-start(bf16[2,4,56,2432]{3,2,1,0:T(8,128)(2,1)S(1)} %fusion.1), channel_id=1, source_target_pairs={{0,1},{1,0},{2,3},{3,2},{4,5},{5,4},{6,7},{7,6},{8,9},{9,8},{10,11... | collective-permute-start | bytes 6537224 | tf_op jit(solution)/shard_map/ppermute | solution.py:77
  163.5 62.7 %collective-permute-start.25 = (bf16[512,896]{1,0:T(8,128)(2,1)S(1)}, bf16[512,896]{1,0:T(8,128)(2,1)S(1)}, u32[]{:S(2)}, u32[]{:S(2)}) collective-permute-start(bf16[512,896]{1,0:T(8,128)(2,1)S(1)} %convert_element_type.405.u_own), channel_id=1, source_target_pairs={{0,8},{8,0},{1,9},{9,1},{2,10},{10,2},{3,11},{11,3},{4,12},{12,4},... | collective-permute-start | bytes 2752520 | tf_op jit(solution)/shard_map/ppermute | solution.py:51
  264.9 25.2 %collective-permute-start.26 = (bf16[2,224,1152]{2,1,0:T(8,128)(2,1)}, bf16[2,224,1152]{2,1,0:T(8,128)(2,1)}, u32[]{:S(2)}, u32[]{:S(2)}) collective-permute-start(bf16[2,224,1152]{2,1,0:T(8,128)(2,1)} %get-tuple-element.260), channel_id=1, source_target_pairs={{0,1},{1,0},{2,3},{3,2},{4,5},{5,4},{6,7},{7,6},{8,9},{9,8},{10,11... | collective-permute-start | bytes 3096584 | tf_op jit(solution)/shard_map/ppermute | solution.py:51
  265.2 24.9 %collective-permute-start.27 = (bf16[2,224,1152]{2,1,0:T(8,128)(2,1)}, bf16[2,224,1152]{2,1,0:T(8,128)(2,1)}, u32[]{:S(2)}, u32[]{:S(2)}) collective-permute-start(bf16[2,224,1152]{2,1,0:T(8,128)(2,1)} %get-tuple-element.262), channel_id=1, source_target_pairs={{0,16},{16,0},{1,17},{17,1},{2,18},{18,2},{3,19},{19,3},{4,20},{20... | collective-permute-start | bytes 3096584 | tf_op jit(solution)/shard_map/ppermute | solution.py:51
  290.2 28.6 %collective-permute-start.28 = (bf16[2,224,1280]{2,1,0:T(8,128)(2,1)}, bf16[2,224,1280]{2,1,0:T(8,128)(2,1)}, u32[]{:S(2)}, u32[]{:S(2)}) collective-permute-start(bf16[2,224,1280]{2,1,0:T(8,128)(2,1)} %get-tuple-element.274), channel_id=1, source_target_pairs={{0,1},{1,0},{2,3},{3,2},{4,5},{5,4},{6,7},{7,6},{8,9},{9,8},{10,11... | collective-permute-start | bytes 3440648 | tf_op jit(solution)/shard_map/ppermute | solution.py:51
  291.9 26.9 %collective-permute-start.29 = (bf16[2,224,1280]{2,1,0:T(8,128)(2,1)}, bf16[2,224,1280]{2,1,0:T(8,128)(2,1)}, u32[]{:S(2)}, u32[]{:S(2)}) collective-permute-start(bf16[2,224,1280]{2,1,0:T(8,128)(2,1)} %get-tuple-element.276), channel_id=1, source_target_pairs={{0,16},{16,0},{1,17},{17,1},{2,18},{18,2},{3,19},{19,3},{4,20},{20... | collective-permute-start | bytes 3440648 | tf_op jit(solution)/shard_map/ppermute | solution.py:51
  335.2 26.4 %collective-permute-start.32 = (bf16[224,2432]{1,0:T(8,128)(2,1)S(1)}, bf16[224,2432]{1,0:T(8,128)(2,1)S(1)}, u32[]{:S(2)}, u32[]{:S(2)}) collective-permute-start(bf16[224,2432]{1,0:T(8,128)(2,1)S(1)} %pad_maximum_fusion.7), channel_id=1, source_target_pairs={{0,16},{16,0},{1,17},{17,1},{2,18},{18,2},{3,19},{19,3},{4,20},{20... | collective-permute-start | bytes 3268616 | tf_op jit(solution)/shard_map/ppermute | solution.py:111
  336.7 26.1 %collective-permute-start.33 = (bf16[224,2432]{1,0:T(8,128)(2,1)S(1)}, bf16[224,2432]{1,0:T(8,128)(2,1)S(1)}, u32[]{:S(2)}, u32[]{:S(2)}) collective-permute-start(bf16[224,2432]{1,0:T(8,128)(2,1)S(1)} %pad_maximum_fusion.9), channel_id=1, source_target_pairs={{0,1},{1,0},{2,3},{3,2},{4,5},{5,4},{6,7},{7,6},{8,9},{9,8},{10,11... | collective-permute-start | bytes 3268616 | tf_op jit(solution)/shard_map/ppermute | solution.py:111
  338.5 78.6 %collective-permute-start.41 = (f32[512,896]{1,0:T(8,128)}, f32[512,896]{1,0:T(8,128)}, u32[]{:S(2)}, u32[]{:S(2)}) collective-permute-start(f32[512,896]{1,0:T(8,128)} %slice.151), channel_id=1, source_target_pairs={{0,8},{8,0},{1,9},{9,1},{2,10},{10,2},{3,11},{11,3},{4,12},{12,4},... | collective-permute-start | bytes 5505032 | tf_op jit(solution)/shard_map/ppermute | solution.py:51
  366.5 30.7 %collective-permute-start.34 = (bf16[56,4864]{1,0:T(8,128)(2,1)}, bf16[56,4864]{1,0:T(8,128)(2,1)}, u32[]{:S(2)}, u32[]{:S(2)}) collective-permute-start(bf16[56,4864]{1,0:T(8,128)(2,1)} %get-tuple-element.312), channel_id=1, source_target_pairs={{0,2},{2,0},{4,6},{6,4},{1,3},{3,1},{5,7},{7,5},{8,10},{10,8},{12,... | collective-permute-start | bytes 1634312 | tf_op jit(solution)/shard_map/ppermute | solution.py:111
  373.4 39.9 %collective-permute-start.35 = (bf16[56,4864]{1,0:T(8,128)(2,1)}, bf16[56,4864]{1,0:T(8,128)(2,1)}, u32[]{:S(2)}, u32[]{:S(2)}) collective-permute-start(bf16[56,4864]{1,0:T(8,128)(2,1)} %get-tuple-element.313), channel_id=1, source_target_pairs={{0,4},{2,6},{4,0},{6,2},{1,5},{3,7},{5,1},{7,3},{8,12},{10,14},{12... | collective-permute-start | bytes 1634312 | tf_op jit(solution)/shard_map/ppermute | solution.py:111
  375.4 37.9 %collective-permute-start.36 = (bf16[56,4864]{1,0:T(8,128)(2,1)}, bf16[56,4864]{1,0:T(8,128)(2,1)}, u32[]{:S(2)}, u32[]{:S(2)}) collective-permute-start(bf16[56,4864]{1,0:T(8,128)(2,1)} %get-tuple-element.314), channel_id=1, source_target_pairs={{0,6},{2,4},{4,2},{6,0},{1,7},{3,5},{5,3},{7,1},{8,14},{10,12},{12... | collective-permute-start | bytes 1634312 | tf_op jit(solution)/shard_map/ppermute | solution.py:111
  429.9 31.9 %collective-permute-start.43 = (bf16[2,2,256,128]{3,2,1,0:T(8,128)(2,1)S(1)}, bf16[2,2,256,128]{3,2,1,0:T(8,128)(2,1)S(1)}, u32[]{:S(2)}, u32[]{:S(2)}) collective-permute-start(bf16[2,2,256,128]{3,2,1,0:T(8,128)(2,1)S(1)} %get-tuple-element.446), channel_id=1, source_target_pairs={{4,0},{6,2},{5,1},{7,3},{12,8},{14,10},{13,9},{15,11},{20,16},{22,... | collective-permute-start | bytes 786440 | tf_op jit(solution)/shard_map/ppermute | solution.py:111
  431.2 30.6 %collective-permute-start.44 = (bf16[2,2,256,128]{3,2,1,0:T(8,128)(2,1)S(1)}, bf16[2,2,256,128]{3,2,1,0:T(8,128)(2,1)S(1)}, u32[]{:S(2)}, u32[]{:S(2)}) collective-permute-start(bf16[2,2,256,128]{3,2,1,0:T(8,128)(2,1)S(1)} %get-tuple-element.443), channel_id=1, source_target_pairs={{4,2},{6,0},{5,3},{7,1},{12,10},{14,8},{13,11},{15,9},{20,18},{22,... | collective-permute-start | bytes 786440 | tf_op jit(solution)/shard_map/ppermute | solution.py:111
  470.7 25.4 %collective-permute-start.52 = (bf16[152,896]{1,0:T(8,128)(2,1)}, bf16[152,896]{1,0:T(8,128)(2,1)S(1)}, u32[]{:S(2)}, u32[]{:S(2)}) collective-permute-start(bf16[152,896]{1,0:T(8,128)(2,1)} %get-tuple-element.470), channel_id=1, source_target_pairs={{0,1},{1,0},{2,3},{3,2},{4,5},{5,4},{6,7},{7,6},{8,9},{9,8},{10,11... | collective-permute-start | bytes 817160 | tf_op jit(solution)/shard_map/ppermute | solution.py:111
  (109 other events, 1074.6 us)
Sparse Core Ops, SparseCore 0:
  104.1 111.7 all-gather.1
  290.3 85.5 reduce-scatter.1
